TPU v7x, 512 devices: a whole 4x4x16 slice. The times are simulated.
512 devices in a mesh: dp: 8 (over z_lo), ep: 64 (over x, y, z_hi, core).
Axes of the slice: x: 4, y: 4, z: 16 (z_hi: 2, z_lo: 8; z = z_hi * 8 + z_lo), core: 2. Of those that a mesh axis runs over, the one named last changes fastest.
Arguments:
- tokens: bfloat16 [2, 3072, 4096], P(None, ('dp', 'ep')), may hold values from -6 to 6
- experts: int32 [2, 3072, 8], P(None, ('dp', 'ep')), may hold values from 0 to 55, all different within a row; in each aligned block of 6 rows (0 to 5, 6 to 11, ..., all dimensions but the last counted through in order) at most 2 rows name the same one
- replicas: int32 [2, 3072, 8], P(None, ('dp', 'ep')), may hold values from 0 to 1
- route_weights: float32 [2, 3072, 8], P(None, ('dp', 'ep')), may hold values from 0.1 to 0.5
- slot_tables: int32 [2, 56, 2], replicated, may hold values from 0 to 63, as said below
- partners: int32 [64], replicated, may hold values from 0 to 63, as said below
- slot_rows: int32 [2, 8, 64], replicated, may hold values from 24 to 48, as said below
- gate_w: bfloat16 [64, 4096, 1024], P('ep', None, 'dp'), may hold values from -0.09375 to 0.09375
- up_w: bfloat16 [64, 4096, 1024], P('ep', None, 'dp'), may hold values from -0.09375 to 0.09375
- down_w: bfloat16 [64, 1024, 4096], P('ep', None, 'dp'), may hold values from -0.1875 to 0.1875
Outputs:
- mixed: bfloat16 [2, 3072, 4096], P(None, ('dp', 'ep'))
Inputs may be any that keep to these rules, and one draw needn't show every extreme that they name: `experts`: in each step, the 6 tokens of one device name one expert at most 2 times. slot_tables[0] gives each expert a slot in column 0; 8 experts have a second slot in column 1, the others repeat column 0; every slot appears exactly once as a column 0 entry or a second slot. slot_tables[1][e, c] = partners[slot_tables[0][e, c]]. partners[partners[s]] = s, and partners[s] is s or s plus or minus 64 // 2; partners[0] = 32. `slot_rows`: each step has some entry equal to 48.
All inputs are finite; a program needn't handle non-finite values.
Results may differ from a plain program's by a relative error of at most 0.0058.
Values may be sent and summed in bfloat16 or wider, within the bound.
No kernel may reach another device: no remote copies, remote signals or barrier semaphores. Data moves between devices by JAX's collectives and lax.ppermute only.
A program may use at most 64 MiB of HBM per device.

v0:
```python
import jax
import jax.numpy as jnp
from jax import lax
from jax.sharding import PartitionSpec as P


def from_partner(block, axis, stride):
    count = lax.axis_size(axis)
    route = []
    for low in range(count):
        high = low | 1 << stride
        if high != low and high < count:
            route += [(low, high), (high, low)]
    return lax.ppermute(block, axis, route)


def lookup_slots(chosen_ids, replica_pick, table):
    labels = jnp.arange(table.shape[0], dtype=jnp.int32)
    onehot = (chosen_ids[:, :, None] == labels[None, None, :]).astype(jnp.int32)
    first = jnp.sum(onehot * table[:, 0][None, None, :], axis=2)
    second = jnp.sum(onehot * table[:, 1][None, None, :], axis=2)
    return jnp.where(replica_pick == 0, first, second)


def moe_step(
    rows_in, chosen_ids, replica_pick, gates, table, limits, host_slot, w_gate, w_up, w_down
):
    tok, top = chosen_ids.shape
    model = rows_in.shape[1]
    n_ep = lax.axis_size("ep")
    n_dp = lax.axis_size("dp")
    kinds = table.shape[0]
    most = max(2, (tok * top + kinds - 1) // kinds)
    capacity = tok * top
    slots = lookup_slots(chosen_ids, replica_pick, table)
    flat_dest = slots.reshape(-1)
    onehot = (flat_dest[:, None] == jnp.arange(n_ep, dtype=jnp.int32)[None, :]).astype(jnp.int32)
    before = jnp.cumsum(onehot, axis=0) - onehot
    position = jnp.sum(before * onehot, axis=1)
    counts = jnp.sum(onehot, axis=0).reshape(n_ep, 1)
    spots = (position[:, None] == jnp.arange(most, dtype=jnp.int32)[None, :]).astype(jnp.int32)
    place = (onehot[:, :, None] * spots[:, None, :]).reshape(tok, top, n_ep * most)
    per_token = jnp.sum(place, axis=1).astype(jnp.bfloat16)
    buffer = jnp.einsum("ts,td->sd", per_token, rows_in, preferred_element_type=jnp.float32).astype(
        jnp.bfloat16
    )
    arrived, arrived_counts = (
        lax.all_to_all(
            buffer.reshape(n_ep, most, model), "ep", split_axis=0, concat_axis=0, tiled=True
        ),
        lax.all_to_all(counts, "ep", split_axis=0, concat_axis=0, tiled=True),
    )
    valid = (
        (jnp.arange(most, dtype=jnp.int32)[None, :] < arrived_counts).astype(jnp.int32).reshape(-1)
    )
    rank = jnp.cumsum(valid) - valid
    my_dp = lax.axis_index("dp")
    which = (jnp.arange(n_dp, dtype=jnp.int32)[:, None] == my_dp) & (
        jnp.arange(limits.shape[1], dtype=jnp.int32)[None, :] == host_slot
    )
    limit = jnp.sum(jnp.where(which, limits, 0))
    kept = valid * (rank < limit).astype(jnp.int32)
    pick = (
        kept[None, :]
        * (rank[None, :] == jnp.arange(capacity, dtype=jnp.int32)[:, None]).astype(jnp.int32)
    ).astype(jnp.bfloat16)
    compact = jnp.dot(
        pick, arrived.reshape(n_ep * most, model), preferred_element_type=jnp.float32
    ).astype(jnp.bfloat16)
    piece = lax.all_gather(compact, "dp", axis=0, tiled=True)
    gate = jnp.dot(piece, w_gate[0], preferred_element_type=jnp.float32)
    up = jnp.dot(piece, w_up[0], preferred_element_type=jnp.float32)
    hidden = (jax.nn.silu(gate) * up).astype(jnp.bfloat16)
    width = w_down.shape[2]
    block = w_down[0]
    output = jnp.dot(
        lax.all_gather(hidden, "dp", axis=1, tiled=True), block, preferred_element_type=jnp.float32
    ).astype(jnp.bfloat16)
    returned = lax.all_to_all(
        output.reshape(n_dp, capacity, width), "dp", split_axis=0, concat_axis=2, tiled=True
    ).reshape(capacity, model)
    spread = jnp.einsum("cs,cd->sd", pick, returned, preferred_element_type=jnp.float32).astype(
        jnp.bfloat16
    )
    back = lax.all_to_all(
        spread.reshape(n_ep, most, model), "ep", split_axis=0, concat_axis=0, tiled=True
    ).reshape(n_ep * most, model)
    weighted = jnp.sum(place.astype(jnp.float32) * gates[:, :, None], axis=1)
    mixed_rows = jnp.dot(weighted, back.astype(jnp.float32), precision=lax.Precision.HIGHEST)
    return mixed_rows.astype(jnp.bfloat16)


def on_device(
    tokens, experts, replicas, route_weights, slot_tables, partners, slot_rows, gate_w, up_w, down_w
):
    my_ep = lax.axis_index("ep")
    labels = jnp.arange(partners.shape[0], dtype=jnp.int32)
    partner_me = jnp.sum(jnp.where(labels == my_ep, partners, 0))
    first = moe_step(
        tokens[0],
        experts[0],
        replicas[0],
        route_weights[0],
        slot_tables[0],
        slot_rows[0],
        my_ep,
        gate_w,
        up_w,
        down_w,
    )
    bit = lax.axis_size("ep").bit_length() - 2
    moved_gate, moved_up, moved_down = from_partner((gate_w, up_w, down_w), "ep", bit)
    moving = partner_me != my_ep
    next_gate = jnp.where(moving, moved_gate, gate_w)
    next_up = jnp.where(moving, moved_up, up_w)
    next_down = jnp.where(moving, moved_down, down_w)
    second = moe_step(
        tokens[1],
        experts[1],
        replicas[1],
        route_weights[1],
        slot_tables[1],
        slot_rows[1],
        my_ep,
        next_gate,
        next_up,
        next_down,
    )
    return jnp.stack([first, second])


def solution(mesh):
    return jax.shard_map(
        on_device,
        mesh=mesh,
        in_specs=(
            P(None, ("dp", "ep"), None),
            P(None, ("dp", "ep"), None),
            P(None, ("dp", "ep"), None),
            P(None, ("dp", "ep"), None),
            P(),
            P(),
            P(),
            P("ep", None, "dp"),
            P("ep", None, "dp"),
            P("ep", None, "dp"),
        ),
        out_specs=P(None, ("dp", "ep"), None),
        check_vma=False,
    )
```

profile of v0, /device:TPU:1, one launch (start us, length us, event | category | flops | bytes accessed | tf_op | source)
XLA Modules:
  0.0 548.1 jit_solution(5869518776763168142)
XLA Ops:
  10.5 22.2 %all-to-all-start = ((s32[64,1,1]{2,1,0:T(1,128)}), s32[64,1,1]{2,1,0:T(1,128)S(1)}, u32[]{:S(2)}, u32[]{:S(2)}) async-start(s32[64,1,1]{2,1,0:T(1,128)} %copy.64), calls=%async_computation | async-start | bytes 65536 | tf_op jit(solution)/shard_map/all_to_all | solution.py:51
  38.4 10.7 %all-to-all-done = s32[64,1,1]{2,1,0:T(1,128)S(1)} async-done(((s32[64,1,1]{2,1,0:T(1,128)}), s32[64,1,1]{2,1,0:T(1,128)S(1)}, u32[]{:S(2)}, u32[]{:S(2)}) %all-to-all-start) | async-done | bytes 288 | tf_op jit(solution)/shard_map/all_to_all | solution.py:51
  49.1 6.8 %all-to-all-start.1 = ((bf16[64,2,4096]{2,1,0:T(2,128)(2,1)}), bf16[64,2,4096]{2,1,0:T(2,128)(2,1)S(1)}, u32[]{:S(2)}, u32[]{:S(2)}) async-start(bf16[64,2,4096]{2,1,0:T(2,128)(2,1)} %reshape.329), calls=%async_computation.1 | async-start | bytes 2097152 | tf_op jit(solution)/shard_map/all_to_all | solution.py:48
  59.3 28.9 %all-to-all-done.1 = bf16[64,2,4096]{2,1,0:T(2,128)(2,1)S(1)} async-done(((bf16[64,2,4096]{2,1,0:T(2,128)(2,1)}), bf16[64,2,4096]{2,1,0:T(2,128)(2,1)S(1)}, u32[]{:S(2)}, u32[]{:S(2)}) %all-to-all-start.1) | async-done | bytes 1048608 | tf_op jit(solution)/shard_map/all_to_all | solution.py:48
  91.2 4.6 all-to-all-start.4
  100.3 12.9 %all-to-all-done.4 = s32[64,1,1]{2,1,0:T(1,128)S(1)} async-done(((s32[64,1,1]{2,1,0:T(1,128)}), s32[64,1,1]{2,1,0:T(1,128)S(1)}, u32[]{:S(2)}, u32[]{:S(2)}) %all-to-all-start.4) | async-done | bytes 288 | tf_op jit(solution)/shard_map/all_to_all | solution.py:51
  113.2 14.0 %all-to-all-start.5 = ((bf16[64,2,4096]{2,1,0:T(2,128)(2,1)}), bf16[64,2,4096]{2,1,0:T(2,128)(2,1)S(1)}, u32[]{:S(2)}, u32[]{:S(2)}) async-start(bf16[64,2,4096]{2,1,0:T(2,128)(2,1)} %reshape.336), calls=%async_computation.5 | async-start | bytes 2097152 | tf_op jit(solution)/shard_map/all_to_all | solution.py:48
  129.9 44.4 %all-to-all-done.5 = bf16[64,2,4096]{2,1,0:T(2,128)(2,1)S(1)} async-done(((bf16[64,2,4096]{2,1,0:T(2,128)(2,1)}), bf16[64,2,4096]{2,1,0:T(2,128)(2,1)S(1)}, u32[]{:S(2)}, u32[]{:S(2)}) %all-to-all-start.5) | async-done | bytes 1048608 | tf_op jit(solution)/shard_map/all_to_all | solution.py:48
  178.0 4.8 collective-permute-start.1
  186.7 50.4 %all-gather.3.cloned.1.call-done = bf16[384,4096]{1,0:T(8,128)(2,1)} async-done(((bf16[48,4096]{1,0:T(8,128)(2,1)}), bf16[384,4096]{1,0:T(8,128)(2,1)}) %all-gather.3.cloned.1.call-update) | async-done | bytes 3145744 | tf_op jit(solution)/shard_map/all_gather | solution.py:70
  237.1 3.3 fusion.10
  241.5 45.9 %all_gather.13 = bf16[384,1024]{1,0:T(8,128)(2,1)S(1)} all-gather(bf16[384,128]{1,0:T(8,128)(2,1)S(1)} %fusion.2), channel_id=1, replica_groups=mesh['dp'=8,'ep'=64] {'dp'}, dimensions={1}, use_global_device_ids=true | all-gather | bytes 884736 | tf_op jit(solution)/shard_map/all_gather | solution.py:77
  288.6 3.8 all-to-all-start.2
  292.5 43.3 %all-gather.5.cloned.1.call-done = bf16[384,4096]{1,0:T(8,128)(2,1)} async-done(((bf16[48,4096]{1,0:T(8,128)(2,1)}), bf16[384,4096]{1,0:T(8,128)(2,1)}) %all-gather.5.cloned.1.call-update) | async-done | bytes 3145744 | tf_op jit(solution)/shard_map/all_gather | solution.py:70
  335.8 3.3 fusion.6
  339.2 2.3 multiply_convert_fusion
  341.5 41.0 %all_gather.15 = bf16[384,1024]{1,0:T(8,128)(2,1)S(1)} all-gather(bf16[384,128]{1,0:T(8,128)(2,1)S(1)} %multiply_convert_fusion), channel_id=1, replica_groups=mesh['dp'=8,'ep'=64] {'dp'}, dimensions={1}, use_global_device_ids=true | all-gather | bytes 884736 | tf_op jit(solution)/shard_map/all_gather | solution.py:77
  382.5 2.5 convolution_convert_fusion.8
  385.1 4.7 all-to-all-start.6
  391.8 11.9 %all-to-all-done.6 = bf16[8,48,512]{2,1,0:T(8,128)(2,1)S(1)} async-done(((bf16[8,48,512]{2,1,0:T(8,128)(2,1)}), bf16[8,48,512]{2,1,0:T(8,128)(2,1)S(1)}, u32[]{:S(2)}, u32[]{:S(2)}) %all-to-all-start.6) | async-done | bytes 393248 | tf_op jit(solution)/shard_map/all_to_all | solution.py:79
  403.7 26.5 %all-to-all-start.3 = ((bf16[64,2,4096]{2,1,0:T(2,128)(2,1)}), bf16[64,2,4096]{2,1,0:T(2,128)(2,1)S(1)}, u32[]{:S(2)}, u32[]{:S(2)}) async-start(bf16[64,2,4096]{2,1,0:T(2,128)(2,1)} %reshape.333), calls=%async_computation.3 | async-start | bytes 2097152 | tf_op jit(solution)/shard_map/all_to_all | solution.py:85
  432.2 52.4 %all-to-all-done.3 = bf16[64,2,4096]{2,1,0:T(2,128)(2,1)S(1)} async-done(((bf16[64,2,4096]{2,1,0:T(2,128)(2,1)}), bf16[64,2,4096]{2,1,0:T(2,128)(2,1)S(1)}, u32[]{:S(2)}, u32[]{:S(2)}) %all-to-all-start.3) | async-done | bytes 1048608 | tf_op jit(solution)/shard_map/all_to_all | solution.py:85
  484.6 4.2 all-to-all-start.7
  490.3 49.2 %all-to-all-done.7 = bf16[64,2,4096]{2,1,0:T(2,128)(2,1)S(1)} async-done(((bf16[64,2,4096]{2,1,0:T(2,128)(2,1)}), bf16[64,2,4096]{2,1,0:T(2,128)(2,1)S(1)}, u32[]{:S(2)}, u32[]{:S(2)}) %all-to-all-start.7) | async-done | bytes 1048608 | tf_op jit(solution)/shard_map/all_to_all | solution.py:85
  (105 shorter events, 39.5 us)
Async XLA Ops:
  10.5 38.6 %all-to-all-start = ((s32[64,1,1]{2,1,0:T(1,128)}), s32[64,1,1]{2,1,0:T(1,128)S(1)}, u32[]{:S(2)}, u32[]{:S(2)}) async-start(s32[64,1,1]{2,1,0:T(1,128)} %copy.64), calls=%async_computation | async-start | bytes 65536 | tf_op jit(solution)/shard_map/all_to_all | solution.py:51
  34.0 22.1 %copy-start.2 = (s32[2,8,64]{2,1,0:T(8,128)S(1)}, s32[2,8,64]{2,1,0:T(8,128)}, u32[]{:S(2)}) copy-start(s32[2,8,64]{2,1,0:T(8,128)} %param.16) | copy-start | bytes 12292
  49.1 39.0 %all-to-all-start.1 = ((bf16[64,2,4096]{2,1,0:T(2,128)(2,1)}), bf16[64,2,4096]{2,1,0:T(2,128)(2,1)S(1)}, u32[]{:S(2)}, u32[]{:S(2)}) async-start(bf16[64,2,4096]{2,1,0:T(2,128)(2,1)} %reshape.329), calls=%async_computation.1 | async-start | bytes 2097152 | tf_op jit(solution)/shard_map/all_to_all | solution.py:48
  55.9 181.2 %all-gather.3.cloned.1.call-start = ((), (), s32[]{:S(2)}) async-start(), calls=%async_computation.8 | async-start | bytes 3538944 | tf_op jit(solution)/shard_map/all_gather | solution.py:70
  91.2 22.0 %all-to-all-start.4 = ((s32[64,1,1]{2,1,0:T(1,128)}), s32[64,1,1]{2,1,0:T(1,128)S(1)}, u32[]{:S(2)}, u32[]{:S(2)}) async-start(s32[64,1,1]{2,1,0:T(1,128)} %copy.71), calls=%async_computation.4 | async-start | bytes 65536 | tf_op jit(solution)/shard_map/all_to_all | solution.py:51
  113.2 61.1 %all-to-all-start.5 = ((bf16[64,2,4096]{2,1,0:T(2,128)(2,1)}), bf16[64,2,4096]{2,1,0:T(2,128)(2,1)S(1)}, u32[]{:S(2)}, u32[]{:S(2)}) async-start(bf16[64,2,4096]{2,1,0:T(2,128)(2,1)} %reshape.336), calls=%async_computation.5 | async-start | bytes 2097152 | tf_op jit(solution)/shard_map/all_to_all | solution.py:48
  127.2 208.6 %all-gather.5.cloned.1.call-start = ((), (), s32[]{:S(2)}) async-start(), calls=%async_computation.9 | async-start | bytes 3538944 | tf_op jit(solution)/shard_map/all_gather | solution.py:70
  175.8 64.6 %copy-start.5 = (bf16[1,4096,128]{2,1,0:T(8,128)(2,1)S(1)}, bf16[1,4096,128]{2,1,0:T(8,128)(2,1)}, u32[]{:S(2)}) copy-start(bf16[1,4096,128]{2,1,0:T(8,128)(2,1)} %param.18) | copy-start | bytes 3145732
  175.8 116.6 %collective-permute-start = (bf16[1,4096,128]{2,1,0:T(8,128)(2,1)}, bf16[1,4096,128]{2,1,0:T(8,128)(2,1)}, u32[]{:S(2)}, u32[]{:S(2)}) collective-permute-start(bf16[1,4096,128]{2,1,0:T(8,128)(2,1)} %param.17), channel_id=1, source_target_pairs={{0,32},{32,0},{1,33},{33,1},{2,34},{34,2},{3,35},{35,3},{4,36},{36... | collective-permute-start | bytes 3145736 | tf_op jit(solution)/shard_map/ppermute | solution.py:14
  178.0 161.1 %collective-permute-start.1 = (bf16[1,4096,128]{2,1,0:T(8,128)(2,1)}, bf16[1,4096,128]{2,1,0:T(8,128)(2,1)}, u32[]{:S(2)}, u32[]{:S(2)}) collective-permute-start(bf16[1,4096,128]{2,1,0:T(8,128)(2,1)} %param.18), channel_id=1, source_target_pairs={{0,32},{32,0},{1,33},{33,1},{2,34},{34,2},{3,35},{35,3},{4,36},{36... | collective-permute-start | bytes 3145736 | tf_op jit(solution)/shard_map/ppermute | solution.py:14
  182.8 199.7 %collective-permute-start.2 = (bf16[1,1024,512]{2,1,0:T(8,128)(2,1)}, bf16[1,1024,512]{2,1,0:T(8,128)(2,1)}, u32[]{:S(2)}, u32[]{:S(2)}) collective-permute-start(bf16[1,1024,512]{2,1,0:T(8,128)(2,1)} %param.19), channel_id=1, source_target_pairs={{0,32},{32,0},{1,33},{33,1},{2,34},{34,2},{3,35},{35,3},{4,36},{36... | collective-permute-start | bytes 3145736 | tf_op jit(solution)/shard_map/ppermute | solution.py:14
  237.1 3.3 copy-start
  240.4 46.9 %copy-start.6 = (bf16[1,1024,512]{2,1,0:T(8,128)(2,1)S(1)}, bf16[1,1024,512]{2,1,0:T(8,128)(2,1)}, u32[]{:S(2)}) copy-start(bf16[1,1024,512]{2,1,0:T(8,128)(2,1)} %param.19) | copy-start | bytes 3145732
  241.4 94.4 %copy-start.1 = (bf16[1,4096,128]{2,1,0:T(8,128)(2,1)S(1)}, bf16[1,4096,128]{2,1,0:T(8,128)(2,1)}, u32[]{:S(2)}) copy-start(bf16[1,4096,128]{2,1,0:T(8,128)(2,1)} %param.17) | copy-start | bytes 3145732
  288.6 96.4 %all-to-all-start.2 = ((bf16[8,48,512]{2,1,0:T(8,128)(2,1)}), bf16[8,48,512]{2,1,0:T(8,128)(2,1)S(1)}, u32[]{:S(2)}, u32[]{:S(2)}) async-start(bf16[8,48,512]{2,1,0:T(8,128)(2,1)} %bitcast.11), calls=%async_computation.2 | async-start | bytes 786432 | tf_op jit(solution)/shard_map/all_to_all | solution.py:79
  335.8 3.3 copy-start.4
  339.1 43.4 %copy-start.7 = (bf16[1,1024,512]{2,1,0:T(8,128)(2,1)S(1)}, bf16[1,1024,512]{2,1,0:T(8,128)(2,1)}, u32[]{:S(2)}) copy-start(bf16[1,1024,512]{2,1,0:T(8,128)(2,1)} %param.19) | copy-start | bytes 3145732
  385.1 18.6 %all-to-all-start.6 = ((bf16[8,48,512]{2,1,0:T(8,128)(2,1)}), bf16[8,48,512]{2,1,0:T(8,128)(2,1)S(1)}, u32[]{:S(2)}, u32[]{:S(2)}) async-start(bf16[8,48,512]{2,1,0:T(8,128)(2,1)} %bitcast.26), calls=%async_computation.6 | async-start | bytes 786432 | tf_op jit(solution)/shard_map/all_to_all | solution.py:79
  403.7 80.9 %all-to-all-start.3 = ((bf16[64,2,4096]{2,1,0:T(2,128)(2,1)}), bf16[64,2,4096]{2,1,0:T(2,128)(2,1)S(1)}, u32[]{:S(2)}, u32[]{:S(2)}) async-start(bf16[64,2,4096]{2,1,0:T(2,128)(2,1)} %reshape.333), calls=%async_computation.3 | async-start | bytes 2097152 | tf_op jit(solution)/shard_map/all_to_all | solution.py:85
  430.2 58.6 %copy-start.3 = (f32[2,6,8]{2,0,1:T(2,128)S(1)}, f32[2,6,8]{2,0,1:T(2,128)}, u32[]{:S(2)}) copy-start(f32[2,6,8]{2,0,1:T(2,128)} %param.13) | copy-start | bytes 1156
  484.6 54.9 %all-to-all-start.7 = ((bf16[64,2,4096]{2,1,0:T(2,128)(2,1)}), bf16[64,2,4096]{2,1,0:T(2,128)(2,1)S(1)}, u32[]{:S(2)}, u32[]{:S(2)}) async-start(bf16[64,2,4096]{2,1,0:T(2,128)(2,1)} %reshape.340), calls=%async_computation.7 | async-start | bytes 2097152 | tf_op jit(solution)/shard_map/all_to_all | solution.py:85
Sparse Core Ops, SparseCore 0:
  89.8 147.3 all-gather.2
  239.2 96.5 all-gather.4
where the time goes:
time: 549 us; the launch traced here: 548 us
  waiting for transfers between devices  304 us (55%)
  starting transfers between devices  96.2 us (18%)
  blocking collectives  86.9 us (16%)
  matrix products  18.7 us (3%)
  between operations  14.5 us (3%)
  local copies, waits for them, and re-layouts  14.1 us (3%)
  other arithmetic  13.6 us (2%)
    all_to_all x2, waiting for transfers between devices, moe_step(): lax.all_to_all(spread.reshape(n_ep, most, model), 'ep', split_axis=0, con...  102 us
    all_gather x2, waiting for transfers between devices, moe_step(): piece = lax.all_gather(compact, 'dp', axis=0, tiled=True)  93.7 us
    all_gather x2, blocking collectives, moe_step(): lax.all_gather(hidden, 'dp', axis=1, tiled=True)  86.9 us
    all_to_all x2, waiting for transfers between devices, moe_step(): lax.all_to_all(buffer.reshape(n_ep, most, model), 'ep', split_axis=0, con...  73.3 us
    all_to_all x2, starting transfers between devices, moe_step(): lax.all_to_all(spread.reshape(n_ep, most, model), 'ep', split_axis=0, con...  30.7 us
    all_to_all x2, starting transfers between devices, moe_step(): lax.all_to_all(counts, 'ep', split_axis=0, concat_axis=0, tiled=True)  26.8 us
    all_to_all x2, waiting for transfers between devices, moe_step(): lax.all_to_all(counts, 'ep', split_axis=0, concat_axis=0, tiled=True)  23.6 us
    all_to_all x2, starting transfers between devices, moe_step(): lax.all_to_all(buffer.reshape(n_ep, most, model), 'ep', split_axis=0, con...  20.8 us
  transfers between devices with their start and end apart: 13, of which 9 were waited for; matrix products, arithmetic and copies ran while one was open for 7% of the time, Pallas kernels for 0%

commit v1 on v0

v1 whole, which is shorter than its diff:
```python
import jax
import jax.numpy as jnp
from jax import lax
from jax.sharding import Mesh, PartitionSpec as P

BF = jnp.bfloat16
F32 = jnp.float32
LANES = 128
ROWS = 48
HOME, HI, MID, ONE, POS = 0, 8, 16, 32, 33


def split_gates(gates):
    high = lax.reduce_precision(gates, 8, 7)
    mid = lax.reduce_precision(gates - high, 8, 7)
    return high.astype(BF), mid.astype(BF)


def pack_meta(experts, replicas, gates, table):
    labels = jnp.arange(table.shape[0], dtype=jnp.int32)
    hot = experts[..., None] == labels
    picked = jnp.where(replicas[..., None] == 0, table[:, 0], table[:, 1])
    home = jnp.sum(jnp.where(hot, picked, 0), axis=-1)
    high, mid = split_gates(gates)
    one = jnp.ones(home.shape, BF)
    meta = jnp.concatenate([home.astype(BF), high, mid, one, one], axis=-1)
    return jnp.pad(meta, ((0, 0), (0, LANES - meta.shape[-1])))


def match_columns(home, me, columns):
    labels = jnp.arange(columns, dtype=jnp.int32) * 4 + me
    return home[..., None] == labels


def occurrence(match, axis):
    count = match.astype(jnp.int32)
    return jnp.cumsum(count, axis=axis) - count


def send_places(home, me, columns, most):
    match = jnp.any(match_columns(home, me, columns), axis=-2)
    earlier = occurrence(match, -2)
    return match[..., None] & (earlier[..., None] == jnp.arange(most, dtype=jnp.int32))


def on_device(
    tokens, experts, replicas, route_weights, slot_tables, partners, slot_rows, gate_w, up_w, down_w
):
    steps, tok, model = tokens.shape
    top = experts.shape[-1]
    n_dp = lax.axis_size("dp")
    columns = lax.axis_size("x") * lax.axis_size("y")
    quad = lax.axis_size("zh") * lax.axis_size("core")
    most = 2
    me = lax.axis_index("zh") * lax.axis_size("core") + lax.axis_index("core")
    column = lax.axis_index("x") * lax.axis_size("y") + lax.axis_index("y")
    my_home = column * quad + me
    my_dp = lax.axis_index("dp")
    mine = steps * tok
    group = quad * mine
    boxes = quad * steps * most
    width = down_w.shape[2]

    meta = pack_meta(
        experts.reshape(mine, top),
        replicas.reshape(mine, top),
        route_weights.reshape(mine, top),
        slot_tables[0],
    )
    packed = jnp.concatenate([tokens.reshape(mine, model), meta], axis=1)
    held = lax.all_gather(packed, ("zh", "core"), axis=0, tiled=True)

    held_meta = held[:, model:]
    home = held_meta[:, HOME : HOME + top].astype(jnp.int32).reshape(quad, steps, tok, top)
    place = send_places(home, me, columns, most)
    same_q = jnp.eye(quad, dtype=jnp.bool_)
    same_u = jnp.eye(steps, dtype=jnp.bool_)
    sender = (
        place.transpose(3, 0, 1, 4, 2)[:, :, :, :, None, None, :]
        & same_q[None, :, None, None, :, None, None]
        & same_u[None, None, :, None, None, :, None]
    ).reshape(columns * boxes, group)
    buffer = jnp.dot(sender.astype(BF), held, preferred_element_type=F32).astype(BF)
    arrived = lax.all_to_all(
        buffer.reshape(columns, boxes, model + LANES),
        ("x", "y"),
        split_axis=0,
        concat_axis=0,
        tiled=True,
    ).reshape(columns * boxes, model + LANES)

    valid = (arrived[:, model + ONE] > 0).reshape(columns, quad, steps, most)
    order = valid.transpose(2, 0, 1, 3).reshape(steps, columns * quad * most)
    rank = occurrence(order, 1)
    labels = jnp.arange(partners.shape[0], dtype=jnp.int32)
    partner_me = jnp.sum(jnp.where(labels == my_home, partners, 0))
    owner = jnp.stack([my_home, partner_me])
    which = (jnp.arange(n_dp, dtype=jnp.int32)[None, :, None] == my_dp) & (
        labels[None, None, :] == owner[:, None, None]
    )
    limit = jnp.sum(jnp.where(which, slot_rows, 0), axis=(1, 2))
    kept = order & (rank < limit[:, None])
    spot = jnp.where(kept, rank + ROWS * jnp.arange(steps, dtype=jnp.int32)[:, None], -1)
    spot = spot.reshape(steps, columns, quad, most).transpose(1, 2, 0, 3).reshape(-1)
    capacity = steps * ROWS
    pick = (spot[None, :] == jnp.arange(capacity, dtype=jnp.int32)[:, None]).astype(BF)
    compact = jnp.dot(pick, arrived[:, :model], preferred_element_type=F32).astype(BF)
    where_from = jnp.dot(
        pick,
        jnp.stack([jnp.arange(columns * boxes), jnp.ones(columns * boxes)], axis=1).astype(BF),
        preferred_element_type=F32,
    )
    position = jnp.where(where_from[:, 1] > 0, where_from[:, 0], -1.0).astype(BF)
    side = jnp.pad(held_meta, ((0, capacity - group), (0, 0)))
    side = jnp.where(
        jnp.arange(LANES, dtype=jnp.int32)[None, :] == POS, position[:, None], side
    )
    rows = lax.all_gather(jnp.concatenate([compact, side], axis=1), "dp", axis=0, tiled=True)

    sides = rows[:, model:].reshape(n_dp, capacity, LANES)
    x = rows[:, :model]
    gate = jnp.dot(x, gate_w[0], preferred_element_type=F32)
    up = jnp.dot(x, up_w[0], preferred_element_type=F32)
    hidden = (jax.nn.silu(gate) * up).astype(BF)
    hiddens = lax.all_gather(hidden, "dp", axis=0, tiled=False)
    output = jnp.einsum(
        "zrh,zhf->rf",
        hiddens,
        down_w[0].reshape(n_dp, hidden.shape[1], width),
        preferred_element_type=F32,
    ).astype(BF)

    positions = sides[:, :, POS].astype(jnp.int32)
    unpick = (
        jnp.arange(columns * boxes, dtype=jnp.int32)[None, :, None] == positions[:, None, :]
    ).astype(BF)
    spread = jnp.einsum(
        "dpc,dcf->dpf",
        unpick,
        output.reshape(n_dp, capacity, width),
        preferred_element_type=F32,
    ).astype(BF)
    back = lax.all_to_all(
        spread.reshape(n_dp, columns, boxes, width).transpose(1, 0, 2, 3),
        ("x", "y"),
        split_axis=0,
        concat_axis=0,
        tiled=True,
    )

    token_meta = sides[:, :group]
    homes = token_meta[..., HOME : HOME + top].astype(jnp.int32).reshape(
        n_dp, quad, steps, tok, top
    )
    hit = match_columns(homes, me, columns)
    places = send_places(homes, me, columns, most)
    parts = []
    for lane in (HI, MID):
        scale = token_meta[..., lane : lane + top].astype(F32).reshape(homes.shape)
        by_column = jnp.sum(jnp.where(hit, scale[..., None], 0.0), axis=-2)
        weight = jnp.where(places, by_column[..., None], 0.0)
        weight = jnp.where(
            same_q[None, :, None, None, None, :, None, None]
            & same_u[None, None, :, None, None, None, :, None],
            weight[:, :, :, :, :, None, None, :],
            0.0,
        )
        parts.append(weight.reshape(n_dp, group, columns * boxes).astype(BF))
    weights = jnp.concatenate(parts, axis=1)
    sums = jnp.einsum(
        "dtp,dpf->dtf",
        weights,
        back.transpose(1, 0, 2, 3).reshape(n_dp, columns * boxes, width),
        preferred_element_type=F32,
    )
    partial = (sums[:, :group] + sums[:, group:]).astype(BF)
    partial = partial.reshape(n_dp, 2, 2, mine, width)
    swapped = lax.all_to_all(
        partial.transpose(2, 1, 0, 3, 4), "core", split_axis=0, concat_axis=0, tiled=True
    )
    halves = jnp.sum(swapped.astype(F32), axis=0).astype(BF)
    pieces = lax.all_to_all(
        halves.reshape(2 * n_dp, mine, width),
        ("zh", "dp"),
        split_axis=0,
        concat_axis=0,
        tiled=True,
    ).reshape(2, n_dp, mine, width)
    mixed = jnp.sum(pieces.astype(F32), axis=0).astype(BF)
    return mixed.transpose(1, 0, 2).reshape(steps, tok, model)


def solution(mesh):
    names = ("dp", "x", "y", "zh", "core")
    grid = Mesh(mesh.devices.reshape(mesh.shape["dp"], 4, 4, 2, 2), names)
    ep = ("x", "y", "zh", "core")
    rows = P(None, names, None)
    return jax.shard_map(
        on_device,
        mesh=grid,
        in_specs=(
            rows,
            rows,
            rows,
            rows,
            P(),
            P(),
            P(),
            P(ep, None, "dp"),
            P(ep, None, "dp"),
            P(ep, None, "dp"),
        ),
        out_specs=rows,
        check_vma=False,
    )
```

time: 549 us -> 428 us (0.78)
  starting transfers between devices: 96.2 us -> 12.7 us
  waiting for transfers between devices: 304 us -> 239 us
  local copies, waits for them, and re-layouts: 14.1 us -> 70.8 us
  blocking collectives: 86.9 us -> 52.6 us
  other arithmetic: 13.6 us -> 19.7 us
    all_to_all x8 -> x2, waiting for transfers between devices: 210 us -> 28.1 us  [the longest x1 28.1 us: on_device(): lax.all_to_all(buffer.reshape(columns, boxes, model + LANES), ('x', 'y'),...]
    all_gather x2, waiting for transfers between devices: 93.7 us -> 211 us  [the longest x1 155 us: on_device(): lax.all_gather(jnp.concatenate([compact, side], axis=1), 'dp', axis=0, ti...]
    all_to_all x8 -> x2, starting transfers between devices: 86.9 us -> 12.6 us  [the longest x1 6.74 us: on_device(): lax.all_to_all(spread.reshape(n_dp, columns, boxes, width).transpose(1, 0...]
    all_gather x2 -> x1, blocking collectives: 86.9 us -> 22.3 us  [on_device(): held = lax.all_gather(packed, ('zh', 'core'), axis=0, tiled=True)]
    broadcast_in_dim x0 -> x13, local copies, waits for them, and re-layouts: none -> 47.1 us  [the longest x9 40.6 us: on_device(): jnp.where(same_q[None, :, None, None, None, :, None, None] & same_u[None,...]
    all_to_all x0 -> x2, blocking collectives: none -> 30.3 us  [the longest x1 19.5 us: on_device(): lax.all_to_all(halves.reshape(2 * n_dp, mine, width), ('zh', 'dp'), split...]
    ppermute x3 -> x0, starting transfers between devices: 8.95 us -> none  [from_partner(): return lax.ppermute(block, axis, route)]
    dot_general x14 -> x8, matrix products: 18.7 us -> 13.9 us  [the longest x1 4.71 us: on_device(): gate = jnp.dot(x, gate_w[0], preferred_element_type=F32)]
  transfers between devices with their start and end apart: 13 -> 4, of which waited for: 9 -> 3; matrix products, arithmetic and copies ran while one was open for 7% -> 18% of each run, Pallas kernels for 0% -> 0%
where the time goes in v1:
time: 428 us; the launch traced here: 423 us
  waiting for transfers between devices  239 us (56%)
  local copies, waits for them, and re-layouts  70.8 us (17%)
  blocking collectives  52.6 us (12%)
  other arithmetic  19.7 us (5%)
  matrix products  13.9 us (3%)
  between operations  13.8 us (3%)
  starting transfers between devices  12.7 us (3%)
    all_gather x1, waiting for transfers between devices, on_device(): lax.all_gather(jnp.concatenate([compact, side], axis=1), 'dp', axis=0, ti...  155 us
    all_gather x1, waiting for transfers between devices, on_device(): hiddens = lax.all_gather(hidden, 'dp', axis=0, tiled=False)  56.8 us
    broadcast_in_dim x9, local copies, waits for them, and re-layouts, on_device(): jnp.where(same_q[None, :, None, None, None, :, None, None] & same_u[None,...  40.6 us
    all_to_all x1, waiting for transfers between devices, on_device(): lax.all_to_all(buffer.reshape(columns, boxes, model + LANES), ('x', 'y'),...  28.1 us
    all_gather x1, blocking collectives, on_device(): held = lax.all_gather(packed, ('zh', 'core'), axis=0, tiled=True)  22.3 us
    all_to_all x1, blocking collectives, on_device(): lax.all_to_all(halves.reshape(2 * n_dp, mine, width), ('zh', 'dp'), split...  19.5 us
    all_to_all x1, blocking collectives, on_device(): lax.all_to_all(partial.transpose(2, 1, 0, 3, 4), 'core', split_axis=0, co...  10.8 us
  transfers between devices with their start and end apart: 4, of which 3 were waited for; matrix products, arithmetic and copies ran while one was open for 18% of the time, Pallas kernels for 0%

profile of v1, /device:TPU:1, one launch (start us, length us, event | category | flops | bytes accessed | tf_op | source)
XLA Modules:
  0.0 422.9 jit_solution(7964712040869351458)
XLA Ops:
  11.4 22.3 %all-gather.1 = bf16[4,12,4224]{2,1,0:T(8,128)(2,1)S(1)} all-gather(bf16[1,12,4224]{2,1,0:T(8,128)(2,1)S(1)} %fusion.25), channel_id=1, replica_groups=mesh['dp'=8,'x'=4,'y'=4,'zh'=2,'core'=2] {'zh','core'}, dimensions={0}, use_global_device_ids=true | all-gather | bytes 506880 | tf_op jit(solution)/shard_map/all_gather | solution.py:71
  36.5 2.0 convolution_convert_fusion
  38.6 5.8 %all-to-all-start = ((bf16[16,16,4224]{2,1,0:T(8,128)(2,1)}), bf16[16,16,4224]{2,1,0:T(8,128)(2,1)S(1)}, u32[]{:S(2)}, u32[]{:S(2)}) async-start(bf16[16,16,4224]{2,1,0:T(8,128)(2,1)} %bitcast.81), calls=%async_computation | async-start | bytes 4325376 | tf_op jit(solution)/shard_map/all_to_all | solution.py:84
  46.2 28.1 %all-to-all-done = bf16[16,16,4224]{2,1,0:T(8,128)(2,1)S(1)} async-done(((bf16[16,16,4224]{2,1,0:T(8,128)(2,1)}), bf16[16,16,4224]{2,1,0:T(8,128)(2,1)S(1)}, u32[]{:S(2)}, u32[]{:S(2)}) %all-to-all-start) | async-done | bytes 2162720 | tf_op jit(solution)/shard_map/all_to_all | solution.py:84
  77.9 154.5 %all-gather.5.cloned.1.call-done = bf16[768,4224]{1,0:T(8,128)(2,1)} async-done(((bf16[96,4224]{1,0:T(8,128)(2,1)}), bf16[768,4224]{1,0:T(8,128)(2,1)}) %all-gather.5.cloned.1.call-update) | async-done | bytes 6488080 | tf_op jit(solution)/shard_map/all_gather | solution.py:118
  232.4 4.7 %fusion.2 = f32[768,128]{1,0:T(8,128)S(1)} fusion(bf16[768,4224]{1,0:T(8,128)(2,1)} %all-gather.5.cloned.1.call-done, bf16[1,4096,128]{2,1,0:T(8,128)(2,1)S(1)} %copy-done.5), kind=kOutput, calls=%fused_computation.3 | convolution fusion | flops 805306368 | bytes 7733248 | tf_op jit(solution)/shard_map/dot_general | solution.py:122
  237.1 2.5 fusion.10
  241.0 56.8 %all-gather.7.cloned.1.call-done = bf16[6144,128]{1,0:T(8,128)(2,1)} async-done(((bf16[768,128]{1,0:T(8,128)(2,1)}), bf16[6144,128]{1,0:T(8,128)(2,1)}) %all-gather.7.cloned.1.call-update) | async-done | bytes 1572880 | tf_op jit(solution)/shard_map/all_gather | solution.py:125
  297.8 2.4 bitcast_convert_fusion
  302.9 6.7 %all-to-all-start.1 = ((bf16[16,8,16,512]{3,2,1,0:T(8,128)(2,1)}), bf16[16,8,16,512]{3,2,1,0:T(8,128)(2,1)S(1)}, u32[]{:S(2)}, u32[]{:S(2)}) async-start(bf16[16,8,16,512]{3,2,1,0:T(8,128)(2,1)} %bitcast.83), calls=%async_computation.1 | async-start | bytes 4194304 | tf_op jit(solution)/shard_map/all_to_all | solution.py:143
  321.0 2.1 copy.253
  325.2 2.1 copy.257
  327.3 3.7 fusion.5
  330.9 2.1 copy.254
  336.6 2.2 copy.251
  338.8 2.1 copy.258
  340.8 3.9 fusion.16
  344.7 4.1 broadcast_in_dim.194
  348.8 12.3 %broadcast_in_dim.195 = bf16[8,48,256]{1,2,0:T(8,128)(2,1)} reshape(bf16[8,4,2,6,16,4,2,2]{3,2,1,7,6,5,4,0:T(2,128)(2,1)} %broadcast_in_dim.194) | data formatting | bytes 393216 | tf_op jit(solution)/shard_map/jit(_where)/broadcast_in_dim | solution.py:162
  361.1 1.9 copy.255
  363.0 5.1 %broadcast_in_dim.201 = bf16[8,4,2,6,16,4,2,2]{3,2,1,7,6,5,4,0:T(2,128)(2,1)} broadcast(bf16[8,4,2,6,16,2]{3,2,1,5,4,0:T(2,128)(2,1)} %get-tuple-element.8), dimensions={0,1,2,3,4,7} | broadcast | bytes 221184 | tf_op jit(solution)/shard_map/jit(_where)/broadcast_in_dim | solution.py:162
  368.2 12.3 %broadcast_in_dim.202 = bf16[8,48,256]{1,2,0:T(8,128)(2,1)} reshape(bf16[8,4,2,6,16,4,2,2]{3,2,1,7,6,5,4,0:T(2,128)(2,1)} %broadcast_in_dim.201) | data formatting | bytes 393216 | tf_op jit(solution)/shard_map/jit(_where)/broadcast_in_dim | solution.py:162
  384.5 10.8 %all_to_all.20 = bf16[2,2,8,12,512]{4,2,3,1,0:T(8,128)(2,1)S(1)} all-to-all(bf16[2,2,8,12,512]{4,2,3,1,0:T(8,128)(2,1)S(1)} %copy.264), channel_id=1, replica_groups=mesh['dp'=8,'x'=4,'y'=4,'zh'=2,'core'=2] {'core'}, dimensions={0} | all-to-all | bytes 786432 | tf_op jit(solution)/shard_map/all_to_all | solution.py:178
  395.6 19.5 %all_to_all.21 = bf16[16,12,512]{2,1,0:T(8,128)(2,1)S(1)} all-to-all(bf16[16,12,512]{2,1,0:T(8,128)(2,1)S(1)} %copy.267), channel_id=1, replica_groups=mesh['dp'=8,'x'=4,'y'=4,'zh'=2,'core'=2] {'zh','dp'}, dimensions={0} | all-to-all | bytes 393216 | tf_op jit(solution)/shard_map/all_to_all | solution.py:182
  (127 shorter events, 39.0 us)
Async XLA Ops:
  6.5 291.3 %copy-start = (bf16[1,1024,512]{2,1,0:T(8,128)(2,1)S(1)}, bf16[1,1024,512]{2,1,0:T(8,128)(2,1)}, u32[]{:S(2)}) copy-start(bf16[1,1024,512]{2,1,0:T(8,128)(2,1)} %param.19) | copy-start | bytes 3145732
  33.8 4.8 %copy-start.1 = (bf16[48,4224]{1,0:T(8,128)(2,1)}, bf16[48,4224]{1,0:T(8,128)(2,1)S(1)}, u32[]{:S(2)}) copy-start(bf16[48,4224]{1,0:T(8,128)(2,1)S(1)} %reshape.244) | copy-start | bytes 1216516
  38.6 6.0 %copy-start.7 = (s32[64]{0:T(128)S(1)}, s32[64]{0:T(128)}, u32[]{:S(2)}) copy-start(s32[64]{0:T(128)} %param.15) | copy-start | bytes 772
  38.6 7.4 %copy-start.3 = (s32[2,8,64]{2,1,0:T(8,128)S(1)}, s32[2,8,64]{2,1,0:T(8,128)}, u32[]{:S(2)}) copy-start(s32[2,8,64]{2,1,0:T(8,128)} %param.16) | copy-start | bytes 12292
  38.6 35.7 %all-to-all-start = ((bf16[16,16,4224]{2,1,0:T(8,128)(2,1)}), bf16[16,16,4224]{2,1,0:T(8,128)(2,1)S(1)}, u32[]{:S(2)}, u32[]{:S(2)}) async-start(bf16[16,16,4224]{2,1,0:T(8,128)(2,1)} %bitcast.81), calls=%async_computation | async-start | bytes 4325376 | tf_op jit(solution)/shard_map/all_to_all | solution.py:84
  44.4 32.3 %slice-start = ((bf16[48,4224]{1,0:T(8,128)(2,1)}), bf16[48,128]{1,0:T(8,128)(2,1)S(1)}, s32[]{:S(2)}) async-start(bf16[48,4224]{1,0:T(8,128)(2,1)} %copy-done.1), calls=%async_computation.6 | async-start | bytes 24576 | tf_op jit(solution)/shard_map/slice | solution.py:73
  44.4 188.0 %all-gather.5.cloned.1.call-start = ((), (), s32[]{:S(2)}) async-start(), calls=%async_computation.4 | async-start | bytes 7299072 | tf_op jit(solution)/shard_map/all_gather | solution.py:118
  76.5 155.9 %copy-start.5 = (bf16[1,4096,128]{2,1,0:T(8,128)(2,1)S(1)}, bf16[1,4096,128]{2,1,0:T(8,128)(2,1)}, u32[]{:S(2)}) copy-start(bf16[1,4096,128]{2,1,0:T(8,128)(2,1)} %param.17) | copy-start | bytes 3145732
  77.8 159.3 %copy-start.6 = (bf16[1,4096,128]{2,1,0:T(8,128)(2,1)S(1)}, bf16[1,4096,128]{2,1,0:T(8,128)(2,1)}, u32[]{:S(2)}) copy-start(bf16[1,4096,128]{2,1,0:T(8,128)(2,1)} %param.18) | copy-start | bytes 3145732
  77.8 220.0 %all-gather.7.cloned.1.call-start = ((), (), s32[]{:S(2)}) async-start(), calls=%async_computation.5 | async-start | bytes 1769472 | tf_op jit(solution)/shard_map/all_gather | solution.py:125
  232.4 4.7 %copy-start.4 = (bf16[768,4224]{1,0:T(8,128)(2,1)S(1)}, bf16[768,4224]{1,0:T(8,128)(2,1)}, u32[]{:S(2)}) copy-start(bf16[768,4224]{1,0:T(8,128)(2,1)} %all-gather.5.cloned.1.call-done) | copy-start | bytes 19464196
  302.9 80.5 %all-to-all-start.1 = ((bf16[16,8,16,512]{3,2,1,0:T(8,128)(2,1)}), bf16[16,8,16,512]{3,2,1,0:T(8,128)(2,1)S(1)}, u32[]{:S(2)}, u32[]{:S(2)}) async-start(bf16[16,8,16,512]{3,2,1,0:T(8,128)(2,1)} %bitcast.83), calls=%async_computation.1 | async-start | bytes 4194304 | tf_op jit(solution)/shard_map/all_to_all | solution.py:143
  330.9 9.9 %copy-start.2 = (pred[8,4,2,6,16]{3,2,1,4,0:T(4,128)(4,1)S(1)}, pred[8,4,2,6,16]{3,2,1,4,0:T(4,128)(4,1)}, u32[]{:S(2)}) copy-start(pred[8,4,2,6,16]{3,2,1,4,0:T(4,128)(4,1)} %copy.250) | copy-start | bytes 18436
Sparse Core Ops, SparseCore 0:
  77.9 154.4 all-gather.4
  239.7 58.0 all-gather.6

commit v2 on v1

v2 whole, which is shorter than its diff:
```python
import jax
import jax.numpy as jnp
from jax import lax
from jax.sharding import Mesh, PartitionSpec as P

BF = jnp.bfloat16
F32 = jnp.float32
LANES = 128
ROWS = 48
MOST = 2
HOME, HI, MID, ONE, POS = 0, 8, 16, 32, 33


def split_gates(gates):
    high = lax.reduce_precision(gates, 8, 7)
    mid = lax.reduce_precision(gates - high, 8, 7)
    return high.astype(BF), mid.astype(BF)


def pack_meta(experts, replicas, gates, table):
    labels = jnp.arange(table.shape[0], dtype=jnp.int32)
    hot = experts[..., None] == labels
    picked = jnp.where(replicas[..., None] == 0, table[:, 0], table[:, 1])
    home = jnp.sum(jnp.where(hot, picked, 0), axis=-1)
    high, mid = split_gates(gates)
    one = jnp.ones(home.shape, BF)
    meta = jnp.concatenate([home.astype(BF), high, mid, one, one], axis=-1)
    return jnp.pad(meta, ((0, 0), (0, LANES - meta.shape[-1])))


def places(meta, me, columns, quad, tok, top):
    n = meta.shape[0]
    box = jnp.arange(columns * quad * MOST, dtype=jnp.int32)[None, :]
    row = jnp.arange(n, dtype=jnp.int32)[:, None]
    target = (box // (quad * MOST) * quad + me).astype(BF)
    same = (row // tok) % quad == (box // MOST) % quad
    hits = [(meta[:, HOME + k : HOME + k + 1] == target) & same for k in range(top)]
    match = hits[0]
    for hit in hits[1:]:
        match = match | hit
    other = jnp.arange(n, dtype=jnp.int32)[None, :]
    before = ((row // tok == other // tok) & (other < row)).astype(BF)
    earlier = jnp.dot(before, match.astype(BF), preferred_element_type=F32)
    return hits, match & (earlier == (box % MOST).astype(F32))


def on_device(
    tokens, experts, replicas, route_weights, slot_tables, partners, slot_rows, gate_w, up_w, down_w
):
    steps, tok, model = tokens.shape
    top = experts.shape[-1]
    n_dp = lax.axis_size("dp")
    columns = lax.axis_size("x") * lax.axis_size("y")
    quad = lax.axis_size("zh") * lax.axis_size("core")
    me = lax.axis_index("zh") * lax.axis_size("core") + lax.axis_index("core")
    column = lax.axis_index("x") * lax.axis_size("y") + lax.axis_index("y")
    my_home = column * quad + me
    my_dp = lax.axis_index("dp")
    mine = steps * tok
    group = quad * tok
    boxes = columns * quad * MOST
    wide = model + LANES
    width = down_w.shape[2]

    right = [[(i, i + 1) for i in range(j, n_dp - 1)] for j in range(n_dp - 1)]
    left = [[(i + 1, i) for i in range(n_dp - 1 - j)] for j in range(n_dp - 1)]

    meta = pack_meta(
        experts.reshape(mine, top),
        replicas.reshape(mine, top),
        route_weights.reshape(mine, top),
        slot_tables[0],
    )
    packed = jnp.concatenate([tokens.reshape(mine, model), meta], axis=1)
    held = lax.all_gather(packed.reshape(steps, tok, wide), ("zh", "core"), axis=1, tiled=True)

    labels = jnp.arange(partners.shape[0], dtype=jnp.int32)
    partner_me = jnp.sum(jnp.where(labels == my_home, partners, 0))
    owners = (my_home, partner_me)
    lanes = jnp.arange(LANES, dtype=jnp.int32)[None, :]
    line = jnp.arange(boxes, dtype=jnp.int32)
    lower = (line[:, None] < line[None, :]).astype(BF)

    def dispatch(step):
        local = held[step]
        local_meta = local[:, model:]
        place = places(local_meta, me, columns, quad, tok, top)[1]
        buffer = lax.dot_general(
            place.astype(BF), local, (((0,), (0,)), ((), ())), preferred_element_type=F32
        ).astype(BF)
        arrived = lax.all_to_all(
            buffer.reshape(columns, quad * MOST, wide),
            ("x", "y"),
            split_axis=0,
            concat_axis=0,
            tiled=True,
        ).reshape(boxes, wide)
        valid = arrived[:, model + ONE]
        rank = jnp.dot(valid[None, :], lower, preferred_element_type=F32)
        which = (jnp.arange(n_dp, dtype=jnp.int32)[:, None] == my_dp) & (
            labels[None, :] == owners[step]
        )
        limit = jnp.sum(jnp.where(which, slot_rows[step], 0)).astype(F32)
        kept = (valid[None, :] > 0) & (rank < limit)
        slot_row = jnp.arange(ROWS, dtype=jnp.int32).astype(F32)[:, None]
        chosen = kept & (rank == slot_row)
        pick = chosen.astype(BF)
        compact = jnp.dot(pick, arrived[:, :model], preferred_element_type=F32).astype(BF)
        position = jnp.sum(
            jnp.where(chosen, line.astype(F32)[None, :] + 1.0, 0.0), axis=1, keepdims=True
        )
        side = jnp.pad(local_meta, ((0, ROWS - group), (0, 0)))
        side = jnp.where(lanes == POS, position.astype(BF), side)
        return jnp.concatenate([compact, side], axis=1)

    def project(block):
        x = block[:, :model]
        gate = jnp.dot(x, gate_w[0], preferred_element_type=F32)
        up = jnp.dot(x, up_w[0], preferred_element_type=F32)
        hidden = (jax.nn.silu(gate) * up).astype(BF)
        return jnp.concatenate([hidden, block[:, model:]], axis=1)

    own = [dispatch(step) for step in range(steps)]
    by_offset = [[project(block)] + [None] * (n_dp - 1) for block in own]
    to_right, to_left = list(own), list(own)
    from_left = [[None] * n_dp for _ in range(steps)]
    from_right = [[None] * n_dp for _ in range(steps)]
    for j in range(n_dp - 1):
        for s in range(steps):
            to_right[s] = lax.ppermute(to_right[s], "dp", right[j])
            to_left[s] = lax.ppermute(to_left[s], "dp", left[j])
            both = project(jnp.concatenate([to_right[s], to_left[s]], axis=0))
            from_left[s][j + 1], from_right[s][j + 1] = both[:ROWS], both[ROWS:]
    for s in range(steps):
        for m in range(1, n_dp):
            by_offset[s][m] = from_right[s][m] + from_left[s][n_dp - m]
    ordered = jnp.stack([jnp.stack(blocks) for blocks in by_offset], axis=1)
    ordered = lax.dynamic_slice_in_dim(
        jnp.concatenate([ordered, ordered], axis=0), n_dp - my_dp, n_dp, axis=0
    )
    batch = n_dp * steps
    hidden = ordered[..., :LANES].reshape(batch * ROWS, LANES)
    sides = ordered[..., LANES:].reshape(batch, ROWS, LANES)

    down = down_w[0].reshape(n_dp, LANES, width)

    def shard(index):
        return lax.dynamic_index_in_dim(down, lax.rem(index + n_dp, n_dp), 0, keepdims=False)

    total = jnp.dot(hidden, shard(my_dp), preferred_element_type=F32)
    going_right, going_left = hidden, hidden
    for j in range(n_dp - 1):
        going_right = lax.ppermute(going_right, "dp", right[j])
        going_left = lax.ppermute(going_left, "dp", left[j])
        total = total + jnp.dot(
            jnp.concatenate([going_right, going_left], axis=1),
            jnp.concatenate([shard(my_dp - j - 1), shard(my_dp + j + 1)], axis=0),
            preferred_element_type=F32,
        )
    output = total.astype(BF)

    positions = sides[:, :, POS].astype(jnp.int32) - 1
    unpick = (line[None, :, None] == positions[:, None, :]).astype(BF)
    spread = jnp.einsum(
        "bpr,brf->bpf",
        unpick,
        output.reshape(batch, ROWS, width),
        preferred_element_type=F32,
    ).astype(BF)
    back = lax.all_to_all(
        spread.reshape(batch, columns, quad * MOST, width).transpose(1, 0, 2, 3),
        ("x", "y"),
        split_axis=0,
        concat_axis=0,
        tiled=True,
    )

    token_meta = sides[:, :group].reshape(batch * group, LANES)
    hits, place = places(token_meta, me, columns, quad, tok, top)
    parts = []
    for lane in (HI, MID):
        weight = jnp.zeros((batch * group, boxes), F32)
        for k in range(top):
            weight = jnp.where(
                hits[k], token_meta[:, lane + k : lane + k + 1].astype(F32), weight
            )
        parts.append(jnp.where(place, weight, 0.0).astype(BF).reshape(batch, group, boxes))
    sums = jnp.einsum(
        "btp,bpf->btf",
        jnp.concatenate(parts, axis=1),
        back.transpose(1, 0, 2, 3).reshape(batch, boxes, width),
        preferred_element_type=F32,
    )
    partial = (sums[:, :group] + sums[:, group:]).astype(BF)
    partial = partial.reshape(n_dp, steps, 2, 2, tok, width).transpose(3, 2, 0, 1, 4, 5)
    swapped = lax.all_to_all(partial, "core", split_axis=0, concat_axis=0, tiled=True)
    halves = jnp.sum(swapped.astype(F32), axis=0).astype(BF)
    pieces = lax.all_to_all(
        halves.reshape(2 * n_dp, mine, width),
        ("zh", "dp"),
        split_axis=0,
        concat_axis=0,
        tiled=True,
    ).reshape(2, n_dp, mine, width)
    mixed = jnp.sum(pieces.astype(F32), axis=0).astype(BF)
    return mixed.transpose(1, 0, 2).reshape(steps, tok, model)


def solution(mesh):
    names = ("dp", "x", "y", "zh", "core")
    grid = Mesh(mesh.devices.reshape(mesh.shape["dp"], 4, 4, 2, 2), names)
    ep = ("x", "y", "zh", "core")
    rows = P(None, names, None)
    return jax.shard_map(
        on_device,
        mesh=grid,
        in_specs=(
            rows,
            rows,
            rows,
            rows,
            P(),
            P(),
            P(),
            P(ep, None, "dp"),
            P(ep, None, "dp"),
            P(ep, None, "dp"),
        ),
        out_specs=rows,
        check_vma=False,
    )
```

time: 428 us -> 345 us (0.81)
  waiting for transfers between devices: 239 us -> 165 us
  local copies, waits for them, and re-layouts: 70.8 us -> 9.75 us
  starting transfers between devices: 12.7 us -> 69.8 us
  other arithmetic: 19.7 us -> 8.42 us
  between operations: 13.8 us -> 2.81 us
  matrix products: 13.9 us -> 23.9 us
  blocking collectives: 52.6 us -> 60.4 us
    all_gather x2 -> x0, waiting for transfers between devices: 211 us -> none  [the longest x1 155 us: on_device(): lax.all_gather(jnp.concatenate([compact, side], axis=1), 'dp', axis=0, ti...]
    ppermute x0 -> x42, waiting for transfers between devices: none -> 126 us  [the longest x14 87.5 us: on_device(): to_left[s] = lax.ppermute(to_left[s], 'dp', left[j])]
    ppermute x0 -> x42, starting transfers between devices: none -> 54.2 us  [the longest x14 21.5 us: on_device(): to_right[s] = lax.ppermute(to_right[s], 'dp', right[j])]
    broadcast_in_dim x13 -> x0, local copies, waits for them, and re-layouts: 47.1 us -> none  [the longest x9 40.6 us: on_device(): jnp.where(same_q[None, :, None, None, None, :, None, None] & same_u[None,...]
    all_to_all x2 -> x3, waiting for transfers between devices: 28.1 us -> 39.8 us  [the longest x2 25.5 us: dispatch(): lax.all_to_all(buffer.reshape(columns, quad * MOST, wide), ('x', 'y'), sp...]
    dot_general x8 -> x49, matrix products: 13.9 us -> 23.9 us  [the longest x16 6.13 us: project(): gate = jnp.dot(x, gate_w[0], preferred_element_type=F32)]
    all_to_all x1, blocking collectives: 10.8 us -> 16.9 us  [on_device(): lax.all_to_all(partial, 'core', split_axis=0, concat_axis=0, tiled=True)]
    all_to_all x2 -> x3, starting transfers between devices: 12.6 us -> 15.6 us  [the longest x2 9.9 us: dispatch(): lax.all_to_all(buffer.reshape(columns, quad * MOST, wide), ('x', 'y'), sp...]
  transfers between devices with their start and end apart: 4 -> 45, of which waited for: 3 -> 25; matrix products, arithmetic and copies ran while one was open for 18% -> 7% of each run, Pallas kernels for 0% -> 0%
where the time goes in v2:
time: 345 us; the launch traced here: 340 us
  waiting for transfers between devices  165 us (48%)
  starting transfers between devices  69.8 us (20%)
  blocking collectives  60.4 us (18%)
  matrix products  23.9 us (7%)
  local copies, waits for them, and re-layouts  9.75 us (3%)
  other arithmetic  8.42 us (2%)
    ppermute x14, waiting for transfers between devices, on_device(): to_left[s] = lax.ppermute(to_left[s], 'dp', left[j])  87.5 us
    ppermute x7, waiting for transfers between devices, on_device(): going_left = lax.ppermute(going_left, 'dp', left[j])  30.9 us
    all_to_all x2, waiting for transfers between devices, dispatch(): lax.all_to_all(buffer.reshape(columns, quad * MOST, wide), ('x', 'y'), sp...  25.5 us
    all_to_all x1, blocking collectives, on_device(): lax.all_to_all(halves.reshape(2 * n_dp, mine, width), ('zh', 'dp'), split...  21.8 us
    all_gather x1, blocking collectives, on_device(): lax.all_gather(packed.reshape(steps, tok, wide), ('zh', 'core'), axis=1,...  21.7 us
    ppermute x14, starting transfers between devices, on_device(): to_right[s] = lax.ppermute(to_right[s], 'dp', right[j])  21.5 us
    ppermute x14, starting transfers between devices, on_device(): to_left[s] = lax.ppermute(to_left[s], 'dp', left[j])  18.1 us
    all_to_all x1, blocking collectives, on_device(): lax.all_to_all(partial, 'core', split_axis=0, concat_axis=0, tiled=True)  16.9 us
  transfers between devices with their start and end apart: 45, of which 25 were waited for; matrix products, arithmetic and copies ran while one was open for 7% of the time, Pallas kernels for 0%

profile of v2, /device:TPU:1, one launch (start us, length us, event | category | flops | bytes accessed | tf_op | source)
XLA Modules:
  0.0 340.4 jit_solution(6828685501850497981)
XLA Ops:
  4.8 21.7 %all_gather.3 = bf16[2,24,4224]{2,0,1:T(2,128)(2,1)S(1)} all-gather(bf16[2,6,4224]{2,0,1:T(2,128)(2,1)S(1)} %pad_maximum_fusion.2), channel_id=1, replica_groups=mesh['dp'=8,'x'=4,'y'=4,'zh'=2,'core'=2] {'zh','core'}, dimensions={1}, use_global_device_ids=true | all-gather | bytes 506880 | tf_op jit(solution)/shard_map/all_gather | solution.py:75
  29.1 5.5 %all-to-all-start.1 = ((bf16[16,8,4224]{2,1,0:T(8,128)(2,1)}), bf16[16,8,4224]{2,1,0:T(8,128)(2,1)S(1)}, u32[]{:S(2)}, u32[]{:S(2)}) async-start(bf16[16,8,4224]{2,1,0:T(8,128)(2,1)} %fusion.1), calls=%async_computation.1 | async-start | bytes 2162688 | tf_op jit(solution)/shard_map/all_to_all | solution.py:91
  36.6 14.5 %all-to-all-done.1 = bf16[16,8,4224]{2,1,0:T(8,128)(2,1)S(1)} async-done(((bf16[16,8,4224]{2,1,0:T(8,128)(2,1)}), bf16[16,8,4224]{2,1,0:T(8,128)(2,1)S(1)}, u32[]{:S(2)}, u32[]{:S(2)}) %all-to-all-start.1) | async-done | bytes 1081376 | tf_op jit(solution)/shard_map/all_to_all | solution.py:91
  59.7 11.0 %all-to-all-done = bf16[16,8,4224]{2,1,0:T(8,128)(2,1)S(1)} async-done(((bf16[16,8,4224]{2,1,0:T(8,128)(2,1)}), bf16[16,8,4224]{2,1,0:T(8,128)(2,1)S(1)}, u32[]{:S(2)}, u32[]{:S(2)}) %all-to-all-start) | async-done | bytes 1081376 | tf_op jit(solution)/shard_map/all_to_all | solution.py:91
  71.8 9.0 %collective-permute-start.14 = (bf16[48,4224]{1,0:T(8,128)(2,1)S(1)}, bf16[48,4224]{1,0:T(8,128)(2,1)S(1)}, u32[]{:S(2)}, u32[]{:S(2)}) collective-permute-start(bf16[48,4224]{1,0:T(8,128)(2,1)S(1)} %pad_maximum_fusion.1), channel_id=1, source_target_pairs={{0,64},{64,128},{128,192},{192,256},{256,320},{320,384},{384,448},... | collective-permute-start | bytes 1216520 | tf_op jit(solution)/shard_map/ppermute | solution.py:130
  90.0 5.9 %collective-permute-done = bf16[48,4224]{1,0:T(8,128)(2,1)S(1)} collective-permute-done((bf16[48,4224]{1,0:T(8,128)(2,1)S(1)}, bf16[48,4224]{1,0:T(8,128)(2,1)S(1)}, u32[]{:S(2)}, u32[]{:S(2)}) %collective-permute-start) | collective-permute-done | bytes 405536 | tf_op jit(solution)/shard_map/ppermute | solution.py:130
  104.9 5.1 %collective-permute-done.22 = bf16[48,4224]{1,0:T(8,128)(2,1)S(1)} collective-permute-done((bf16[48,4224]{1,0:T(8,128)(2,1)S(1)}, bf16[48,4224]{1,0:T(8,128)(2,1)S(1)}, u32[]{:S(2)}, u32[]{:S(2)}) %collective-permute-start.22) | collective-permute-done | bytes 405536 | tf_op jit(solution)/shard_map/ppermute | solution.py:131
  110.9 7.9 %collective-permute-done.8 = bf16[48,4224]{1,0:T(8,128)(2,1)S(1)} collective-permute-done((bf16[48,4224]{1,0:T(8,128)(2,1)S(1)}, bf16[48,4224]{1,0:T(8,128)(2,1)S(1)}, u32[]{:S(2)}, u32[]{:S(2)}) %collective-permute-start.8) | collective-permute-done | bytes 405536 | tf_op jit(solution)/shard_map/ppermute | solution.py:131
  128.7 7.9 %collective-permute-done.9 = bf16[48,4224]{1,0:T(8,128)(2,1)S(1)} collective-permute-done((bf16[48,4224]{1,0:T(8,128)(2,1)S(1)}, bf16[48,4224]{1,0:T(8,128)(2,1)S(1)}, u32[]{:S(2)}, u32[]{:S(2)}) %collective-permute-start.9) | collective-permute-done | bytes 405536 | tf_op jit(solution)/shard_map/ppermute | solution.py:131
  141.6 6.4 %collective-permute-done.24 = bf16[48,4224]{1,0:T(8,128)(2,1)S(1)} collective-permute-done((bf16[48,4224]{1,0:T(8,128)(2,1)S(1)}, bf16[48,4224]{1,0:T(8,128)(2,1)S(1)}, u32[]{:S(2)}, u32[]{:S(2)}) %collective-permute-start.24) | collective-permute-done | bytes 405536 | tf_op jit(solution)/shard_map/ppermute | solution.py:131
  148.9 7.8 %collective-permute-done.10 = bf16[48,4224]{1,0:T(8,128)(2,1)S(1)} collective-permute-done((bf16[48,4224]{1,0:T(8,128)(2,1)S(1)}, bf16[48,4224]{1,0:T(8,128)(2,1)S(1)}, u32[]{:S(2)}, u32[]{:S(2)}) %collective-permute-start.10) | collective-permute-done | bytes 405536 | tf_op jit(solution)/shard_map/ppermute | solution.py:131
  161.6 7.8 %collective-permute-done.25 = bf16[48,4224]{1,0:T(8,128)(2,1)S(1)} collective-permute-done((bf16[48,4224]{1,0:T(8,128)(2,1)S(1)}, bf16[48,4224]{1,0:T(8,128)(2,1)S(1)}, u32[]{:S(2)}, u32[]{:S(2)}) %collective-permute-start.25) | collective-permute-done | bytes 405536 | tf_op jit(solution)/shard_map/ppermute | solution.py:131
  170.2 7.8 %collective-permute-done.11 = bf16[48,4224]{1,0:T(8,128)(2,1)S(1)} collective-permute-done((bf16[48,4224]{1,0:T(8,128)(2,1)S(1)}, bf16[48,4224]{1,0:T(8,128)(2,1)S(1)}, u32[]{:S(2)}, u32[]{:S(2)}) %collective-permute-start.11) | collective-permute-done | bytes 405536 | tf_op jit(solution)/shard_map/ppermute | solution.py:131
  183.0 8.0 %collective-permute-done.26 = bf16[48,4224]{1,0:T(8,128)(2,1)S(1)} collective-permute-done((bf16[48,4224]{1,0:T(8,128)(2,1)S(1)}, bf16[48,4224]{1,0:T(8,128)(2,1)S(1)}, u32[]{:S(2)}, u32[]{:S(2)}) %collective-permute-start.26) | collective-permute-done | bytes 405536 | tf_op jit(solution)/shard_map/ppermute | solution.py:131
  191.9 7.8 %collective-permute-done.12 = bf16[48,4224]{1,0:T(8,128)(2,1)S(1)} collective-permute-done((bf16[48,4224]{1,0:T(8,128)(2,1)S(1)}, bf16[48,4224]{1,0:T(8,128)(2,1)S(1)}, u32[]{:S(2)}, u32[]{:S(2)}) %collective-permute-start.12) | collective-permute-done | bytes 405536 | tf_op jit(solution)/shard_map/ppermute | solution.py:131
  204.0 5.2 %collective-permute-done.27 = bf16[48,4224]{1,0:T(8,128)(2,1)S(1)} collective-permute-done((bf16[48,4224]{1,0:T(8,128)(2,1)S(1)}, bf16[48,4224]{1,0:T(8,128)(2,1)S(1)}, u32[]{:S(2)}, u32[]{:S(2)}) %collective-permute-start.27) | collective-permute-done | bytes 405536 | tf_op jit(solution)/shard_map/ppermute | solution.py:131
  209.7 8.2 %collective-permute-done.13 = bf16[48,4224]{1,0:T(8,128)(2,1)S(1)} collective-permute-done((bf16[48,4224]{1,0:T(8,128)(2,1)S(1)}, bf16[48,4224]{1,0:T(8,128)(2,1)S(1)}, u32[]{:S(2)}, u32[]{:S(2)}) %collective-permute-start.13) | collective-permute-done | bytes 405536 | tf_op jit(solution)/shard_map/ppermute | solution.py:131
  229.5 5.5 %collective-permute-done.31 = bf16[768,128]{1,0:T(8,128)(2,1)} collective-permute-done((bf16[768,128]{1,0:T(8,128)(2,1)S(1)}, bf16[768,128]{1,0:T(8,128)(2,1)}, u32[]{:S(2)}, u32[]{:S(2)}) %collective-permute-start.31) | collective-permute-done | bytes 196640 | tf_op jit(solution)/shard_map/ppermute | solution.py:154
  237.2 6.3 %collective-permute-done.33 = bf16[768,128]{1,0:T(8,128)(2,1)S(1)} collective-permute-done((bf16[768,128]{1,0:T(8,128)(2,1)}, bf16[768,128]{1,0:T(8,128)(2,1)S(1)}, u32[]{:S(2)}, u32[]{:S(2)}) %collective-permute-start.33) | collective-permute-done | bytes 196640 | tf_op jit(solution)/shard_map/ppermute | solution.py:154
  246.3 4.9 %collective-permute-done.35 = bf16[768,128]{1,0:T(8,128)(2,1)S(1)} collective-permute-done((bf16[768,128]{1,0:T(8,128)(2,1)S(1)}, bf16[768,128]{1,0:T(8,128)(2,1)S(1)}, u32[]{:S(2)}, u32[]{:S(2)}) %collective-permute-start.35) | collective-permute-done | bytes 196640 | tf_op jit(solution)/shard_map/ppermute | solution.py:154
  274.4 5.7 %all-to-all-start.2 = ((bf16[16,16,8,512]{3,2,1,0:T(8,128)(2,1)}), bf16[16,16,8,512]{3,2,1,0:T(8,128)(2,1)S(1)}, u32[]{:S(2)}, u32[]{:S(2)}) async-start(bf16[16,16,8,512]{3,2,1,0:T(8,128)(2,1)} %bitcast.268), calls=%async_computation.2 | async-start | bytes 4194304 | tf_op jit(solution)/shard_map/all_to_all | solution.py:170
  284.2 14.3 %all-to-all-done.2 = bf16[16,16,8,512]{3,2,1,0:T(8,128)(2,1)S(1)} async-done(((bf16[16,16,8,512]{3,2,1,0:T(8,128)(2,1)}), bf16[16,16,8,512]{3,2,1,0:T(8,128)(2,1)S(1)}, u32[]{:S(2)}, u32[]{:S(2)}) %all-to-all-start.2) | async-done | bytes 2097184 | tf_op jit(solution)/shard_map/all_to_all | solution.py:170
  299.7 16.9 %all_to_all.25 = bf16[2,2,8,2,6,512]{5,3,2,4,1,0:T(2,128)(2,1)S(1)} all-to-all(bf16[2,2,8,2,6,512]{5,3,2,4,1,0:T(2,128)(2,1)S(1)} %copy.95), channel_id=1, replica_groups=mesh['dp'=8,'x'=4,'y'=4,'zh'=2,'core'=2] {'core'}, dimensions={0} | all-to-all | bytes 786432 | tf_op jit(solution)/shard_map/all_to_all | solution.py:196
  317.6 21.8 %all_to_all.26 = bf16[16,12,512]{2,1,0:T(8,128)(2,1)S(1)} all-to-all(bf16[16,12,512]{2,1,0:T(8,128)(2,1)S(1)} %copy.98), channel_id=1, replica_groups=mesh['dp'=8,'x'=4,'y'=4,'zh'=2,'core'=2] {'zh','dp'}, dimensions={0} | all-to-all | bytes 393216 | tf_op jit(solution)/shard_map/all_to_all | solution.py:198
  (255 shorter events, 114.6 us)
Async XLA Ops:
  29.1 22.0 %all-to-all-start.1 = ((bf16[16,8,4224]{2,1,0:T(8,128)(2,1)}), bf16[16,8,4224]{2,1,0:T(8,128)(2,1)S(1)}, u32[]{:S(2)}, u32[]{:S(2)}) async-start(bf16[16,8,4224]{2,1,0:T(8,128)(2,1)} %fusion.1), calls=%async_computation.1 | async-start | bytes 2162688 | tf_op jit(solution)/shard_map/all_to_all | solution.py:91
  51.1 19.6 %all-to-all-start = ((bf16[16,8,4224]{2,1,0:T(8,128)(2,1)}), bf16[16,8,4224]{2,1,0:T(8,128)(2,1)S(1)}, u32[]{:S(2)}, u32[]{:S(2)}) async-start(bf16[16,8,4224]{2,1,0:T(8,128)(2,1)} %fusion), calls=%async_computation | async-start | bytes 2162688 | tf_op jit(solution)/shard_map/all_to_all | solution.py:91
  71.8 17.4 %collective-permute-start.14 = (bf16[48,4224]{1,0:T(8,128)(2,1)S(1)}, bf16[48,4224]{1,0:T(8,128)(2,1)S(1)}, u32[]{:S(2)}, u32[]{:S(2)}) collective-permute-start(bf16[48,4224]{1,0:T(8,128)(2,1)S(1)} %pad_maximum_fusion.1), channel_id=1, source_target_pairs={{0,64},{64,128},{128,192},{192,256},{256,320},{320,384},{384,448},... | collective-permute-start | bytes 1216520 | tf_op jit(solution)/shard_map/ppermute | solution.py:130
  80.8 15.1 %collective-permute-start.15 = (bf16[48,4224]{1,0:T(8,128)(2,1)S(1)}, bf16[48,4224]{1,0:T(8,128)(2,1)S(1)}, u32[]{:S(2)}, u32[]{:S(2)}) collective-permute-start(bf16[48,4224]{1,0:T(8,128)(2,1)S(1)} %pad_maximum_fusion.1), channel_id=1, source_target_pairs={{64,0},{128,64},{192,128},{256,192},{320,256},{384,320},{448,384},... | collective-permute-start | bytes 1216520 | tf_op jit(solution)/shard_map/ppermute | solution.py:131
  82.5 13.4 %collective-permute-start = (bf16[48,4224]{1,0:T(8,128)(2,1)S(1)}, bf16[48,4224]{1,0:T(8,128)(2,1)S(1)}, u32[]{:S(2)}, u32[]{:S(2)}) collective-permute-start(bf16[48,4224]{1,0:T(8,128)(2,1)S(1)} %pad_maximum_fusion), channel_id=1, source_target_pairs={{0,64},{64,128},{128,192},{192,256},{256,320},{320,384},{384,448},... | collective-permute-start | bytes 1216520 | tf_op jit(solution)/shard_map/ppermute | solution.py:130
  86.6 13.4 %collective-permute-start.1 = (bf16[48,4224]{1,0:T(8,128)(2,1)S(1)}, bf16[48,4224]{1,0:T(8,128)(2,1)S(1)}, u32[]{:S(2)}, u32[]{:S(2)}) collective-permute-start(bf16[48,4224]{1,0:T(8,128)(2,1)S(1)} %pad_maximum_fusion), channel_id=1, source_target_pairs={{64,0},{128,64},{192,128},{256,192},{320,256},{384,320},{448,384},... | collective-permute-start | bytes 1216520 | tf_op jit(solution)/shard_map/ppermute | solution.py:131
  89.2 14.9 %collective-permute-start.16 = (bf16[48,4224]{1,0:T(8,128)(2,1)S(1)}, bf16[48,4224]{1,0:T(8,128)(2,1)S(1)}, u32[]{:S(2)}, u32[]{:S(2)}) collective-permute-start(bf16[48,4224]{1,0:T(8,128)(2,1)S(1)} %collective-permute-done.14), channel_id=1, source_target_pairs={{64,128},{128,192},{192,256},{256,320},{320,384},{384,448},{65,129... | collective-permute-start | bytes 1216520 | tf_op jit(solution)/shard_map/ppermute | solution.py:130
  100.5 9.6 %collective-permute-start.22 = (bf16[48,4224]{1,0:T(8,128)(2,1)S(1)}, bf16[48,4224]{1,0:T(8,128)(2,1)S(1)}, u32[]{:S(2)}, u32[]{:S(2)}) collective-permute-start(bf16[48,4224]{1,0:T(8,128)(2,1)S(1)} %collective-permute-done.15), channel_id=1, source_target_pairs={{64,0},{128,64},{192,128},{256,192},{320,256},{384,320},{65,1},{12... | collective-permute-start | bytes 1216520 | tf_op jit(solution)/shard_map/ppermute | solution.py:131
  102.5 16.3 %collective-permute-start.8 = (bf16[48,4224]{1,0:T(8,128)(2,1)S(1)}, bf16[48,4224]{1,0:T(8,128)(2,1)S(1)}, u32[]{:S(2)}, u32[]{:S(2)}) collective-permute-start(bf16[48,4224]{1,0:T(8,128)(2,1)S(1)} %collective-permute-done.1), channel_id=1, source_target_pairs={{64,0},{128,64},{192,128},{256,192},{320,256},{384,320},{65,1},{12... | collective-permute-start | bytes 1216520 | tf_op jit(solution)/shard_map/ppermute | solution.py:131
  104.1 18.7 %collective-permute-start.17 = (bf16[48,4224]{1,0:T(8,128)(2,1)S(1)}, bf16[48,4224]{1,0:T(8,128)(2,1)S(1)}, u32[]{:S(2)}, u32[]{:S(2)}) collective-permute-start(bf16[48,4224]{1,0:T(8,128)(2,1)S(1)} %collective-permute-done.16), channel_id=1, source_target_pairs={{128,192},{192,256},{256,320},{320,384},{384,448},{129,193},{193,2... | collective-permute-start | bytes 1216520 | tf_op jit(solution)/shard_map/ppermute | solution.py:130
  121.2 15.4 %collective-permute-start.9 = (bf16[48,4224]{1,0:T(8,128)(2,1)S(1)}, bf16[48,4224]{1,0:T(8,128)(2,1)S(1)}, u32[]{:S(2)}, u32[]{:S(2)}) collective-permute-start(bf16[48,4224]{1,0:T(8,128)(2,1)S(1)} %collective-permute-done.8), channel_id=1, source_target_pairs={{64,0},{128,64},{192,128},{256,192},{320,256},{65,1},{129,65},{193... | collective-permute-start | bytes 1216520 | tf_op jit(solution)/shard_map/ppermute | solution.py:131
  122.9 17.8 %collective-permute-start.18 = (bf16[48,4224]{1,0:T(8,128)(2,1)S(1)}, bf16[48,4224]{1,0:T(8,128)(2,1)S(1)}, u32[]{:S(2)}, u32[]{:S(2)}) collective-permute-start(bf16[48,4224]{1,0:T(8,128)(2,1)S(1)} %collective-permute-done.17), channel_id=1, source_target_pairs={{192,256},{256,320},{320,384},{384,448},{193,257},{257,321},{321,3... | collective-permute-start | bytes 1216520 | tf_op jit(solution)/shard_map/ppermute | solution.py:130
  137.0 11.0 %collective-permute-start.24 = (bf16[48,4224]{1,0:T(8,128)(2,1)S(1)}, bf16[48,4224]{1,0:T(8,128)(2,1)S(1)}, u32[]{:S(2)}, u32[]{:S(2)}) collective-permute-start(bf16[48,4224]{1,0:T(8,128)(2,1)S(1)} %collective-permute-done.23), channel_id=1, source_target_pairs={{64,0},{128,64},{192,128},{256,192},{65,1},{129,65},{193,129},{257... | collective-permute-start | bytes 1216520 | tf_op jit(solution)/shard_map/ppermute | solution.py:131
  139.0 17.7 %collective-permute-start.10 = (bf16[48,4224]{1,0:T(8,128)(2,1)S(1)}, bf16[48,4224]{1,0:T(8,128)(2,1)S(1)}, u32[]{:S(2)}, u32[]{:S(2)}) collective-permute-start(bf16[48,4224]{1,0:T(8,128)(2,1)S(1)} %collective-permute-done.9), channel_id=1, source_target_pairs={{64,0},{128,64},{192,128},{256,192},{65,1},{129,65},{193,129},{257... | collective-permute-start | bytes 1216520 | tf_op jit(solution)/shard_map/ppermute | solution.py:131
  140.7 20.2 %collective-permute-start.19 = (bf16[48,4224]{1,0:T(8,128)(2,1)S(1)}, bf16[48,4224]{1,0:T(8,128)(2,1)S(1)}, u32[]{:S(2)}, u32[]{:S(2)}) collective-permute-start(bf16[48,4224]{1,0:T(8,128)(2,1)S(1)} %collective-permute-done.18), channel_id=1, source_target_pairs={{256,320},{320,384},{384,448},{257,321},{321,385},{385,449},{258,3... | collective-permute-start | bytes 1216520 | tf_op jit(solution)/shard_map/ppermute | solution.py:130
  157.2 12.2 %collective-permute-start.25 = (bf16[48,4224]{1,0:T(8,128)(2,1)S(1)}, bf16[48,4224]{1,0:T(8,128)(2,1)S(1)}, u32[]{:S(2)}, u32[]{:S(2)}) collective-permute-start(bf16[48,4224]{1,0:T(8,128)(2,1)S(1)} %collective-permute-done.24), channel_id=1, source_target_pairs={{64,0},{128,64},{192,128},{65,1},{129,65},{193,129},{66,2},{130,66... | collective-permute-start | bytes 1216520 | tf_op jit(solution)/shard_map/ppermute | solution.py:131
  159.2 18.9 %collective-permute-start.11 = (bf16[48,4224]{1,0:T(8,128)(2,1)S(1)}, bf16[48,4224]{1,0:T(8,128)(2,1)S(1)}, u32[]{:S(2)}, u32[]{:S(2)}) collective-permute-start(bf16[48,4224]{1,0:T(8,128)(2,1)S(1)} %collective-permute-done.10), channel_id=1, source_target_pairs={{64,0},{128,64},{192,128},{65,1},{129,65},{193,129},{66,2},{130,66... | collective-permute-start | bytes 1216520 | tf_op jit(solution)/shard_map/ppermute | solution.py:131
  160.8 21.4 %collective-permute-start.20 = (bf16[48,4224]{1,0:T(8,128)(2,1)S(1)}, bf16[48,4224]{1,0:T(8,128)(2,1)S(1)}, u32[]{:S(2)}, u32[]{:S(2)}) collective-permute-start(bf16[48,4224]{1,0:T(8,128)(2,1)S(1)} %collective-permute-done.19), channel_id=1, source_target_pairs={{320,384},{384,448},{321,385},{385,449},{322,386},{386,450},{323,3... | collective-permute-start | bytes 1216520 | tf_op jit(solution)/shard_map/ppermute | solution.py:130
  178.5 12.5 %collective-permute-start.26 = (bf16[48,4224]{1,0:T(8,128)(2,1)S(1)}, bf16[48,4224]{1,0:T(8,128)(2,1)S(1)}, u32[]{:S(2)}, u32[]{:S(2)}) collective-permute-start(bf16[48,4224]{1,0:T(8,128)(2,1)S(1)} %collective-permute-done.25), channel_id=1, source_target_pairs={{64,0},{128,64},{65,1},{129,65},{66,2},{130,66},{67,3},{131,67},{6... | collective-permute-start | bytes 1216520 | tf_op jit(solution)/shard_map/ppermute | solution.py:131
  180.5 19.2 %collective-permute-start.12 = (bf16[48,4224]{1,0:T(8,128)(2,1)S(1)}, bf16[48,4224]{1,0:T(8,128)(2,1)S(1)}, u32[]{:S(2)}, u32[]{:S(2)}) collective-permute-start(bf16[48,4224]{1,0:T(8,128)(2,1)S(1)} %collective-permute-done.11), channel_id=1, source_target_pairs={{64,0},{128,64},{65,1},{129,65},{66,2},{130,66},{67,3},{131,67},{6... | collective-permute-start | bytes 1216520 | tf_op jit(solution)/shard_map/ppermute | solution.py:131
  182.2 21.7 %collective-permute-start.21 = (bf16[48,4224]{1,0:T(8,128)(2,1)S(1)}, bf16[48,4224]{1,0:T(8,128)(2,1)S(1)}, u32[]{:S(2)}, u32[]{:S(2)}) collective-permute-start(bf16[48,4224]{1,0:T(8,128)(2,1)S(1)} %collective-permute-done.20), channel_id=1, source_target_pairs={{384,448},{385,449},{386,450},{387,451},{388,452},{389,453},{390,4... | collective-permute-start | bytes 1216520 | tf_op jit(solution)/shard_map/ppermute | solution.py:130
  202.2 15.7 %collective-permute-start.13 = (bf16[48,4224]{1,0:T(8,128)(2,1)S(1)}, bf16[48,4224]{1,0:T(8,128)(2,1)S(1)}, u32[]{:S(2)}, u32[]{:S(2)}) collective-permute-start(bf16[48,4224]{1,0:T(8,128)(2,1)S(1)} %collective-permute-done.12), channel_id=1, source_target_pairs={{64,0},{65,1},{66,2},{67,3},{68,4},{69,5},{70,6},{71,7},{72,8},{73... | collective-permute-start | bytes 1216520 | tf_op jit(solution)/shard_map/ppermute | solution.py:131
  236.5 9.1 %collective-permute-start.34 = (bf16[768,128]{1,0:T(8,128)(2,1)S(1)}, bf16[768,128]{1,0:T(8,128)(2,1)S(1)}, u32[]{:S(2)}, u32[]{:S(2)}) collective-permute-start(bf16[768,128]{1,0:T(8,128)(2,1)S(1)} %collective-permute-done.32), channel_id=1, source_target_pairs={{192,256},{256,320},{320,384},{384,448},{193,257},{257,321},{321,3... | collective-permute-start | bytes 589832 | tf_op jit(solution)/shard_map/ppermute | solution.py:153
  274.4 24.1 %all-to-all-start.2 = ((bf16[16,16,8,512]{3,2,1,0:T(8,128)(2,1)}), bf16[16,16,8,512]{3,2,1,0:T(8,128)(2,1)S(1)}, u32[]{:S(2)}, u32[]{:S(2)}) async-start(bf16[16,16,8,512]{3,2,1,0:T(8,128)(2,1)} %bitcast.268), calls=%async_computation.2 | async-start | bytes 4194304 | tf_op jit(solution)/shard_map/all_to_all | solution.py:170
  (27 other events, 294.8 us)

commit v3 on v2

--- a/solution.py
+++ b/solution.py
@@ -81,20 +81,23 @@
     line = jnp.arange(boxes, dtype=jnp.int32)
     lower = (line[:, None] < line[None, :]).astype(BF)
 
-    def dispatch(step):
+    send = []
+    for step in range(steps):
         local = held[step]
-        local_meta = local[:, model:]
-        place = places(local_meta, me, columns, quad, tok, top)[1]
-        buffer = lax.dot_general(
-            place.astype(BF), local, (((0,), (0,)), ((), ())), preferred_element_type=F32
-        ).astype(BF)
-        arrived = lax.all_to_all(
-            buffer.reshape(columns, quad * MOST, wide),
-            ("x", "y"),
-            split_axis=0,
-            concat_axis=0,
-            tiled=True,
-        ).reshape(boxes, wide)
+        place = places(local[:, model:], me, columns, quad, tok, top)[1]
+        send.append(
+            lax.dot_general(
+                place.astype(BF), local, (((0,), (0,)), ((), ())), preferred_element_type=F32
+            )
+            .astype(BF)
+            .reshape(columns, quad * MOST, wide)
+        )
+    received = lax.all_to_all(
+        jnp.concatenate(send, axis=1), ("x", "y"), split_axis=0, concat_axis=0, tiled=True
+    )
+
+    def compacted(step):
+        arrived = received[:, step * quad * MOST : (step + 1) * quad * MOST].reshape(boxes, wide)
         valid = arrived[:, model + ONE]
         rank = jnp.dot(valid[None, :], lower, preferred_element_type=F32)
         which = (jnp.arange(n_dp, dtype=jnp.int32)[:, None] == my_dp) & (
@@ -109,7 +112,7 @@
         position = jnp.sum(
             jnp.where(chosen, line.astype(F32)[None, :] + 1.0, 0.0), axis=1, keepdims=True
         )
-        side = jnp.pad(local_meta, ((0, ROWS - group), (0, 0)))
+        side = jnp.pad(held[step][:, model:], ((0, ROWS - group), (0, 0)))
         side = jnp.where(lanes == POS, position.astype(BF), side)
         return jnp.concatenate([compact, side], axis=1)
 
@@ -120,44 +123,52 @@
         hidden = (jax.nn.silu(gate) * up).astype(BF)
         return jnp.concatenate([hidden, block[:, model:]], axis=1)
 
-    own = [dispatch(step) for step in range(steps)]
-    by_offset = [[project(block)] + [None] * (n_dp - 1) for block in own]
-    to_right, to_left = list(own), list(own)
-    from_left = [[None] * n_dp for _ in range(steps)]
-    from_right = [[None] * n_dp for _ in range(steps)]
-    for j in range(n_dp - 1):
-        for s in range(steps):
-            to_right[s] = lax.ppermute(to_right[s], "dp", right[j])
-            to_left[s] = lax.ppermute(to_left[s], "dp", left[j])
-            both = project(jnp.concatenate([to_right[s], to_left[s]], axis=0))
-            from_left[s][j + 1], from_right[s][j + 1] = both[:ROWS], both[ROWS:]
-    for s in range(steps):
-        for m in range(1, n_dp):
-            by_offset[s][m] = from_right[s][m] + from_left[s][n_dp - m]
-    ordered = jnp.stack([jnp.stack(blocks) for blocks in by_offset], axis=1)
-    ordered = lax.dynamic_slice_in_dim(
-        jnp.concatenate([ordered, ordered], axis=0), n_dp - my_dp, n_dp, axis=0
-    )
-    batch = n_dp * steps
-    hidden = ordered[..., :LANES].reshape(batch * ROWS, LANES)
-    sides = ordered[..., LANES:].reshape(batch, ROWS, LANES)
+    def ring(chunks):
+        to_right, to_left = list(chunks), list(chunks)
+        from_left = [[None] * n_dp for _ in chunks]
+        from_right = [[None] * n_dp for _ in chunks]
+        for j in range(n_dp - 1):
+            for s in range(len(chunks)):
+                to_right[s] = lax.ppermute(to_right[s], "dp", right[j])
+                to_left[s] = lax.ppermute(to_left[s], "dp", left[j])
+                from_left[s][j + 1], from_right[s][n_dp - 1 - j] = to_right[s], to_left[s]
+        return [
+            [own] + [a + b for a, b in zip(from_left[s][1:], from_right[s][1:])]
+            for s, own in enumerate(chunks)
+        ]
+
+    early = [m for m in range(n_dp) if m not in (1, n_dp - 1)]
+    late = [1, n_dp - 1]
+    ordered = []
+    for slots in ring([compacted(step) for step in range(steps)]):
+        blocks = [None] * n_dp
+        for some in (early, late):
+            done = project(jnp.concatenate([slots[m] for m in some], axis=0))
+            for i, m in enumerate(some):
+                blocks[-m % n_dp] = done[i * ROWS : (i + 1) * ROWS]
+        twice = jnp.stack(blocks + blocks)
+        ordered.append(lax.dynamic_slice_in_dim(twice, n_dp - my_dp, n_dp, axis=0))
+    batch = steps * n_dp
+    hidden = [one[..., :LANES].reshape(n_dp * ROWS, LANES) for one in ordered]
+    sides = jnp.concatenate([one[..., LANES:] for one in ordered], axis=0)
 
     down = down_w[0].reshape(n_dp, LANES, width)
-
-    def shard(index):
-        return lax.dynamic_index_in_dim(down, lax.rem(index + n_dp, n_dp), 0, keepdims=False)
-
-    total = jnp.dot(hidden, shard(my_dp), preferred_element_type=F32)
-    going_right, going_left = hidden, hidden
-    for j in range(n_dp - 1):
-        going_right = lax.ppermute(going_right, "dp", right[j])
-        going_left = lax.ppermute(going_left, "dp", left[j])
-        total = total + jnp.dot(
-            jnp.concatenate([going_right, going_left], axis=1),
-            jnp.concatenate([shard(my_dp - j - 1), shard(my_dp + j + 1)], axis=0),
-            preferred_element_type=F32,
-        )
-    output = total.astype(BF)
+    down = [
+        lax.dynamic_index_in_dim(down, lax.rem(my_dp - m + n_dp, n_dp), 0, keepdims=False)
+        for m in range(n_dp)
+    ]
+    output = []
+    for slots in ring(hidden):
+        sums = [
+            jnp.dot(
+                jnp.concatenate([slots[m] for m in some], axis=1),
+                jnp.concatenate([down[m] for m in some], axis=0),
+                preferred_element_type=F32,
+            )
+            for some in (early, late)
+        ]
+        output.append(sums[0] + sums[1])
+    output = jnp.stack(output).astype(BF)
 
     positions = sides[:, :, POS].astype(jnp.int32) - 1
     unpick = (line[None, :, None] == positions[:, None, :]).astype(BF)
@@ -192,11 +203,11 @@
         preferred_element_type=F32,
     )
     partial = (sums[:, :group] + sums[:, group:]).astype(BF)
-    partial = partial.reshape(n_dp, steps, 2, 2, tok, width).transpose(3, 2, 0, 1, 4, 5)
+    partial = partial.reshape(steps, n_dp, 2, 2, tok, width).transpose(3, 2, 1, 0, 4, 5)
     swapped = lax.all_to_all(partial, "core", split_axis=0, concat_axis=0, tiled=True)
     halves = jnp.sum(swapped.astype(F32), axis=0).astype(BF)
     pieces = lax.all_to_all(
-        halves.reshape(2 * n_dp, mine, width),
+        halves.reshape(2 * n_dp, mine * width // LANES, LANES),
         ("zh", "dp"),
         split_axis=0,
         concat_axis=0,

time: 345 us -> 357 us (1.035)
  waiting for transfers between devices: 165 us -> 126 us
  other arithmetic: 8.42 us -> 32.5 us
  starting transfers between devices: 69.8 us -> 91.8 us
  local copies, waits for them, and re-layouts: 9.75 us -> 26.9 us
  matrix products: 23.9 us -> 13.4 us
    ppermute x42 -> x56, waiting for transfers between devices: 126 us -> 100 us  [the longest x28 100 us: ring(): to_left[s] = lax.ppermute(to_left[s], 'dp', left[j])]
    ppermute x42 -> x56, starting transfers between devices: 54.2 us -> 77.3 us  [the longest x28 41.1 us: ring(): to_right[s] = lax.ppermute(to_right[s], 'dp', right[j])]
    unnamed x29 -> x84, local copies, waits for them, and re-layouts: 1.28 us -> 16.1 us
    all_to_all x1, waiting for transfers between devices: 14.3 us -> 0.01 us  [on_device(): lax.all_to_all(spread.reshape(batch, columns, quad * MOST, width).transpo...]
    unnamed x14 -> x38, other arithmetic: 0.15 us -> 12.5 us
    broadcast_in_dim x1 -> x16, other arithmetic: 0.97 us -> 7.25 us  [on_device(): jnp.where(hits[k], token_meta[:, lane + k:lane + k + 1].astype(F32), weight)]
    all_to_all x2 -> x1, starting transfers between devices: 9.9 us -> 5.68 us  [on_device(): lax.all_to_all(jnp.concatenate(send, axis=1), ('x', 'y'), split_axis=0, c...]
    dot_general x16 -> x4, matrix products: 6.13 us -> 2.31 us  [project(): gate = jnp.dot(x, gate_w[0], preferred_element_type=F32)]
  transfers between devices with their start and end apart: 45 -> 58, of which waited for: 25 -> 24; matrix products, arithmetic and copies ran while one was open for 7% -> 14% of each run, Pallas kernels for 0% -> 0%
where the time goes in v3:
time: 357 us; the launch traced here: 351 us
  waiting for transfers between devices  126 us (35%)
  starting transfers between devices  91.8 us (26%)
  blocking collectives  57.6 us (16%)
  other arithmetic  32.5 us (9%)
  local copies, waits for them, and re-layouts  26.9 us (8%)
  matrix products  13.4 us (4%)
    ppermute x28, waiting for transfers between devices, ring(): to_left[s] = lax.ppermute(to_left[s], 'dp', left[j])  100 us
    ppermute x28, starting transfers between devices, ring(): to_right[s] = lax.ppermute(to_right[s], 'dp', right[j])  41.1 us
    ppermute x28, starting transfers between devices, ring(): to_left[s] = lax.ppermute(to_left[s], 'dp', left[j])  36.1 us
    all_to_all x1, waiting for transfers between devices, on_device(): lax.all_to_all(jnp.concatenate(send, axis=1), ('x', 'y'), split_axis=0, c...  25.8 us
    all_gather x1, blocking collectives, on_device(): lax.all_gather(packed.reshape(steps, tok, wide), ('zh', 'core'), axis=1,...  21.6 us
    all_to_all x1, blocking collectives, on_device(): lax.all_to_all(halves.reshape(2 * n_dp, mine * width // LANES, LANES), ('...  21.5 us
    unnamed x84, local copies, waits for them, and re-layouts  16.1 us
    all_to_all x1, blocking collectives, on_device(): lax.all_to_all(partial, 'core', split_axis=0, concat_axis=0, tiled=True)  14.4 us
  transfers between devices with their start and end apart: 58, of which 24 were waited for; matrix products, arithmetic and copies ran while one was open for 14% of the time, Pallas kernels for 0%

profile of v3, /device:TPU:1, one launch (start us, length us, event | category | flops | bytes accessed | tf_op | source)
XLA Modules:
  0.0 351.3 jit_solution(905715534847553703)
XLA Ops:
  4.9 21.6 %all_gather.3 = bf16[2,24,4224]{2,0,1:T(2,128)(2,1)S(1)} all-gather(bf16[2,6,4224]{2,0,1:T(2,128)(2,1)S(1)} %pad_maximum_fusion.8), channel_id=1, replica_groups=mesh['dp'=8,'x'=4,'y'=4,'zh'=2,'core'=2] {'zh','core'}, dimensions={1}, use_global_device_ids=true | all-gather | bytes 506880 | tf_op jit(solution)/shard_map/all_gather | solution.py:75
  33.3 5.7 %all-to-all-start = ((bf16[16,16,4224]{2,1,0:T(8,128)(2,1)}), bf16[16,16,4224]{2,1,0:T(8,128)(2,1)S(1)}, u32[]{:S(2)}, u32[]{:S(2)}) async-start(bf16[16,16,4224]{2,1,0:T(8,128)(2,1)} %pad_maximum_fusion), calls=%async_computation | async-start | bytes 4325376 | tf_op jit(solution)/shard_map/all_to_all | solution.py:95
  43.0 25.8 %all-to-all-done = bf16[16,16,4224]{2,1,0:T(8,128)(2,1)S(1)} async-done(((bf16[16,16,4224]{2,1,0:T(8,128)(2,1)}), bf16[16,16,4224]{2,1,0:T(8,128)(2,1)S(1)}, u32[]{:S(2)}, u32[]{:S(2)}) %all-to-all-start) | async-done | bytes 2162720 | tf_op jit(solution)/shard_map/all_to_all | solution.py:95
  71.0 9.0 %collective-permute-start = (bf16[48,4224]{1,0:T(8,128)(2,1)S(1)}, bf16[48,4224]{1,0:T(8,128)(2,1)S(1)}, u32[]{:S(2)}, u32[]{:S(2)}) collective-permute-start(bf16[48,4224]{1,0:T(8,128)(2,1)S(1)} %get-tuple-element.41), channel_id=1, source_target_pairs={{0,64},{64,128},{128,192},{192,256},{256,320},{320,384},{384,448},... | collective-permute-start | bytes 1216520 | tf_op jit(solution)/shard_map/ppermute | solution.py:132
  83.7 4.6 %collective-permute-start.14 = (bf16[48,4224]{1,0:T(8,128)(2,1)S(1)}, bf16[48,4224]{1,0:T(8,128)(2,1)S(1)}, u32[]{:S(2)}, u32[]{:S(2)}) collective-permute-start(bf16[48,4224]{1,0:T(8,128)(2,1)S(1)} %get-tuple-element.43), channel_id=1, source_target_pairs={{0,64},{64,128},{128,192},{192,256},{256,320},{320,384},{384,448},... | collective-permute-start | bytes 1216520 | tf_op jit(solution)/shard_map/ppermute | solution.py:132
  93.9 5.2 %collective-permute-done.16 = bf16[48,4224]{1,0:T(8,128)(2,1)S(1)} collective-permute-done((bf16[48,4224]{1,0:T(8,128)(2,1)S(1)}, bf16[48,4224]{1,0:T(8,128)(2,1)S(1)}, u32[]{:S(2)}, u32[]{:S(2)}) %collective-permute-start.16) | collective-permute-done | bytes 405536 | tf_op jit(solution)/shard_map/ppermute | solution.py:133
  101.1 6.7 %collective-permute-done.3 = bf16[48,4224]{1,0:T(8,128)(2,1)S(1)} collective-permute-done((bf16[48,4224]{1,0:T(8,128)(2,1)S(1)}, bf16[48,4224]{1,0:T(8,128)(2,1)S(1)}, u32[]{:S(2)}, u32[]{:S(2)}) %collective-permute-start.3) | collective-permute-done | bytes 405536 | tf_op jit(solution)/shard_map/ppermute | solution.py:133
  110.6 5.9 %collective-permute-done.17 = bf16[48,4224]{1,0:T(8,128)(2,1)S(1)} collective-permute-done((bf16[48,4224]{1,0:T(8,128)(2,1)S(1)}, bf16[48,4224]{1,0:T(8,128)(2,1)S(1)}, u32[]{:S(2)}, u32[]{:S(2)}) %collective-permute-start.17) | collective-permute-done | bytes 405536 | tf_op jit(solution)/shard_map/ppermute | solution.py:133
  119.3 6.0 %collective-permute-done.4 = bf16[48,4224]{1,0:T(8,128)(2,1)} collective-permute-done((bf16[48,4224]{1,0:T(8,128)(2,1)S(1)}, bf16[48,4224]{1,0:T(8,128)(2,1)}, u32[]{:S(2)}, u32[]{:S(2)}) %collective-permute-start.4) | collective-permute-done | bytes 405536 | tf_op jit(solution)/shard_map/ppermute | solution.py:133
  128.1 5.9 %collective-permute-done.18 = bf16[48,4224]{1,0:T(8,128)(2,1)} collective-permute-done((bf16[48,4224]{1,0:T(8,128)(2,1)S(1)}, bf16[48,4224]{1,0:T(8,128)(2,1)}, u32[]{:S(2)}, u32[]{:S(2)}) %collective-permute-start.18) | collective-permute-done | bytes 405536 | tf_op jit(solution)/shard_map/ppermute | solution.py:133
  136.7 5.9 %collective-permute-done.5 = bf16[48,4224]{1,0:T(8,128)(2,1)} collective-permute-done((bf16[48,4224]{1,0:T(8,128)(2,1)}, bf16[48,4224]{1,0:T(8,128)(2,1)}, u32[]{:S(2)}, u32[]{:S(2)}) %collective-permute-start.5) | collective-permute-done | bytes 405536 | tf_op jit(solution)/shard_map/ppermute | solution.py:133
  145.5 5.8 %collective-permute-done.19 = bf16[48,4224]{1,0:T(8,128)(2,1)} collective-permute-done((bf16[48,4224]{1,0:T(8,128)(2,1)}, bf16[48,4224]{1,0:T(8,128)(2,1)}, u32[]{:S(2)}, u32[]{:S(2)}) %collective-permute-start.19) | collective-permute-done | bytes 405536 | tf_op jit(solution)/shard_map/ppermute | solution.py:133
  154.1 5.9 %collective-permute-done.6 = bf16[48,4224]{1,0:T(8,128)(2,1)} collective-permute-done((bf16[48,4224]{1,0:T(8,128)(2,1)}, bf16[48,4224]{1,0:T(8,128)(2,1)}, u32[]{:S(2)}, u32[]{:S(2)}) %collective-permute-start.6) | collective-permute-done | bytes 405536 | tf_op jit(solution)/shard_map/ppermute | solution.py:133
  162.7 6.0 %collective-permute-done.20 = bf16[48,4224]{1,0:T(8,128)(2,1)} collective-permute-done((bf16[48,4224]{1,0:T(8,128)(2,1)}, bf16[48,4224]{1,0:T(8,128)(2,1)}, u32[]{:S(2)}, u32[]{:S(2)}) %collective-permute-start.20) | collective-permute-done | bytes 405536 | tf_op jit(solution)/shard_map/ppermute | solution.py:133
  170.7 6.7 %collective-permute-done.7 = bf16[48,4224]{1,0:T(8,128)(2,1)} collective-permute-done((bf16[48,4224]{1,0:T(8,128)(2,1)}, bf16[48,4224]{1,0:T(8,128)(2,1)}, u32[]{:S(2)}, u32[]{:S(2)}) %collective-permute-start.7) | collective-permute-done | bytes 405536 | tf_op jit(solution)/shard_map/ppermute | solution.py:133
  198.5 11.9 %collective-permute-done.26 = bf16[48,4224]{1,0:T(8,128)(2,1)S(1)} collective-permute-done((bf16[48,4224]{1,0:T(8,128)(2,1)S(1)}, bf16[48,4224]{1,0:T(8,128)(2,1)S(1)}, u32[]{:S(2)}, u32[]{:S(2)}) %collective-permute-start.26) | collective-permute-done | bytes 405536 | tf_op jit(solution)/shard_map/ppermute | solution.py:133
  215.6 4.6 %collective-permute-start.28 = (bf16[384,128]{1,0:T(8,128)(2,1)S(1)}, bf16[384,128]{1,0:T(8,128)(2,1)}, u32[]{:S(2)}, u32[]{:S(2)}) collective-permute-start(bf16[384,128]{1,0:T(8,128)(2,1)S(1)} %bitcast.220), channel_id=1, source_target_pairs={{0,64},{64,128},{128,192},{192,256},{256,320},{320,384},{384,448},... | collective-permute-start | bytes 294920 | tf_op jit(solution)/shard_map/ppermute | solution.py:132
  231.8 6.7 %collective-permute-done.31 = bf16[384,128]{1,0:T(8,128)(2,1)S(1)} collective-permute-done((bf16[384,128]{1,0:T(8,128)(2,1)}, bf16[384,128]{1,0:T(8,128)(2,1)S(1)}, u32[]{:S(2)}, u32[]{:S(2)}) %collective-permute-start.31) | collective-permute-done | bytes 98336 | tf_op jit(solution)/shard_map/ppermute | solution.py:133
  251.8 4.0 %collective-permute-done.48 = bf16[384,128]{1,0:T(8,128)(2,1)S(1)} collective-permute-done((bf16[384,128]{1,0:T(8,128)(2,1)S(1)}, bf16[384,128]{1,0:T(8,128)(2,1)S(1)}, u32[]{:S(2)}, u32[]{:S(2)}) %collective-permute-start.48) | collective-permute-done | bytes 98336 | tf_op jit(solution)/shard_map/ppermute | solution.py:133
  264.9 5.0 %collective-permute-done.35 = bf16[384,128]{1,0:T(8,128)(2,1)S(1)} collective-permute-done((bf16[384,128]{1,0:T(8,128)(2,1)S(1)}, bf16[384,128]{1,0:T(8,128)(2,1)S(1)}, u32[]{:S(2)}, u32[]{:S(2)}) %collective-permute-start.35) | collective-permute-done | bytes 98336 | tf_op jit(solution)/shard_map/ppermute | solution.py:133
  272.6 2.4 collective-permute-done.54
  281.9 8.8 %all-to-all-start.1 = ((bf16[16,16,8,512]{3,2,1,0:T(8,128)(2,1)}), bf16[16,16,8,512]{3,2,1,0:T(8,128)(2,1)S(1)}, u32[]{:S(2)}, u32[]{:S(2)}) async-start(bf16[16,16,8,512]{3,2,1,0:T(8,128)(2,1)} %bitcast.206), calls=%async_computation.1 | async-start | bytes 4194304 | tf_op jit(solution)/shard_map/all_to_all | solution.py:181
  313.9 14.4 %all_to_all.20 = bf16[2,2,8,2,6,512]{5,2,3,4,1,0:T(8,128)(2,1)S(1)} all-to-all(bf16[2,2,8,2,6,512]{5,2,3,4,1,0:T(8,128)(2,1)S(1)} %copy.163), channel_id=1, replica_groups=mesh['dp'=8,'x'=4,'y'=4,'zh'=2,'core'=2] {'core'}, dimensions={0} | all-to-all | bytes 786432 | tf_op jit(solution)/shard_map/all_to_all | solution.py:207
  328.6 21.5 %all_to_all.21 = bf16[16,48,128]{2,1,0:T(8,128)(2,1)S(1)} all-to-all(bf16[16,48,128]{2,1,0:T(8,128)(2,1)S(1)} %reshape.381), channel_id=1, replica_groups=mesh['dp'=8,'x'=4,'y'=4,'zh'=2,'core'=2] {'zh','dp'}, dimensions={0} | all-to-all | bytes 393216 | tf_op jit(solution)/shard_map/all_to_all | solution.py:209
  (339 shorter events, 142.1 us)
Async XLA Ops:
  33.3 35.5 %all-to-all-start = ((bf16[16,16,4224]{2,1,0:T(8,128)(2,1)}), bf16[16,16,4224]{2,1,0:T(8,128)(2,1)S(1)}, u32[]{:S(2)}, u32[]{:S(2)}) async-start(bf16[16,16,4224]{2,1,0:T(8,128)(2,1)} %pad_maximum_fusion), calls=%async_computation | async-start | bytes 4325376 | tf_op jit(solution)/shard_map/all_to_all | solution.py:95
  71.0 20.7 %collective-permute-start = (bf16[48,4224]{1,0:T(8,128)(2,1)S(1)}, bf16[48,4224]{1,0:T(8,128)(2,1)S(1)}, u32[]{:S(2)}, u32[]{:S(2)}) collective-permute-start(bf16[48,4224]{1,0:T(8,128)(2,1)S(1)} %get-tuple-element.41), channel_id=1, source_target_pairs={{0,64},{64,128},{128,192},{192,256},{256,320},{320,384},{384,448},... | collective-permute-start | bytes 1216520 | tf_op jit(solution)/shard_map/ppermute | solution.py:132
  90.4 17.4 %collective-permute-start.3 = (bf16[48,4224]{1,0:T(8,128)(2,1)S(1)}, bf16[48,4224]{1,0:T(8,128)(2,1)S(1)}, u32[]{:S(2)}, u32[]{:S(2)}) collective-permute-start(bf16[48,4224]{1,0:T(8,128)(2,1)S(1)} %collective-permute-done.2), channel_id=1, source_target_pairs={{64,0},{128,64},{192,128},{256,192},{320,256},{384,320},{65,1},{12... | collective-permute-start | bytes 1216520 | tf_op jit(solution)/shard_map/ppermute | solution.py:133
  99.1 17.4 %collective-permute-start.17 = (bf16[48,4224]{1,0:T(8,128)(2,1)S(1)}, bf16[48,4224]{1,0:T(8,128)(2,1)S(1)}, u32[]{:S(2)}, u32[]{:S(2)}) collective-permute-start(bf16[48,4224]{1,0:T(8,128)(2,1)S(1)} %collective-permute-done.16), channel_id=1, source_target_pairs={{64,0},{128,64},{192,128},{256,192},{320,256},{384,320},{65,1},{12... | collective-permute-start | bytes 1216520 | tf_op jit(solution)/shard_map/ppermute | solution.py:133
  100.4 17.4 %collective-permute-start.15 = (bf16[48,4224]{1,0:T(8,128)(2,1)S(1)}, bf16[48,4224]{1,0:T(8,128)(2,1)S(1)}, u32[]{:S(2)}, u32[]{:S(2)}) collective-permute-start(bf16[48,4224]{1,0:T(8,128)(2,1)S(1)} %collective-permute-done.14), channel_id=1, source_target_pairs={{64,128},{128,192},{192,256},{256,320},{320,384},{384,448},{65,129... | collective-permute-start | bytes 1216520 | tf_op jit(solution)/shard_map/ppermute | solution.py:132
  107.8 17.5 %collective-permute-start.4 = (bf16[48,4224]{1,0:T(8,128)(2,1)S(1)}, bf16[48,4224]{1,0:T(8,128)(2,1)}, u32[]{:S(2)}, u32[]{:S(2)}) collective-permute-start(bf16[48,4224]{1,0:T(8,128)(2,1)S(1)} %collective-permute-done.3), channel_id=1, source_target_pairs={{64,0},{128,64},{192,128},{256,192},{320,256},{65,1},{129,65},{193... | collective-permute-start | bytes 1216520 | tf_op jit(solution)/shard_map/ppermute | solution.py:133
  109.1 17.5 %collective-permute-start.8 = (bf16[48,4224]{1,0:T(8,128)(2,1)}, bf16[48,4224]{1,0:T(8,128)(2,1)}, u32[]{:S(2)}, u32[]{:S(2)}) collective-permute-start(bf16[48,4224]{1,0:T(8,128)(2,1)} %collective-permute-done.1), channel_id=1, source_target_pairs={{128,192},{192,256},{256,320},{320,384},{384,448},{129,193},{193,2... | collective-permute-start | bytes 1216520 | tf_op jit(solution)/shard_map/ppermute | solution.py:132
  116.5 17.5 %collective-permute-start.18 = (bf16[48,4224]{1,0:T(8,128)(2,1)S(1)}, bf16[48,4224]{1,0:T(8,128)(2,1)}, u32[]{:S(2)}, u32[]{:S(2)}) collective-permute-start(bf16[48,4224]{1,0:T(8,128)(2,1)S(1)} %collective-permute-done.17), channel_id=1, source_target_pairs={{64,0},{128,64},{192,128},{256,192},{320,256},{65,1},{129,65},{193... | collective-permute-start | bytes 1216520 | tf_op jit(solution)/shard_map/ppermute | solution.py:133
  117.8 17.5 %collective-permute-start.22 = (bf16[48,4224]{1,0:T(8,128)(2,1)S(1)}, bf16[48,4224]{1,0:T(8,128)(2,1)}, u32[]{:S(2)}, u32[]{:S(2)}) collective-permute-start(bf16[48,4224]{1,0:T(8,128)(2,1)S(1)} %collective-permute-done.15), channel_id=1, source_target_pairs={{128,192},{192,256},{256,320},{320,384},{384,448},{129,193},{193,2... | collective-permute-start | bytes 1216520 | tf_op jit(solution)/shard_map/ppermute | solution.py:132
  125.3 17.4 %collective-permute-start.5 = (bf16[48,4224]{1,0:T(8,128)(2,1)}, bf16[48,4224]{1,0:T(8,128)(2,1)}, u32[]{:S(2)}, u32[]{:S(2)}) collective-permute-start(bf16[48,4224]{1,0:T(8,128)(2,1)} %collective-permute-done.4), channel_id=1, source_target_pairs={{64,0},{128,64},{192,128},{256,192},{65,1},{129,65},{193,129},{257... | collective-permute-start | bytes 1216520 | tf_op jit(solution)/shard_map/ppermute | solution.py:133
  126.6 17.5 %collective-permute-start.9 = (bf16[48,4224]{1,0:T(8,128)(2,1)}, bf16[48,4224]{1,0:T(8,128)(2,1)}, u32[]{:S(2)}, u32[]{:S(2)}) collective-permute-start(bf16[48,4224]{1,0:T(8,128)(2,1)} %collective-permute-done.8), channel_id=1, source_target_pairs={{192,256},{256,320},{320,384},{384,448},{193,257},{257,321},{321,3... | collective-permute-start | bytes 1216520 | tf_op jit(solution)/shard_map/ppermute | solution.py:132
  134.0 17.4 %collective-permute-start.19 = (bf16[48,4224]{1,0:T(8,128)(2,1)}, bf16[48,4224]{1,0:T(8,128)(2,1)}, u32[]{:S(2)}, u32[]{:S(2)}) collective-permute-start(bf16[48,4224]{1,0:T(8,128)(2,1)} %collective-permute-done.18), channel_id=1, source_target_pairs={{64,0},{128,64},{192,128},{256,192},{65,1},{129,65},{193,129},{257... | collective-permute-start | bytes 1216520 | tf_op jit(solution)/shard_map/ppermute | solution.py:133
  135.3 17.4 %collective-permute-start.23 = (bf16[48,4224]{1,0:T(8,128)(2,1)}, bf16[48,4224]{1,0:T(8,128)(2,1)}, u32[]{:S(2)}, u32[]{:S(2)}) collective-permute-start(bf16[48,4224]{1,0:T(8,128)(2,1)} %collective-permute-done.22), channel_id=1, source_target_pairs={{192,256},{256,320},{320,384},{384,448},{193,257},{257,321},{321,3... | collective-permute-start | bytes 1216520 | tf_op jit(solution)/shard_map/ppermute | solution.py:132
  142.7 17.4 %collective-permute-start.6 = (bf16[48,4224]{1,0:T(8,128)(2,1)}, bf16[48,4224]{1,0:T(8,128)(2,1)}, u32[]{:S(2)}, u32[]{:S(2)}) collective-permute-start(bf16[48,4224]{1,0:T(8,128)(2,1)} %collective-permute-done.5), channel_id=1, source_target_pairs={{64,0},{128,64},{192,128},{65,1},{129,65},{193,129},{66,2},{130,66... | collective-permute-start | bytes 1216520 | tf_op jit(solution)/shard_map/ppermute | solution.py:133
  144.1 17.9 %collective-permute-start.10 = (bf16[48,4224]{1,0:T(8,128)(2,1)}, bf16[48,4224]{1,0:T(8,128)(2,1)}, u32[]{:S(2)}, u32[]{:S(2)}) collective-permute-start(bf16[48,4224]{1,0:T(8,128)(2,1)} %collective-permute-done.9), channel_id=1, source_target_pairs={{256,320},{320,384},{384,448},{257,321},{321,385},{385,449},{258,3... | collective-permute-start | bytes 1216520 | tf_op jit(solution)/shard_map/ppermute | solution.py:132
  151.4 17.4 %collective-permute-start.20 = (bf16[48,4224]{1,0:T(8,128)(2,1)}, bf16[48,4224]{1,0:T(8,128)(2,1)}, u32[]{:S(2)}, u32[]{:S(2)}) collective-permute-start(bf16[48,4224]{1,0:T(8,128)(2,1)} %collective-permute-done.19), channel_id=1, source_target_pairs={{64,0},{128,64},{192,128},{65,1},{129,65},{193,129},{66,2},{130,66... | collective-permute-start | bytes 1216520 | tf_op jit(solution)/shard_map/ppermute | solution.py:133
  152.7 17.4 %collective-permute-start.24 = (bf16[48,4224]{1,0:T(8,128)(2,1)}, bf16[48,4224]{1,0:T(8,128)(2,1)}, u32[]{:S(2)}, u32[]{:S(2)}) collective-permute-start(bf16[48,4224]{1,0:T(8,128)(2,1)} %collective-permute-done.23), channel_id=1, source_target_pairs={{256,320},{320,384},{384,448},{257,321},{321,385},{385,449},{258,3... | collective-permute-start | bytes 1216520 | tf_op jit(solution)/shard_map/ppermute | solution.py:132
  160.1 17.4 %collective-permute-start.7 = (bf16[48,4224]{1,0:T(8,128)(2,1)}, bf16[48,4224]{1,0:T(8,128)(2,1)}, u32[]{:S(2)}, u32[]{:S(2)}) collective-permute-start(bf16[48,4224]{1,0:T(8,128)(2,1)} %collective-permute-done.6), channel_id=1, source_target_pairs={{64,0},{128,64},{65,1},{129,65},{66,2},{130,66},{67,3},{131,67},{6... | collective-permute-start | bytes 1216520 | tf_op jit(solution)/shard_map/ppermute | solution.py:133
  162.0 28.0 %collective-permute-start.11 = (bf16[48,4224]{1,0:T(8,128)(2,1)}, bf16[48,4224]{1,0:T(8,128)(2,1)S(1)}, u32[]{:S(2)}, u32[]{:S(2)}) collective-permute-start(bf16[48,4224]{1,0:T(8,128)(2,1)} %collective-permute-done.10), channel_id=1, source_target_pairs={{320,384},{384,448},{321,385},{385,449},{322,386},{386,450},{323,3... | collective-permute-start | bytes 1216520 | tf_op jit(solution)/shard_map/ppermute | solution.py:132
  168.7 17.3 %collective-permute-start.21 = (bf16[48,4224]{1,0:T(8,128)(2,1)}, bf16[48,4224]{1,0:T(8,128)(2,1)S(1)}, u32[]{:S(2)}, u32[]{:S(2)}) collective-permute-start(bf16[48,4224]{1,0:T(8,128)(2,1)} %collective-permute-done.20), channel_id=1, source_target_pairs={{64,0},{128,64},{65,1},{129,65},{66,2},{130,66},{67,3},{131,67},{6... | collective-permute-start | bytes 1216520 | tf_op jit(solution)/shard_map/ppermute | solution.py:133
  170.0 21.0 %collective-permute-start.25 = (bf16[48,4224]{1,0:T(8,128)(2,1)}, bf16[48,4224]{1,0:T(8,128)(2,1)S(1)}, u32[]{:S(2)}, u32[]{:S(2)}) collective-permute-start(bf16[48,4224]{1,0:T(8,128)(2,1)} %collective-permute-done.24), channel_id=1, source_target_pairs={{320,384},{384,448},{321,385},{385,449},{322,386},{386,450},{323,3... | collective-permute-start | bytes 1216520 | tf_op jit(solution)/shard_map/ppermute | solution.py:132
  193.4 20.9 %collective-permute-start.13 = (bf16[48,4224]{1,0:T(8,128)(2,1)S(1)}, bf16[48,4224]{1,0:T(8,128)(2,1)S(1)}, u32[]{:S(2)}, u32[]{:S(2)}) collective-permute-start(bf16[48,4224]{1,0:T(8,128)(2,1)S(1)} %collective-permute-done.11), channel_id=1, source_target_pairs={{384,448},{385,449},{386,450},{387,451},{388,452},{389,453},{390,4... | collective-permute-start | bytes 1216520 | tf_op jit(solution)/shard_map/ppermute | solution.py:132
  194.2 20.2 %collective-permute-start.12 = (bf16[48,4224]{1,0:T(8,128)(2,1)}, bf16[48,4224]{1,0:T(8,128)(2,1)S(1)}, u32[]{:S(2)}, u32[]{:S(2)}) collective-permute-start(bf16[48,4224]{1,0:T(8,128)(2,1)} %collective-permute-done.7), channel_id=1, source_target_pairs={{64,0},{65,1},{66,2},{67,3},{68,4},{69,5},{70,6},{71,7},{72,8},{73... | collective-permute-start | bytes 1216520 | tf_op jit(solution)/shard_map/ppermute | solution.py:133
  281.9 31.3 %all-to-all-start.1 = ((bf16[16,16,8,512]{3,2,1,0:T(8,128)(2,1)}), bf16[16,16,8,512]{3,2,1,0:T(8,128)(2,1)S(1)}, u32[]{:S(2)}, u32[]{:S(2)}) async-start(bf16[16,16,8,512]{3,2,1,0:T(8,128)(2,1)} %bitcast.206), calls=%async_computation.1 | async-start | bytes 4194304 | tf_op jit(solution)/shard_map/all_to_all | solution.py:181
  (60 other events, 832.3 us)

commit v4 on v3

--- a/solution.py
+++ b/solution.py
@@ -1,6 +1,10 @@
+import functools
+
 import jax
 import jax.numpy as jnp
 from jax import lax
+from jax.experimental import pallas as pl
+from jax.experimental.pallas import tpu as pltpu
 from jax.sharding import Mesh, PartitionSpec as P
 
 BF = jnp.bfloat16
@@ -8,6 +12,7 @@
 LANES = 128
 ROWS = 48
 MOST = 2
+EARLY = 5
 HOME, HI, MID, ONE, POS = 0, 8, 16, 32, 33
 
 
@@ -42,6 +47,83 @@
     before = ((row // tok == other // tok) & (other < row)).astype(BF)
     earlier = jnp.dot(before, match.astype(BF), preferred_element_type=F32)
     return hits, match & (earlier == (box % MOST).astype(F32))
+
+
+def project_kernel(count, passed, extra, weight_ref, *refs):
+    blocks = refs[:count]
+    outs = refs[count + extra + passed : 2 * count + extra + passed]
+    rows_ref, sems = refs[-2:]
+    width = weight_ref.shape[1] // 2
+    model = weight_ref.shape[0]
+    copies = [
+        pltpu.make_async_copy(
+            blocks[i], rows_ref.at[pl.ds(i * ROWS, ROWS)], sems.at[i]
+        )
+        for i in range(count)
+    ]
+    for copy in copies:
+        copy.start()
+    for copy in copies:
+        copy.wait()
+    both = jnp.dot(rows_ref[:, :model], weight_ref[...], preferred_element_type=F32)
+    gate, up = both[:, :width], both[:, width:]
+    hidden = (gate / (1.0 + jnp.exp(-gate)) * up).astype(BF)
+    for i in range(count):
+        outs[i][:, :width] = hidden[i * ROWS : (i + 1) * ROWS]
+        outs[i][:, width:] = rows_ref[i * ROWS : (i + 1) * ROWS, model:]
+
+
+SMALL = pl.CostEstimate(flops=1000, bytes_accessed=1000, transcendentals=0)
+
+
+def project(weight, blocks, passed, extra=()):
+    vmem = pl.BlockSpec(memory_space=pltpu.VMEM)
+    there = pl.BlockSpec(memory_space=pl.ANY)
+    count = len(blocks)
+    out = pl.pallas_call(
+        functools.partial(project_kernel, count, passed, len(extra)),
+        out_shape=[jax.ShapeDtypeStruct(block.shape, BF) for block in blocks[:passed]]
+        + [jax.ShapeDtypeStruct((ROWS, 2 * LANES), BF)] * count,
+        in_specs=[vmem] + [there] * (count + len(extra)),
+        out_specs=[there] * passed + [vmem] * count,
+        input_output_aliases={1 + i: i for i in range(passed)},
+        scratch_shapes=[
+            pltpu.VMEM((count * ROWS, blocks[0].shape[1]), BF),
+            pltpu.SemaphoreType.DMA((count,)),
+        ],
+        compiler_params=pltpu.CompilerParams(vmem_limit_bytes=24 * 2**20),
+        cost_estimate=SMALL,
+    )(weight, *blocks, *extra)
+    return out[:passed], out[passed:]
+
+
+def assemble_kernel(plan, low, n_dp, dp_ref, *refs):
+    out_ref = refs[-1]
+    z = dp_ref[0]
+    for (s, m), members in plan:
+        value = refs[members[0]][:, low : low + LANES]
+        for other in members[1:]:
+            value = value + refs[other][:, low : low + LANES]
+        spot = s * n_dp + lax.rem(z - m + n_dp, n_dp)
+        out_ref[pl.ds(pl.multiple_of(spot * ROWS, ROWS), ROWS), :] = value
+
+
+def assemble(done, low, my_dp):
+    plan, flat = [], []
+    for s, slots in enumerate(done):
+        for m, parts in enumerate(slots):
+            plan.append(((s, m), tuple(range(len(flat), len(flat) + len(parts)))))
+            flat += parts
+    n_dp = len(done[0])
+    vmem = pl.BlockSpec(memory_space=pltpu.VMEM)
+    return pl.pallas_call(
+        functools.partial(assemble_kernel, plan, low, n_dp),
+        out_shape=jax.ShapeDtypeStruct((len(plan) * ROWS, LANES), BF),
+        in_specs=[pl.BlockSpec(memory_space=pltpu.SMEM)] + [vmem] * len(flat),
+        out_specs=vmem,
+        compiler_params=pltpu.CompilerParams(vmem_limit_bytes=8 * 2**20),
+        cost_estimate=SMALL,
+    )(my_dp.astype(jnp.int32).reshape(1), *flat)
 
 
 def on_device(
@@ -116,59 +198,61 @@
         side = jnp.where(lanes == POS, position.astype(BF), side)
         return jnp.concatenate([compact, side], axis=1)
 
-    def project(block):
-        x = block[:, :model]
-        gate = jnp.dot(x, gate_w[0], preferred_element_type=F32)
-        up = jnp.dot(x, up_w[0], preferred_element_type=F32)
-        hidden = (jax.nn.silu(gate) * up).astype(BF)
-        return jnp.concatenate([hidden, block[:, model:]], axis=1)
-
-    def ring(chunks):
-        to_right, to_left = list(chunks), list(chunks)
-        from_left = [[None] * n_dp for _ in chunks]
-        from_right = [[None] * n_dp for _ in chunks]
-        for j in range(n_dp - 1):
-            for s in range(len(chunks)):
-                to_right[s] = lax.ppermute(to_right[s], "dp", right[j])
-                to_left[s] = lax.ppermute(to_left[s], "dp", left[j])
-                from_left[s][j + 1], from_right[s][n_dp - 1 - j] = to_right[s], to_left[s]
-        return [
-            [own] + [a + b for a, b in zip(from_left[s][1:], from_right[s][1:])]
-            for s, own in enumerate(chunks)
-        ]
-
-    early = [m for m in range(n_dp) if m not in (1, n_dp - 1)]
-    late = [1, n_dp - 1]
-    ordered = []
-    for slots in ring([compacted(step) for step in range(steps)]):
-        blocks = [None] * n_dp
-        for some in (early, late):
-            done = project(jnp.concatenate([slots[m] for m in some], axis=0))
-            for i, m in enumerate(some):
-                blocks[-m % n_dp] = done[i * ROWS : (i + 1) * ROWS]
-        twice = jnp.stack(blocks + blocks)
-        ordered.append(lax.dynamic_slice_in_dim(twice, n_dp - my_dp, n_dp, axis=0))
+    both_w = jnp.concatenate([gate_w[0], up_w[0]], axis=1)
     batch = steps * n_dp
-    hidden = [one[..., :LANES].reshape(n_dp * ROWS, LANES) for one in ordered]
-    sides = jnp.concatenate([one[..., LANES:] for one in ordered], axis=0)
-
-    down = down_w[0].reshape(n_dp, LANES, width)
-    down = [
-        lax.dynamic_index_in_dim(down, lax.rem(my_dp - m + n_dp, n_dp), 0, keepdims=False)
-        for m in range(n_dp)
-    ]
-    output = []
-    for slots in ring(hidden):
-        sums = [
-            jnp.dot(
-                jnp.concatenate([slots[m] for m in some], axis=1),
-                jnp.concatenate([down[m] for m in some], axis=0),
-                preferred_element_type=F32,
-            )
-            for some in (early, late)
-        ]
-        output.append(sums[0] + sums[1])
-    output = jnp.stack(output).astype(BF)
+    own = [compacted(step) for step in range(steps)]
+    to_right, to_left = list(own), list(own)
+    done = [[[] for _ in range(n_dp)] for _ in range(steps)]
+    far = [[None] * n_dp for _ in range(steps)]
+    hidden = None
+    for j in range(1, n_dp):
+        for s in range(steps):
+            to_right[s] = lax.ppermute(to_right[s], "dp", right[j - 1])
+            to_left[s] = lax.ppermute(to_left[s], "dp", left[j - 1])
+            blocks = [to_right[s], to_left[s]] + ([own[s]] if j == 1 else [])
+            passed = 2 if j < n_dp - 1 else 0
+            extra = [hidden] if j == EARLY + 1 and s == 0 else []
+            sent, made = project(both_w, blocks, passed, extra)
+            if passed:
+                to_right[s], to_left[s] = sent
+            if j > EARLY:
+                far[s][j] = made[0][:, :LANES] + made[1][:, :LANES]
+            done[s][j].append(made[0])
+            done[s][n_dp - j].append(made[1])
+            if j == 1:
+                done[s][0].append(made[2])
+        if j == EARLY:
+            hidden = assemble(done, 0, my_dp)
+    gathered = lax.all_gather(hidden, "dp", axis=0, tiled=False).reshape(
+        n_dp, steps, n_dp, ROWS, LANES
+    )
+    beyond = range(EARLY + 1, n_dp)
+    rest = jnp.stack([jnp.stack([far[s][k] for k in beyond]) for s in range(steps)])
+    rest = lax.all_to_all(
+        jnp.broadcast_to(
+            rest.reshape(1, steps * len(beyond) * ROWS, LANES),
+            (n_dp, steps * len(beyond) * ROWS, LANES),
+        ),
+        "dp",
+        split_axis=0,
+        concat_axis=0,
+        tiled=True,
+    ).reshape(n_dp, steps, len(beyond), ROWS, LANES)
+    for z in range(n_dp):
+        for i, k in enumerate(beyond):
+            for d in (z - k, z + k):
+                if 0 <= d < n_dp:
+                    gathered = lax.dynamic_update_slice(
+                        gathered, rest[z : z + 1, :, i : i + 1], (z, 0, d, 0, 0)
+                    )
+    output = jnp.einsum(
+        "zrh,zhf->rf",
+        gathered.reshape(n_dp, batch * ROWS, LANES),
+        down_w[0].reshape(n_dp, LANES, width),
+        preferred_element_type=F32,
+    ).astype(BF)
+
+    sides = assemble(done, LANES, my_dp).reshape(batch, ROWS, LANES)
 
     positions = sides[:, :, POS].astype(jnp.int32) - 1
     unpick = (line[None, :, None] == positions[:, None, :]).astype(BF)

time: 357 us -> 343 us (0.961)
  starting transfers between devices: 91.8 us -> 63.5 us
  other arithmetic: 32.5 us -> 9.06 us
  Pallas kernels: 0 us -> 20.6 us
  waiting for transfers between devices: 126 us -> 143 us
  between operations: 3 us -> 16.2 us
  matrix products: 13.4 us -> 7.91 us
  blocking collectives: 57.6 us -> 53.1 us
    ppermute x56 -> x28, waiting for transfers between devices: 100 us -> 68.7 us  [the longest x14 60.7 us: on_device(): to_left[s] = lax.ppermute(to_left[s], 'dp', left[j - 1])]
    ppermute x56 -> x28, starting transfers between devices: 77.3 us -> 46.2 us  [the longest x14 28.1 us: on_device(): to_right[s] = lax.ppermute(to_right[s], 'dp', right[j - 1])]
    pallas_call x0 -> x16, Pallas kernels: none -> 20.6 us  [the longest x14 19.8 us: project(): pl.pallas_call(functools.partial(project_kernel, count, passed, len(extra...]
    all_to_all x1, waiting for transfers between devices: 0.01 us -> 20.1 us  [on_device(): lax.all_to_all(spread.reshape(batch, columns, quad * MOST, width).transpo...]
    all_to_all x0 -> x1, waiting for transfers between devices: none -> 14.9 us  [on_device(): lax.all_to_all(jnp.broadcast_to(rest.reshape(1, steps * len(beyond) * ROW...]
    all_gather x0 -> x1, waiting for transfers between devices: none -> 13.8 us  [on_device(): lax.all_gather(hidden, 'dp', axis=0, tiled=False)]
    unnamed x38 -> x0, other arithmetic: 12.5 us -> none
    broadcast_in_dim x16 -> x1, other arithmetic: 7.25 us -> 0.97 us  [on_device(): jnp.where(hits[k], token_meta[:, lane + k:lane + k + 1].astype(F32), weight)]
  transfers between devices with their start and end apart: 58 -> 32, of which waited for: 24 -> 18; matrix products, arithmetic and copies ran while one was open for 14% -> 3% of each run, Pallas kernels for 0% -> 6%
where the time goes in v4:
time: 343 us; the launch traced here: 338 us
  waiting for transfers between devices  143 us (42%)
  starting transfers between devices  63.5 us (19%)
  blocking collectives  53.1 us (15%)
  local copies, waits for them, and re-layouts  24.6 us (7%)
  Pallas kernels  20.6 us (6%)
  between operations  16.2 us (5%)
  other arithmetic  9.06 us (3%)
  matrix products  7.91 us (2%)
    ppermute x14, waiting for transfers between devices, on_device(): to_left[s] = lax.ppermute(to_left[s], 'dp', left[j - 1])  60.7 us
    ppermute x14, starting transfers between devices, on_device(): to_right[s] = lax.ppermute(to_right[s], 'dp', right[j - 1])  28.1 us
    all_to_all x1, waiting for transfers between devices, on_device(): lax.all_to_all(jnp.concatenate(send, axis=1), ('x', 'y'), split_axis=0, c...  25.7 us
    all_gather x1, blocking collectives, on_device(): lax.all_gather(packed.reshape(steps, tok, wide), ('zh', 'core'), axis=1,...  21.7 us
    all_to_all x1, blocking collectives, on_device(): lax.all_to_all(halves.reshape(2 * n_dp, mine * width // LANES, LANES), ('...  21.1 us
    all_to_all x1, waiting for transfers between devices, on_device(): lax.all_to_all(spread.reshape(batch, columns, quad * MOST, width).transpo...  20.1 us
    pallas_call x14, Pallas kernels, project(): pl.pallas_call(functools.partial(project_kernel, count, passed, len(extra...  19.8 us
    ppermute x14, starting transfers between devices, on_device(): to_left[s] = lax.ppermute(to_left[s], 'dp', left[j - 1])  18.2 us
  transfers between devices with their start and end apart: 32, of which 18 were waited for; matrix products, arithmetic and copies ran while one was open for 3% of the time, Pallas kernels for 6%

profile of v4, /device:TPU:1, one launch (start us, length us, event | category | flops | bytes accessed | tf_op | source)
XLA Modules:
  0.0 338.2 jit_solution(11685419236047227974)
XLA Ops:
  11.4 21.7 %all_gather.9 = bf16[2,24,4224]{2,0,1:T(2,128)(2,1)S(1)} all-gather(bf16[2,6,4224]{2,0,1:T(2,128)(2,1)S(1)} %pad_maximum_fusion.4), channel_id=1, replica_groups=mesh['dp'=8,'x'=4,'y'=4,'zh'=2,'core'=2] {'zh','core'}, dimensions={1}, use_global_device_ids=true | all-gather | bytes 506880 | tf_op jit(solution)/shard_map/all_gather | solution.py:157
  37.1 5.7 %all-to-all-start = ((bf16[16,16,4224]{2,1,0:T(8,128)(2,1)}), bf16[16,16,4224]{2,1,0:T(8,128)(2,1)S(1)}, u32[]{:S(2)}, u32[]{:S(2)}) async-start(bf16[16,16,4224]{2,1,0:T(8,128)(2,1)} %pad_maximum_fusion), calls=%async_computation | async-start | bytes 4325376 | tf_op jit(solution)/shard_map/all_to_all | solution.py:177
  46.9 25.7 %all-to-all-done = bf16[16,16,4224]{2,1,0:T(8,128)(2,1)S(1)} async-done(((bf16[16,16,4224]{2,1,0:T(8,128)(2,1)}), bf16[16,16,4224]{2,1,0:T(8,128)(2,1)S(1)}, u32[]{:S(2)}, u32[]{:S(2)}) %all-to-all-start) | async-done | bytes 2162720 | tf_op jit(solution)/shard_map/all_to_all | solution.py:177
  74.1 9.1 %collective-permute-start.12 = (bf16[48,4224]{1,0:T(8,128)(2,1)S(1)}, bf16[48,4224]{1,0:T(8,128)(2,1)S(1)}, u32[]{:S(2)}, u32[]{:S(2)}) collective-permute-start(bf16[48,4224]{1,0:T(8,128)(2,1)S(1)} %pad_maximum_fusion.3.refs_2_), channel_id=1, source_target_pairs={{0,64},{64,128},{128,192},{192,256},{256,320},{320,384},{384,448},... | collective-permute-start | bytes 1216520 | tf_op jit(solution)/shard_map/ppermute | solution.py:210
  84.9 4.0 %collective-permute-start = (bf16[48,4224]{1,0:T(8,128)(2,1)S(1)}, bf16[48,4224]{1,0:T(8,128)(2,1)S(1)}, u32[]{:S(2)}, u32[]{:S(2)}) collective-permute-start(bf16[48,4224]{1,0:T(8,128)(2,1)S(1)} %pad_maximum_fusion.2.refs_2_), channel_id=1, source_target_pairs={{0,64},{64,128},{128,192},{192,256},{256,320},{320,384},{384,448},... | collective-permute-start | bytes 1216520 | tf_op jit(solution)/shard_map/ppermute | solution.py:210
  90.5 8.0 %collective-permute-done.refs_0_ = bf16[48,4224]{1,0:T(8,128)(2,1)S(1)} collective-permute-done((bf16[48,4224]{1,0:T(8,128)(2,1)S(1)}, bf16[48,4224]{1,0:T(8,128)(2,1)S(1)}, u32[]{:S(2)}, u32[]{:S(2)}) %collective-permute-start) | collective-permute-done | bytes 405536 | tf_op jit(solution)/shard_map/ppermute | solution.py:210
  98.5 3.9 %collective-permute-done.1.refs_1_ = bf16[48,4224]{1,0:T(8,128)(2,1)S(1)} collective-permute-done((bf16[48,4224]{1,0:T(8,128)(2,1)S(1)}, bf16[48,4224]{1,0:T(8,128)(2,1)S(1)}, u32[]{:S(2)}, u32[]{:S(2)}) %collective-permute-start.1) | collective-permute-done | bytes 405536 | tf_op jit(solution)/shard_map/ppermute | solution.py:211
  110.1 5.0 %collective-permute-done.3.refs_1_ = bf16[48,4224]{1,0:T(8,128)(2,1)S(1)} collective-permute-done((bf16[48,4224]{1,0:T(8,128)(2,1)S(1)}, bf16[48,4224]{1,0:T(8,128)(2,1)S(1)}, u32[]{:S(2)}, u32[]{:S(2)}) %collective-permute-start.3) | collective-permute-done | bytes 405536 | tf_op jit(solution)/shard_map/ppermute | solution.py:211
  119.3 5.9 %collective-permute-done.15.refs_1_ = bf16[48,4224]{1,0:T(8,128)(2,1)S(1)} collective-permute-done((bf16[48,4224]{1,0:T(8,128)(2,1)S(1)}, bf16[48,4224]{1,0:T(8,128)(2,1)S(1)}, u32[]{:S(2)}, u32[]{:S(2)}) %collective-permute-start.15) | collective-permute-done | bytes 405536 | tf_op jit(solution)/shard_map/ppermute | solution.py:211
  129.5 4.4 %collective-permute-done.5.refs_1_ = bf16[48,4224]{1,0:T(8,128)(2,1)S(1)} collective-permute-done((bf16[48,4224]{1,0:T(8,128)(2,1)S(1)}, bf16[48,4224]{1,0:T(8,128)(2,1)S(1)}, u32[]{:S(2)}, u32[]{:S(2)}) %collective-permute-start.5) | collective-permute-done | bytes 405536 | tf_op jit(solution)/shard_map/ppermute | solution.py:211
  138.2 4.4 %collective-permute-done.17.refs_1_ = bf16[48,4224]{1,0:T(8,128)(2,1)S(1)} collective-permute-done((bf16[48,4224]{1,0:T(8,128)(2,1)S(1)}, bf16[48,4224]{1,0:T(8,128)(2,1)S(1)}, u32[]{:S(2)}, u32[]{:S(2)}) %collective-permute-start.17) | collective-permute-done | bytes 405536 | tf_op jit(solution)/shard_map/ppermute | solution.py:211
  146.9 4.4 %collective-permute-done.7.refs_1_ = bf16[48,4224]{1,0:T(8,128)(2,1)S(1)} collective-permute-done((bf16[48,4224]{1,0:T(8,128)(2,1)S(1)}, bf16[48,4224]{1,0:T(8,128)(2,1)S(1)}, u32[]{:S(2)}, u32[]{:S(2)}) %collective-permute-start.7) | collective-permute-done | bytes 405536 | tf_op jit(solution)/shard_map/ppermute | solution.py:211
  161.6 5.5 %collective-permute-done.9.refs_1_ = bf16[48,4224]{1,0:T(8,128)(2,1)} collective-permute-done((bf16[48,4224]{1,0:T(8,128)(2,1)S(1)}, bf16[48,4224]{1,0:T(8,128)(2,1)}, u32[]{:S(2)}, u32[]{:S(2)}) %collective-permute-start.9) | collective-permute-done | bytes 405536 | tf_op jit(solution)/shard_map/ppermute | solution.py:211
  170.8 5.0 %collective-permute-done.21.refs_1_ = bf16[48,4224]{1,0:T(8,128)(2,1)} collective-permute-done((bf16[48,4224]{1,0:T(8,128)(2,1)S(1)}, bf16[48,4224]{1,0:T(8,128)(2,1)}, u32[]{:S(2)}, u32[]{:S(2)}) %collective-permute-start.21) | collective-permute-done | bytes 405536 | tf_op jit(solution)/shard_map/ppermute | solution.py:211
  188.4 4.1 %collective-permute-done.25.refs_1_ = bf16[48,4224]{1,0:T(8,128)(2,1)} collective-permute-done((bf16[48,4224]{1,0:T(8,128)(2,1)}, bf16[48,4224]{1,0:T(8,128)(2,1)}, u32[]{:S(2)}, u32[]{:S(2)}) %collective-permute-start.25) | collective-permute-done | bytes 405536 | tf_op jit(solution)/shard_map/ppermute | solution.py:211
  196.3 5.2 %collective-permute-done.23.refs_1_ = bf16[48,4224]{1,0:T(8,128)(2,1)S(1)} collective-permute-done((bf16[48,4224]{1,0:T(8,128)(2,1)}, bf16[48,4224]{1,0:T(8,128)(2,1)S(1)}, u32[]{:S(2)}, u32[]{:S(2)}) %collective-permute-start.23) | collective-permute-done | bytes 405536 | tf_op jit(solution)/shard_map/ppermute | solution.py:211
  202.6 8.4 %collective-permute-done.27.refs_1_ = bf16[48,4224]{1,0:T(8,128)(2,1)S(1)} collective-permute-done((bf16[48,4224]{1,0:T(8,128)(2,1)}, bf16[48,4224]{1,0:T(8,128)(2,1)S(1)}, u32[]{:S(2)}, u32[]{:S(2)}) %collective-permute-start.27) | collective-permute-done | bytes 405536 | tf_op jit(solution)/shard_map/ppermute | solution.py:211
  213.4 4.5 %all-to-all-start.1 = ((bf16[8,192,128]{2,1,0:T(8,128)(2,1)}), bf16[8,192,128]{2,1,0:T(8,128)(2,1)S(1)}, u32[]{:S(2)}, u32[]{:S(2)}) async-start(bf16[8,192,128]{2,1,0:T(8,128)(2,1)} %broadcast_in_dim.331), calls=%async_computation.1 | async-start | bytes 786432 | tf_op jit(solution)/shard_map/all_to_all | solution.py:231
  228.9 14.9 %all-to-all-done.1 = bf16[8,192,128]{2,1,0:T(8,128)(2,1)S(1)} async-done(((bf16[8,192,128]{2,1,0:T(8,128)(2,1)}), bf16[8,192,128]{2,1,0:T(8,128)(2,1)S(1)}, u32[]{:S(2)}, u32[]{:S(2)}) %all-to-all-start.1) | async-done | bytes 393248 | tf_op jit(solution)/shard_map/all_to_all | solution.py:231
  243.7 13.8 %all-gather.3.cloned.1.call-done = bf16[6144,128]{1,0:T(8,128)(2,1)} async-done(((bf16[768,128]{1,0:T(8,128)(2,1)}), bf16[6144,128]{1,0:T(8,128)(2,1)}) %all-gather.3.cloned.1.call-update) | async-done | bytes 1572880 | tf_op jit(solution)/shard_map/all_gather | solution.py:226
  266.5 7.1 %all-to-all-start.2 = ((bf16[16,16,8,512]{3,2,1,0:T(8,128)(2,1)}), bf16[16,16,8,512]{3,2,1,0:T(8,128)(2,1)S(1)}, u32[]{:S(2)}, u32[]{:S(2)}) async-start(bf16[16,16,8,512]{3,2,1,0:T(8,128)(2,1)} %bitcast.95), calls=%async_computation.2 | async-start | bytes 4194304 | tf_op jit(solution)/shard_map/all_to_all | solution.py:265
  277.7 20.1 %all-to-all-done.2 = bf16[16,16,8,512]{3,2,1,0:T(8,128)(2,1)S(1)} async-done(((bf16[16,16,8,512]{3,2,1,0:T(8,128)(2,1)}), bf16[16,16,8,512]{3,2,1,0:T(8,128)(2,1)S(1)}, u32[]{:S(2)}, u32[]{:S(2)}) %all-to-all-start.2) | async-done | bytes 2097184 | tf_op jit(solution)/shard_map/all_to_all | solution.py:265
  298.5 10.3 %all_to_all.25 = bf16[2,2,8,2,6,512]{5,2,3,4,1,0:T(8,128)(2,1)S(1)} all-to-all(bf16[2,2,8,2,6,512]{5,2,3,4,1,0:T(8,128)(2,1)S(1)} %copy.93), channel_id=1, replica_groups=mesh['dp'=8,'x'=4,'y'=4,'zh'=2,'core'=2] {'core'}, dimensions={0} | all-to-all | bytes 786432 | tf_op jit(solution)/shard_map/all_to_all | solution.py:291
  309.2 21.1 %all_to_all.26 = bf16[16,48,128]{2,1,0:T(8,128)(2,1)S(1)} all-to-all(bf16[16,48,128]{2,1,0:T(8,128)(2,1)S(1)} %reshape.397), channel_id=1, replica_groups=mesh['dp'=8,'x'=4,'y'=4,'zh'=2,'core'=2] {'zh','dp'}, dimensions={0} | all-to-all | bytes 393216 | tf_op jit(solution)/shard_map/all_to_all | solution.py:293
  (288 shorter events, 99.8 us)
Async XLA Ops:
  37.1 35.5 %all-to-all-start = ((bf16[16,16,4224]{2,1,0:T(8,128)(2,1)}), bf16[16,16,4224]{2,1,0:T(8,128)(2,1)S(1)}, u32[]{:S(2)}, u32[]{:S(2)}) async-start(bf16[16,16,4224]{2,1,0:T(8,128)(2,1)} %pad_maximum_fusion), calls=%async_computation | async-start | bytes 4325376 | tf_op jit(solution)/shard_map/all_to_all | solution.py:177
  42.8 214.8 %all-gather.3.cloned.1.call-start = ((), (), s32[]{:S(2)}) async-start(), calls=%async_computation.5 | async-start | bytes 1769472 | tf_op jit(solution)/shard_map/all_gather | solution.py:226
  74.1 32.1 %collective-permute-start.12 = (bf16[48,4224]{1,0:T(8,128)(2,1)S(1)}, bf16[48,4224]{1,0:T(8,128)(2,1)S(1)}, u32[]{:S(2)}, u32[]{:S(2)}) collective-permute-start(bf16[48,4224]{1,0:T(8,128)(2,1)S(1)} %pad_maximum_fusion.3.refs_2_), channel_id=1, source_target_pairs={{0,64},{64,128},{128,192},{192,256},{256,320},{320,384},{384,448},... | collective-permute-start | bytes 1216520 | tf_op jit(solution)/shard_map/ppermute | solution.py:210
  83.2 23.0 %collective-permute-start.13 = (bf16[48,4224]{1,0:T(8,128)(2,1)S(1)}, bf16[48,4224]{1,0:T(8,128)(2,1)S(1)}, u32[]{:S(2)}, u32[]{:S(2)}) collective-permute-start(bf16[48,4224]{1,0:T(8,128)(2,1)S(1)} %pad_maximum_fusion.3.refs_2_), channel_id=1, source_target_pairs={{64,0},{128,64},{192,128},{256,192},{320,256},{384,320},{448,384},... | collective-permute-start | bytes 1216520 | tf_op jit(solution)/shard_map/ppermute | solution.py:211
  84.9 13.6 %collective-permute-start = (bf16[48,4224]{1,0:T(8,128)(2,1)S(1)}, bf16[48,4224]{1,0:T(8,128)(2,1)S(1)}, u32[]{:S(2)}, u32[]{:S(2)}) collective-permute-start(bf16[48,4224]{1,0:T(8,128)(2,1)S(1)} %pad_maximum_fusion.2.refs_2_), channel_id=1, source_target_pairs={{0,64},{64,128},{128,192},{192,256},{256,320},{320,384},{384,448},... | collective-permute-start | bytes 1216520 | tf_op jit(solution)/shard_map/ppermute | solution.py:210
  88.9 13.4 %collective-permute-start.1 = (bf16[48,4224]{1,0:T(8,128)(2,1)S(1)}, bf16[48,4224]{1,0:T(8,128)(2,1)S(1)}, u32[]{:S(2)}, u32[]{:S(2)}) collective-permute-start(bf16[48,4224]{1,0:T(8,128)(2,1)S(1)} %pad_maximum_fusion.2.refs_2_), channel_id=1, source_target_pairs={{64,0},{128,64},{192,128},{256,192},{320,256},{384,320},{448,384},... | collective-permute-start | bytes 1216520 | tf_op jit(solution)/shard_map/ppermute | solution.py:211
  107.4 11.9 %collective-permute-start.14 = (bf16[48,4224]{1,0:T(8,128)(2,1)S(1)}, bf16[48,4224]{1,0:T(8,128)(2,1)}, u32[]{:S(2)}, u32[]{:S(2)}) collective-permute-start(bf16[48,4224]{1,0:T(8,128)(2,1)S(1)} %get-tuple-element.82), channel_id=1, source_target_pairs={{64,128},{128,192},{192,256},{256,320},{320,384},{384,448},{65,129... | collective-permute-start | bytes 1216520 | tf_op jit(solution)/shard_map/ppermute | solution.py:210
  108.8 16.4 %collective-permute-start.15 = (bf16[48,4224]{1,0:T(8,128)(2,1)S(1)}, bf16[48,4224]{1,0:T(8,128)(2,1)S(1)}, u32[]{:S(2)}, u32[]{:S(2)}) collective-permute-start(bf16[48,4224]{1,0:T(8,128)(2,1)S(1)} %get-tuple-element.83), channel_id=1, source_target_pairs={{64,0},{128,64},{192,128},{256,192},{320,256},{384,320},{65,1},{12... | collective-permute-start | bytes 1216520 | tf_op jit(solution)/shard_map/ppermute | solution.py:211
  116.6 12.9 %collective-permute-start.4 = (bf16[48,4224]{1,0:T(8,128)(2,1)}, bf16[48,4224]{1,0:T(8,128)(2,1)}, u32[]{:S(2)}, u32[]{:S(2)}) collective-permute-start(bf16[48,4224]{1,0:T(8,128)(2,1)} %get-tuple-element.63), channel_id=1, source_target_pairs={{128,192},{192,256},{256,320},{320,384},{384,448},{129,193},{193,2... | collective-permute-start | bytes 1216520 | tf_op jit(solution)/shard_map/ppermute | solution.py:210
  118.0 15.9 %collective-permute-start.5 = (bf16[48,4224]{1,0:T(8,128)(2,1)S(1)}, bf16[48,4224]{1,0:T(8,128)(2,1)S(1)}, u32[]{:S(2)}, u32[]{:S(2)}) collective-permute-start(bf16[48,4224]{1,0:T(8,128)(2,1)S(1)} %get-tuple-element.64), channel_id=1, source_target_pairs={{64,0},{128,64},{192,128},{256,192},{320,256},{65,1},{129,65},{193... | collective-permute-start | bytes 1216520 | tf_op jit(solution)/shard_map/ppermute | solution.py:211
  128.2 14.4 %collective-permute-start.17 = (bf16[48,4224]{1,0:T(8,128)(2,1)S(1)}, bf16[48,4224]{1,0:T(8,128)(2,1)S(1)}, u32[]{:S(2)}, u32[]{:S(2)}) collective-permute-start(bf16[48,4224]{1,0:T(8,128)(2,1)S(1)} %get-tuple-element.86), channel_id=1, source_target_pairs={{64,0},{128,64},{192,128},{256,192},{320,256},{65,1},{129,65},{193... | collective-permute-start | bytes 1216520 | tf_op jit(solution)/shard_map/ppermute | solution.py:211
  135.5 11.4 %collective-permute-start.6 = (bf16[48,4224]{1,0:T(8,128)(2,1)}, bf16[48,4224]{1,0:T(8,128)(2,1)}, u32[]{:S(2)}, u32[]{:S(2)}) collective-permute-start(bf16[48,4224]{1,0:T(8,128)(2,1)} %get-tuple-element.65), channel_id=1, source_target_pairs={{192,256},{256,320},{320,384},{384,448},{193,257},{257,321},{321,3... | collective-permute-start | bytes 1216520 | tf_op jit(solution)/shard_map/ppermute | solution.py:210
  136.9 14.4 %collective-permute-start.7 = (bf16[48,4224]{1,0:T(8,128)(2,1)S(1)}, bf16[48,4224]{1,0:T(8,128)(2,1)S(1)}, u32[]{:S(2)}, u32[]{:S(2)}) collective-permute-start(bf16[48,4224]{1,0:T(8,128)(2,1)S(1)} %get-tuple-element.66), channel_id=1, source_target_pairs={{64,0},{128,64},{192,128},{256,192},{65,1},{129,65},{193,129},{257... | collective-permute-start | bytes 1216520 | tf_op jit(solution)/shard_map/ppermute | solution.py:211
  145.6 11.7 %collective-permute-start.19 = (bf16[48,4224]{1,0:T(8,128)(2,1)S(1)}, bf16[48,4224]{1,0:T(8,128)(2,1)S(1)}, u32[]{:S(2)}, u32[]{:S(2)}) collective-permute-start(bf16[48,4224]{1,0:T(8,128)(2,1)S(1)} %get-tuple-element.89), channel_id=1, source_target_pairs={{64,0},{128,64},{192,128},{256,192},{65,1},{129,65},{193,129},{257... | collective-permute-start | bytes 1216520 | tf_op jit(solution)/shard_map/ppermute | solution.py:211
  154.3 12.9 %collective-permute-start.9 = (bf16[48,4224]{1,0:T(8,128)(2,1)S(1)}, bf16[48,4224]{1,0:T(8,128)(2,1)}, u32[]{:S(2)}, u32[]{:S(2)}) collective-permute-start(bf16[48,4224]{1,0:T(8,128)(2,1)S(1)} %get-tuple-element.68), channel_id=1, source_target_pairs={{64,0},{128,64},{192,128},{65,1},{129,65},{193,129},{66,2},{130,66... | collective-permute-start | bytes 1216520 | tf_op jit(solution)/shard_map/ppermute | solution.py:211
  158.9 11.9 %collective-permute-start.20 = (bf16[48,4224]{1,0:T(8,128)(2,1)}, bf16[48,4224]{1,0:T(8,128)(2,1)}, u32[]{:S(2)}, u32[]{:S(2)}) collective-permute-start(bf16[48,4224]{1,0:T(8,128)(2,1)} %get-tuple-element.90), channel_id=1, source_target_pairs={{256,320},{320,384},{384,448},{257,321},{321,385},{385,449},{258,3... | collective-permute-start | bytes 1216520 | tf_op jit(solution)/shard_map/ppermute | solution.py:210
  160.3 15.5 %collective-permute-start.21 = (bf16[48,4224]{1,0:T(8,128)(2,1)S(1)}, bf16[48,4224]{1,0:T(8,128)(2,1)}, u32[]{:S(2)}, u32[]{:S(2)}) collective-permute-start(bf16[48,4224]{1,0:T(8,128)(2,1)S(1)} %get-tuple-element.91), channel_id=1, source_target_pairs={{64,0},{128,64},{192,128},{65,1},{129,65},{193,129},{66,2},{130,66... | collective-permute-start | bytes 1216520 | tf_op jit(solution)/shard_map/ppermute | solution.py:211
  168.8 13.0 %collective-permute-start.10 = (bf16[48,4224]{1,0:T(8,128)(2,1)}, bf16[48,4224]{1,0:T(8,128)(2,1)S(1)}, u32[]{:S(2)}, u32[]{:S(2)}) collective-permute-start(bf16[48,4224]{1,0:T(8,128)(2,1)} %get-tuple-element.69), channel_id=1, source_target_pairs={{320,384},{384,448},{321,385},{385,449},{322,386},{386,450},{323,3... | collective-permute-start | bytes 1216520 | tf_op jit(solution)/shard_map/ppermute | solution.py:210
  169.5 15.0 %collective-permute-start.11 = (bf16[48,4224]{1,0:T(8,128)(2,1)}, bf16[48,4224]{1,0:T(8,128)(2,1)}, u32[]{:S(2)}, u32[]{:S(2)}) collective-permute-start(bf16[48,4224]{1,0:T(8,128)(2,1)} %get-tuple-element.70), channel_id=1, source_target_pairs={{64,0},{128,64},{65,1},{129,65},{66,2},{130,66},{67,3},{131,67},{6... | collective-permute-start | bytes 1216520 | tf_op jit(solution)/shard_map/ppermute | solution.py:211
  178.9 13.6 %collective-permute-start.25 = (bf16[48,4224]{1,0:T(8,128)(2,1)}, bf16[48,4224]{1,0:T(8,128)(2,1)}, u32[]{:S(2)}, u32[]{:S(2)}) collective-permute-start(bf16[48,4224]{1,0:T(8,128)(2,1)} %get-tuple-element.106), channel_id=1, source_target_pairs={{64,0},{128,64},{65,1},{129,65},{66,2},{130,66},{67,3},{131,67},{6... | collective-permute-start | bytes 1216520 | tf_op jit(solution)/shard_map/ppermute | solution.py:211
  186.9 14.5 %collective-permute-start.23 = (bf16[48,4224]{1,0:T(8,128)(2,1)}, bf16[48,4224]{1,0:T(8,128)(2,1)S(1)}, u32[]{:S(2)}, u32[]{:S(2)}) collective-permute-start(bf16[48,4224]{1,0:T(8,128)(2,1)} %get-tuple-element.100), channel_id=1, source_target_pairs={{64,0},{65,1},{66,2},{67,3},{68,4},{69,5},{70,6},{71,7},{72,8},{73... | collective-permute-start | bytes 1216520 | tf_op jit(solution)/shard_map/ppermute | solution.py:211
  194.9 16.1 %collective-permute-start.27 = (bf16[48,4224]{1,0:T(8,128)(2,1)}, bf16[48,4224]{1,0:T(8,128)(2,1)S(1)}, u32[]{:S(2)}, u32[]{:S(2)}) collective-permute-start(bf16[48,4224]{1,0:T(8,128)(2,1)} %get-tuple-element.108), channel_id=1, source_target_pairs={{64,0},{65,1},{66,2},{67,3},{68,4},{69,5},{70,6},{71,7},{72,8},{73... | collective-permute-start | bytes 1216520 | tf_op jit(solution)/shard_map/ppermute | solution.py:211
  213.4 30.4 %all-to-all-start.1 = ((bf16[8,192,128]{2,1,0:T(8,128)(2,1)}), bf16[8,192,128]{2,1,0:T(8,128)(2,1)S(1)}, u32[]{:S(2)}, u32[]{:S(2)}) async-start(bf16[8,192,128]{2,1,0:T(8,128)(2,1)} %broadcast_in_dim.331), calls=%async_computation.1 | async-start | bytes 786432 | tf_op jit(solution)/shard_map/all_to_all | solution.py:231
  266.5 31.3 %all-to-all-start.2 = ((bf16[16,16,8,512]{3,2,1,0:T(8,128)(2,1)}), bf16[16,16,8,512]{3,2,1,0:T(8,128)(2,1)S(1)}, u32[]{:S(2)}, u32[]{:S(2)}) async-start(bf16[16,16,8,512]{3,2,1,0:T(8,128)(2,1)} %bitcast.95), calls=%async_computation.2 | async-start | bytes 4194304 | tf_op jit(solution)/shard_map/all_to_all | solution.py:265
  (78 other events, 1699.0 us)
Sparse Core Ops, SparseCore 0:
  182.0 75.5 all-gather.2

commit v5 on v4

--- a/solution.py
+++ b/solution.py
@@ -12,7 +12,8 @@
 LANES = 128
 ROWS = 48
 MOST = 2
-EARLY = 5
+EARLY = 3
+STEPS = 5
 HOME, HI, MID, ONE, POS = 0, 8, 16, 32, 33
 
 
@@ -100,20 +101,29 @@
 def assemble_kernel(plan, low, n_dp, dp_ref, *refs):
     out_ref = refs[-1]
     z = dp_ref[0]
-    for (s, m), members in plan:
-        value = refs[members[0]][:, low : low + LANES]
-        for other in members[1:]:
-            value = value + refs[other][:, low : low + LANES]
+    for s, m, members in plan:
+        value = None
+        for index, least, most in members:
+            part = refs[index][:, low : low + LANES]
+            if least > 0 or most < n_dp - 1:
+                here = ((z >= least) & (z <= most)).astype(F32)
+                part = (part.astype(F32) * here).astype(BF)
+            value = part if value is None else value + part
         spot = s * n_dp + lax.rem(z - m + n_dp, n_dp)
         out_ref[pl.ds(pl.multiple_of(spot * ROWS, ROWS), ROWS), :] = value
 
 
 def assemble(done, low, my_dp):
-    plan, flat = [], []
+    plan, flat, known = [], [], {}
     for s, slots in enumerate(done):
         for m, parts in enumerate(slots):
-            plan.append(((s, m), tuple(range(len(flat), len(flat) + len(parts)))))
-            flat += parts
+            members = []
+            for block, least, most in parts:
+                if id(block) not in known:
+                    known[id(block)] = len(flat)
+                    flat.append(block)
+                members.append((known[id(block)], least, most))
+            plan.append((s, m, members))
     n_dp = len(done[0])
     vmem = pl.BlockSpec(memory_space=pltpu.VMEM)
     return pl.pallas_call(
@@ -163,30 +173,34 @@
     line = jnp.arange(boxes, dtype=jnp.int32)
     lower = (line[:, None] < line[None, :]).astype(BF)
 
-    send = []
-    for step in range(steps):
-        local = held[step]
-        place = places(local[:, model:], me, columns, quad, tok, top)[1]
-        send.append(
-            lax.dot_general(
-                place.astype(BF), local, (((0,), (0,)), ((), ())), preferred_element_type=F32
+    def exchange(sets, after=None):
+        send = []
+        for i, local in enumerate(sets):
+            place = places(local[:, model:], me, columns, quad, tok, top)[1]
+            if after is not None and i == len(sets) - 1:
+                place = place & after
+            send.append(
+                lax.dot_general(
+                    place.astype(BF), local, (((0,), (0,)), ((), ())), preferred_element_type=F32
+                )
+                .astype(BF)
+                .reshape(columns, quad * MOST, wide)
             )
-            .astype(BF)
-            .reshape(columns, quad * MOST, wide)
+        return lax.all_to_all(
+            jnp.concatenate(send, axis=1), ("x", "y"), split_axis=0, concat_axis=0, tiled=True
         )
-    received = lax.all_to_all(
-        jnp.concatenate(send, axis=1), ("x", "y"), split_axis=0, concat_axis=0, tiled=True
-    )
-
-    def compacted(step):
-        arrived = received[:, step * quad * MOST : (step + 1) * quad * MOST].reshape(boxes, wide)
+
+    def compacted(received, index, local, step, dp, after=None):
+        arrived = received[:, index * quad * MOST : (index + 1) * quad * MOST].reshape(boxes, wide)
         valid = arrived[:, model + ONE]
         rank = jnp.dot(valid[None, :], lower, preferred_element_type=F32)
-        which = (jnp.arange(n_dp, dtype=jnp.int32)[:, None] == my_dp) & (
+        which = (jnp.arange(n_dp, dtype=jnp.int32)[:, None] == dp) & (
             labels[None, :] == owners[step]
         )
         limit = jnp.sum(jnp.where(which, slot_rows[step], 0)).astype(F32)
         kept = (valid[None, :] > 0) & (rank < limit)
+        if after is not None:
+            kept = kept & after
         slot_row = jnp.arange(ROWS, dtype=jnp.int32).astype(F32)[:, None]
         chosen = kept & (rank == slot_row)
         pick = chosen.astype(BF)
@@ -194,52 +208,103 @@
         position = jnp.sum(
             jnp.where(chosen, line.astype(F32)[None, :] + 1.0, 0.0), axis=1, keepdims=True
         )
-        side = jnp.pad(held[step][:, model:], ((0, ROWS - group), (0, 0)))
+        side = jnp.pad(local[:, model:], ((0, ROWS - group), (0, 0)))
         side = jnp.where(lanes == POS, position.astype(BF), side)
         return jnp.concatenate([compact, side], axis=1)
 
+    received = exchange([held[step] for step in range(steps)])
+
+    beyond = list(range(STEPS + 1, n_dp))
+    half = lax.dynamic_index_in_dim(
+        held.reshape(steps, 2, 2, tok, wide), lax.axis_index("core"), 2, keepdims=False
+    )
+    half = half.reshape(steps * 2 * tok, wide)
+    distant = jnp.stack(
+        [
+            lax.ppermute(
+                half,
+                "dp",
+                [(i, i + k) for i in range(n_dp - k)] + [(i + k, i) for i in range(n_dp - k)],
+            )
+            for k in beyond
+        ]
+    ).reshape(len(beyond), steps, 2, tok, wide)
+    distant = lax.all_gather(distant, "core", axis=3, tiled=False).reshape(
+        len(beyond), steps, group, wide
+    )
     both_w = jnp.concatenate([gate_w[0], up_w[0]], axis=1)
     batch = steps * n_dp
-    own = [compacted(step) for step in range(steps)]
+    own = [compacted(received, step, held[step], step, my_dp) for step in range(steps)]
+    ready = own[-1][0, 0] == own[-1][0, 0]
+    received_far = exchange(
+        [distant[i, step] for i in range(len(beyond)) for step in range(steps)], ready
+    )
     to_right, to_left = list(own), list(own)
     done = [[[] for _ in range(n_dp)] for _ in range(steps)]
-    far = [[None] * n_dp for _ in range(steps)]
+    middle = [{} for _ in range(steps)]
+    last = n_dp - 1
     hidden = None
-    for j in range(1, n_dp):
+    for j in range(1, STEPS + 1):
         for s in range(steps):
             to_right[s] = lax.ppermute(to_right[s], "dp", right[j - 1])
             to_left[s] = lax.ppermute(to_left[s], "dp", left[j - 1])
             blocks = [to_right[s], to_left[s]] + ([own[s]] if j == 1 else [])
-            passed = 2 if j < n_dp - 1 else 0
+            passed = 2 if j < STEPS else 0
             extra = [hidden] if j == EARLY + 1 and s == 0 else []
+            extra += [made[0]] if (j, s) != (1, 0) else []
             sent, made = project(both_w, blocks, passed, extra)
             if passed:
                 to_right[s], to_left[s] = sent
             if j > EARLY:
-                far[s][j] = made[0][:, :LANES] + made[1][:, :LANES]
-            done[s][j].append(made[0])
-            done[s][n_dp - j].append(made[1])
+                middle[s][j] = made[0][:, :LANES] + made[1][:, :LANES]
+            done[s][j].append((made[0], 0, last))
+            done[s][n_dp - j].append((made[1], 0, last))
             if j == 1:
-                done[s][0].append(made[2])
+                done[s][0].append((made[2], 0, last))
         if j == EARLY:
-            hidden = assemble(done, 0, my_dp)
+            ready = made[0][0, 0] == made[0][0, 0]
+            blocks = [
+                compacted(
+                    received_far,
+                    i * steps + s,
+                    distant[i, s],
+                    s,
+                    jnp.where(my_dp >= k, my_dp - k, my_dp + k),
+                    ready,
+                )
+                for i, k in enumerate(beyond)
+                for s in range(steps)
+            ]
+            late = project(both_w, blocks, 0)[1]
+            for i, k in enumerate(beyond):
+                for s in range(steps):
+                    done[s][k].append((late[i * steps + s], k, last))
+                    done[s][n_dp - k].append((late[i * steps + s], 0, last - k))
+            hidden = assemble(
+                [
+                    [parts if parts else [(done[s][0][0][0], n_dp, n_dp)] for parts in done[s]]
+                    for s in range(steps)
+                ],
+                0,
+                my_dp,
+            )
     gathered = lax.all_gather(hidden, "dp", axis=0, tiled=False).reshape(
         n_dp, steps, n_dp, ROWS, LANES
     )
-    beyond = range(EARLY + 1, n_dp)
-    rest = jnp.stack([jnp.stack([far[s][k] for k in beyond]) for s in range(steps)])
+    span = range(EARLY + 1, STEPS + 1)
+    rest = jnp.stack([jnp.stack([middle[s][k] for k in span]) for s in range(steps)])
     rest = lax.all_to_all(
         jnp.broadcast_to(
-            rest.reshape(1, steps * len(beyond) * ROWS, LANES),
-            (n_dp, steps * len(beyond) * ROWS, LANES),
+            rest.reshape(1, steps * len(span) * ROWS, LANES),
+            (n_dp, steps * len(span) * ROWS, LANES),
         ),
         "dp",
         split_axis=0,
         concat_axis=0,
         tiled=True,
-    ).reshape(n_dp, steps, len(beyond), ROWS, LANES)
+    ).reshape(n_dp, steps, len(span), ROWS, LANES)
     for z in range(n_dp):
-        for i, k in enumerate(beyond):
+        for i, k in enumerate(span):
             for d in (z - k, z + k):
                 if 0 <= d < n_dp:
                     gathered = lax.dynamic_update_slice(

time: 343 us -> 359 us (1.047)
  waiting for transfers between devices: 143 us -> 97.4 us
  local copies, waits for them, and re-layouts: 24.6 us -> 53.9 us
  matrix products: 7.91 us -> 18.5 us
  starting transfers between devices: 63.5 us -> 72.7 us
  blocking collectives: 53.1 us -> 59.5 us
  between operations: 16.2 us -> 21.4 us
  other arithmetic: 9.06 us -> 14 us
  Pallas kernels: 20.6 us -> 16.3 us
    ppermute x14 -> x10, waiting for transfers between devices: 60.7 us -> 22.2 us  [on_device(): to_left[s] = lax.ppermute(to_left[s], 'dp', left[j - 1])]
    all_to_all x2 -> x3, waiting for transfers between devices: 40.6 us -> 18.5 us  [the longest x2 9.31 us: exchange(): lax.all_to_all(jnp.concatenate(send, axis=1), ('x', 'y'), split_axis=0, c...]
    all_gather x1, waiting for transfers between devices: 13.8 us -> 35.4 us  [on_device(): lax.all_gather(hidden, 'dp', axis=0, tiled=False)]
    all_to_all x2 -> x3, starting transfers between devices: 10.1 us -> 24 us  [the longest x1 12.4 us: on_device(): lax.all_to_all(jnp.broadcast_to(rest.reshape(1, steps * len(span) * ROWS,...]
    ppermute x0 -> x2, starting transfers between devices: none -> 13 us  [on_device(): lax.ppermute(half, 'dp', [(i, i + k) for i in range(n_dp - k)] + [(i + k,...]
    ppermute x14 -> x10, starting transfers between devices: 28.1 us -> 16.5 us  [on_device(): to_right[s] = lax.ppermute(to_right[s], 'dp', right[j - 1])]
    dot_general x2 -> x6, matrix products: 1.42 us -> 10.1 us  [exchange(): lax.dot_general(place.astype(BF), local, (((0,), (0,)), ((), ())), prefer...]
    slice x3 -> x10, local copies, waits for them, and re-layouts: 1.26 us -> 9.35 us  [the longest x6 6.6 us: exchange(): place = places(local[:, model:], me, columns, quad, tok, top)[1]]
  transfers between devices with their start and end apart: 32 -> 27, of which waited for: 18 -> 10; matrix products, arithmetic and copies ran while one was open for 3% -> 11% of each run, Pallas kernels for 6% -> 5%
where the time goes in v5:
time: 359 us; the launch traced here: 354 us
  waiting for transfers between devices  97.4 us (27%)
  starting transfers between devices  72.7 us (20%)
  blocking collectives  59.5 us (17%)
  local copies, waits for them, and re-layouts  53.9 us (15%)
  between operations  21.4 us (6%)
  matrix products  18.5 us (5%)
  Pallas kernels  16.3 us (5%)
  other arithmetic  14 us (4%)
    all_gather x1, waiting for transfers between devices, on_device(): lax.all_gather(hidden, 'dp', axis=0, tiled=False)  35.4 us
    all_to_all x1, blocking collectives, on_device(): lax.all_to_all(halves.reshape(2 * n_dp, mine * width // LANES, LANES), ('...  24.6 us
    ppermute x10, waiting for transfers between devices, on_device(): to_left[s] = lax.ppermute(to_left[s], 'dp', left[j - 1])  22.2 us
    all_gather x1, blocking collectives, on_device(): lax.all_gather(packed.reshape(steps, tok, wide), ('zh', 'core'), axis=1,...  21.7 us
    all_to_all x1, waiting for transfers between devices, on_device(): lax.all_to_all(spread.reshape(batch, columns, quad * MOST, width).transpo...  20.2 us
    unnamed x197, local copies, waits for them, and re-layouts  18.6 us
    ppermute x10, starting transfers between devices, on_device(): to_right[s] = lax.ppermute(to_right[s], 'dp', right[j - 1])  16.5 us
    pallas_call x11, Pallas kernels, project(): pl.pallas_call(functools.partial(project_kernel, count, passed, len(extra...  15.5 us
  transfers between devices with their start and end apart: 27, of which 10 were waited for; matrix products, arithmetic and copies ran while one was open for 11% of the time, Pallas kernels for 5%

profile of v5, /device:TPU:1, one launch (start us, length us, event | category | flops | bytes accessed | tf_op | source)
XLA Modules:
  0.0 353.7 jit_solution(3300513035554601021)
XLA Ops:
  11.4 21.7 %all_gather.12 = bf16[2,24,4224]{2,0,1:T(2,128)(2,1)S(1)} all-gather(bf16[2,6,4224]{2,0,1:T(2,128)(2,1)S(1)} %pad_maximum_fusion.10), channel_id=1, replica_groups=mesh['dp'=8,'x'=4,'y'=4,'zh'=2,'core'=2] {'zh','core'}, dimensions={1}, use_global_device_ids=true | all-gather | bytes 506880 | tf_op jit(solution)/shard_map/all_gather | solution.py:167
  34.0 7.5 %collective-permute-start.3 = (bf16[24,4224]{1,0:T(8,128)(2,1)}, bf16[24,4224]{1,0:T(8,128)(2,1)}, u32[]{:S(2)}, u32[]{:S(2)}) collective-permute-start(bf16[24,4224]{1,0:T(8,128)(2,1)} %reshape.492), channel_id=1, source_target_pairs={{0,448},{448,0},{1,449},{449,1},{2,450},{450,2},{3,451},{451,3},{4... | collective-permute-start | bytes 608264 | tf_op jit(solution)/shard_map/ppermute | solution.py:224
  41.5 5.4 %collective-permute-start.2 = (bf16[24,4224]{1,0:T(8,128)(2,1)}, bf16[24,4224]{1,0:T(8,128)(2,1)}, u32[]{:S(2)}, u32[]{:S(2)}) collective-permute-start(bf16[24,4224]{1,0:T(8,128)(2,1)} %reshape.492), channel_id=1, source_target_pairs={{0,384},{64,448},{384,0},{448,64},{1,385},{65,449},{385,1},{449,65... | collective-permute-start | bytes 608264 | tf_op jit(solution)/shard_map/ppermute | solution.py:224
  51.1 6.9 %all-to-all-start = ((bf16[16,16,4224]{2,1,0:T(8,128)(2,1)}), bf16[16,16,4224]{2,1,0:T(8,128)(2,1)S(1)}, u32[]{:S(2)}, u32[]{:S(2)}) async-start(bf16[16,16,4224]{2,1,0:T(8,128)(2,1)} %pad_maximum_fusion.1), calls=%async_computation | async-start | bytes 4325376 | tf_op jit(solution)/shard_map/all_to_all | solution.py:189
  64.7 2.9 all_gather.13
  71.6 2.7 fusion.4
  75.9 2.6 fusion.3
  78.6 9.3 %all-to-all-done = bf16[16,16,4224]{2,1,0:T(8,128)(2,1)S(1)} async-done(((bf16[16,16,4224]{2,1,0:T(8,128)(2,1)}), bf16[16,16,4224]{2,1,0:T(8,128)(2,1)S(1)}, u32[]{:S(2)}, u32[]{:S(2)}) %all-to-all-start) | async-done | bytes 2162720 | tf_op jit(solution)/shard_map/all_to_all | solution.py:189
  94.1 3.3 pad_maximum_fusion
  97.4 4.7 %all-to-all-start.1 = ((bf16[16,32,4224]{2,1,0:T(8,128)(2,1)}), bf16[16,32,4224]{2,1,0:T(8,128)(2,1)}, u32[]{:S(2)}, u32[]{:S(2)}) async-start(bf16[16,32,4224]{2,1,0:T(8,128)(2,1)} %pad_maximum_fusion), calls=%async_computation.1 | async-start | bytes 8650752 | tf_op jit(solution)/shard_map/all_to_all | solution.py:189
  106.6 4.0 %collective-permute-start = (bf16[48,4224]{1,0:T(8,128)(2,1)S(1)}, bf16[48,4224]{1,0:T(8,128)(2,1)S(1)}, u32[]{:S(2)}, u32[]{:S(2)}) collective-permute-start(bf16[48,4224]{1,0:T(8,128)(2,1)S(1)} %pad_maximum_fusion.4.refs_2_), channel_id=1, source_target_pairs={{0,64},{64,128},{128,192},{192,256},{256,320},{320,384},{384,448},... | collective-permute-start | bytes 1216520 | tf_op jit(solution)/shard_map/ppermute | solution.py:249
  112.0 4.0 %collective-permute-start.4 = (bf16[48,4224]{1,0:T(8,128)(2,1)S(1)}, bf16[48,4224]{1,0:T(8,128)(2,1)S(1)}, u32[]{:S(2)}, u32[]{:S(2)}) collective-permute-start(bf16[48,4224]{1,0:T(8,128)(2,1)S(1)} %pad_maximum_fusion.5.refs_2_), channel_id=1, source_target_pairs={{0,64},{64,128},{128,192},{192,256},{256,320},{320,384},{384,448},... | collective-permute-start | bytes 1216520 | tf_op jit(solution)/shard_map/ppermute | solution.py:249
  120.2 4.0 %collective-permute-done.5.refs_1_ = bf16[48,4224]{1,0:T(8,128)(2,1)S(1)} collective-permute-done((bf16[48,4224]{1,0:T(8,128)(2,1)S(1)}, bf16[48,4224]{1,0:T(8,128)(2,1)S(1)}, u32[]{:S(2)}, u32[]{:S(2)}) %collective-permute-start.5) | collective-permute-done | bytes 405536 | tf_op jit(solution)/shard_map/ppermute | solution.py:250
  135.4 6.4 %collective-permute-done.7.refs_1_ = bf16[48,4224]{1,0:T(8,128)(2,1)} collective-permute-done((bf16[48,4224]{1,0:T(8,128)(2,1)S(1)}, bf16[48,4224]{1,0:T(8,128)(2,1)}, u32[]{:S(2)}, u32[]{:S(2)}) %collective-permute-start.7) | collective-permute-done | bytes 405536 | tf_op jit(solution)/shard_map/ppermute | solution.py:250
  168.7 2.6 slice_bitcast_fusion.1
  187.6 6.0 %collective-permute-done.17.refs_1_ = bf16[48,4224]{1,0:T(8,128)(2,1)S(1)} collective-permute-done((bf16[48,4224]{1,0:T(8,128)(2,1)}, bf16[48,4224]{1,0:T(8,128)(2,1)S(1)}, u32[]{:S(2)}, u32[]{:S(2)}) %collective-permute-start.17) | collective-permute-done | bytes 405536 | tf_op jit(solution)/shard_map/ppermute | solution.py:250
  194.6 3.4 collective-permute-done.21.refs_1_
  200.4 12.4 %all-to-all-start.2 = ((bf16[8,192,128]{2,1,0:T(8,128)(2,1)}), bf16[8,192,128]{2,1,0:T(8,128)(2,1)S(1)}, u32[]{:S(2)}, u32[]{:S(2)}) async-start(bf16[8,192,128]{2,1,0:T(8,128)(2,1)} %broadcast_in_dim.435), calls=%async_computation.2 | async-start | bytes 786432 | tf_op jit(solution)/shard_map/all_to_all | solution.py:296
  220.9 9.2 %all-to-all-done.2 = bf16[8,192,128]{2,1,0:T(8,128)(2,1)S(1)} async-done(((bf16[8,192,128]{2,1,0:T(8,128)(2,1)}), bf16[8,192,128]{2,1,0:T(8,128)(2,1)S(1)}, u32[]{:S(2)}, u32[]{:S(2)}) %all-to-all-start.2) | async-done | bytes 393248 | tf_op jit(solution)/shard_map/all_to_all | solution.py:296
  230.0 35.4 %all-gather.3.cloned.1.call-done = bf16[6144,128]{1,0:T(8,128)(2,1)} async-done(((bf16[768,128]{1,0:T(8,128)(2,1)}), bf16[6144,128]{1,0:T(8,128)(2,1)}) %all-gather.3.cloned.1.call-update) | async-done | bytes 1572880 | tf_op jit(solution)/shard_map/all_gather | solution.py:291
  279.2 6.3 %all-to-all-start.3 = ((bf16[16,16,8,512]{3,2,1,0:T(8,128)(2,1)}), bf16[16,16,8,512]{3,2,1,0:T(8,128)(2,1)S(1)}, u32[]{:S(2)}, u32[]{:S(2)}) async-start(bf16[16,16,8,512]{3,2,1,0:T(8,128)(2,1)} %bitcast.169), calls=%async_computation.3 | async-start | bytes 4194304 | tf_op jit(solution)/shard_map/all_to_all | solution.py:330
  289.6 20.2 %all-to-all-done.3 = bf16[16,16,8,512]{3,2,1,0:T(8,128)(2,1)S(1)} async-done(((bf16[16,16,8,512]{3,2,1,0:T(8,128)(2,1)}), bf16[16,16,8,512]{3,2,1,0:T(8,128)(2,1)S(1)}, u32[]{:S(2)}, u32[]{:S(2)}) %all-to-all-start.3) | async-done | bytes 2097184 | tf_op jit(solution)/shard_map/all_to_all | solution.py:330
  310.5 10.3 %all_to_all.30 = bf16[2,2,8,2,6,512]{5,2,3,4,1,0:T(8,128)(2,1)S(1)} all-to-all(bf16[2,2,8,2,6,512]{5,2,3,4,1,0:T(8,128)(2,1)S(1)} %copy.115), channel_id=1, replica_groups=mesh['dp'=8,'x'=4,'y'=4,'zh'=2,'core'=2] {'core'}, dimensions={0} | all-to-all | bytes 786432 | tf_op jit(solution)/shard_map/all_to_all | solution.py:356
  321.2 24.6 %all_to_all.31 = bf16[16,48,128]{2,1,0:T(8,128)(2,1)S(1)} all-to-all(bf16[16,48,128]{2,1,0:T(8,128)(2,1)S(1)} %reshape.514), channel_id=1, replica_groups=mesh['dp'=8,'x'=4,'y'=4,'zh'=2,'core'=2] {'zh','dp'}, dimensions={0} | all-to-all | bytes 393216 | tf_op jit(solution)/shard_map/all_to_all | solution.py:358
  (385 shorter events, 116.6 us)
Async XLA Ops:
  34.0 26.8 %collective-permute-start.3 = (bf16[24,4224]{1,0:T(8,128)(2,1)}, bf16[24,4224]{1,0:T(8,128)(2,1)}, u32[]{:S(2)}, u32[]{:S(2)}) collective-permute-start(bf16[24,4224]{1,0:T(8,128)(2,1)} %reshape.492), channel_id=1, source_target_pairs={{0,448},{448,0},{1,449},{449,1},{2,450},{450,2},{3,451},{451,3},{4... | collective-permute-start | bytes 608264 | tf_op jit(solution)/shard_map/ppermute | solution.py:224
  41.5 20.3 %collective-permute-start.2 = (bf16[24,4224]{1,0:T(8,128)(2,1)}, bf16[24,4224]{1,0:T(8,128)(2,1)}, u32[]{:S(2)}, u32[]{:S(2)}) collective-permute-start(bf16[24,4224]{1,0:T(8,128)(2,1)} %reshape.492), channel_id=1, source_target_pairs={{0,384},{64,448},{384,0},{448,64},{1,385},{65,449},{385,1},{449,65... | collective-permute-start | bytes 608264 | tf_op jit(solution)/shard_map/ppermute | solution.py:224
  51.1 36.7 %all-to-all-start = ((bf16[16,16,4224]{2,1,0:T(8,128)(2,1)}), bf16[16,16,4224]{2,1,0:T(8,128)(2,1)S(1)}, u32[]{:S(2)}, u32[]{:S(2)}) async-start(bf16[16,16,4224]{2,1,0:T(8,128)(2,1)} %pad_maximum_fusion.1), calls=%async_computation | async-start | bytes 4325376 | tf_op jit(solution)/shard_map/all_to_all | solution.py:189
  97.4 71.2 %all-to-all-start.1 = ((bf16[16,32,4224]{2,1,0:T(8,128)(2,1)}), bf16[16,32,4224]{2,1,0:T(8,128)(2,1)}, u32[]{:S(2)}, u32[]{:S(2)}) async-start(bf16[16,32,4224]{2,1,0:T(8,128)(2,1)} %pad_maximum_fusion), calls=%async_computation.1 | async-start | bytes 8650752 | tf_op jit(solution)/shard_map/all_to_all | solution.py:189
  102.1 163.3 %all-gather.3.cloned.1.call-start = ((), (), s32[]{:S(2)}) async-start(), calls=%async_computation.6 | async-start | bytes 1769472 | tf_op jit(solution)/shard_map/all_gather | solution.py:291
  105.3 11.0 %collective-permute-start.1 = (bf16[48,4224]{1,0:T(8,128)(2,1)S(1)}, bf16[48,4224]{1,0:T(8,128)(2,1)S(1)}, u32[]{:S(2)}, u32[]{:S(2)}) collective-permute-start(bf16[48,4224]{1,0:T(8,128)(2,1)S(1)} %pad_maximum_fusion.4.refs_2_), channel_id=1, source_target_pairs={{64,0},{128,64},{192,128},{256,192},{320,256},{384,320},{448,384},... | collective-permute-start | bytes 1216520 | tf_op jit(solution)/shard_map/ppermute | solution.py:250
  106.6 9.7 %collective-permute-start = (bf16[48,4224]{1,0:T(8,128)(2,1)S(1)}, bf16[48,4224]{1,0:T(8,128)(2,1)S(1)}, u32[]{:S(2)}, u32[]{:S(2)}) collective-permute-start(bf16[48,4224]{1,0:T(8,128)(2,1)S(1)} %pad_maximum_fusion.4.refs_2_), channel_id=1, source_target_pairs={{0,64},{64,128},{128,192},{192,256},{256,320},{320,384},{384,448},... | collective-permute-start | bytes 1216520 | tf_op jit(solution)/shard_map/ppermute | solution.py:249
  110.7 13.5 %collective-permute-start.5 = (bf16[48,4224]{1,0:T(8,128)(2,1)S(1)}, bf16[48,4224]{1,0:T(8,128)(2,1)S(1)}, u32[]{:S(2)}, u32[]{:S(2)}) collective-permute-start(bf16[48,4224]{1,0:T(8,128)(2,1)S(1)} %pad_maximum_fusion.5.refs_2_), channel_id=1, source_target_pairs={{64,0},{128,64},{192,128},{256,192},{320,256},{384,320},{448,384},... | collective-permute-start | bytes 1216520 | tf_op jit(solution)/shard_map/ppermute | solution.py:250
  112.0 13.2 %collective-permute-start.4 = (bf16[48,4224]{1,0:T(8,128)(2,1)S(1)}, bf16[48,4224]{1,0:T(8,128)(2,1)S(1)}, u32[]{:S(2)}, u32[]{:S(2)}) collective-permute-start(bf16[48,4224]{1,0:T(8,128)(2,1)S(1)} %pad_maximum_fusion.5.refs_2_), channel_id=1, source_target_pairs={{0,64},{64,128},{128,192},{192,256},{256,320},{320,384},{384,448},... | collective-permute-start | bytes 1216520 | tf_op jit(solution)/shard_map/ppermute | solution.py:249
  117.5 11.8 %collective-permute-start.8 = (bf16[48,4224]{1,0:T(8,128)(2,1)S(1)}, bf16[48,4224]{1,0:T(8,128)(2,1)}, u32[]{:S(2)}, u32[]{:S(2)}) collective-permute-start(bf16[48,4224]{1,0:T(8,128)(2,1)S(1)} %get-tuple-element.51), channel_id=1, source_target_pairs={{64,128},{128,192},{192,256},{256,320},{320,384},{384,448},{65,129... | collective-permute-start | bytes 1216520 | tf_op jit(solution)/shard_map/ppermute | solution.py:249
  118.9 12.8 %collective-permute-start.9 = (bf16[48,4224]{1,0:T(8,128)(2,1)S(1)}, bf16[48,4224]{1,0:T(8,128)(2,1)}, u32[]{:S(2)}, u32[]{:S(2)}) collective-permute-start(bf16[48,4224]{1,0:T(8,128)(2,1)S(1)} %get-tuple-element.52), channel_id=1, source_target_pairs={{64,0},{128,64},{192,128},{256,192},{320,256},{384,320},{65,1},{12... | collective-permute-start | bytes 1216520 | tf_op jit(solution)/shard_map/ppermute | solution.py:250
  127.9 14.0 %collective-permute-start.7 = (bf16[48,4224]{1,0:T(8,128)(2,1)S(1)}, bf16[48,4224]{1,0:T(8,128)(2,1)}, u32[]{:S(2)}, u32[]{:S(2)}) collective-permute-start(bf16[48,4224]{1,0:T(8,128)(2,1)S(1)} %get-tuple-element.50), channel_id=1, source_target_pairs={{64,0},{128,64},{192,128},{256,192},{320,256},{384,320},{65,1},{12... | collective-permute-start | bytes 1216520 | tf_op jit(solution)/shard_map/ppermute | solution.py:250
  133.4 21.6 %collective-permute-start.12 = (bf16[48,4224]{1,0:T(8,128)(2,1)}, bf16[48,4224]{1,0:T(8,128)(2,1)S(1)}, u32[]{:S(2)}, u32[]{:S(2)}) collective-permute-start(bf16[48,4224]{1,0:T(8,128)(2,1)} %get-tuple-element.57), channel_id=1, source_target_pairs={{128,192},{192,256},{256,320},{320,384},{384,448},{129,193},{193,2... | collective-permute-start | bytes 1216520 | tf_op jit(solution)/shard_map/ppermute | solution.py:249
  134.1 20.9 %collective-permute-start.13 = (bf16[48,4224]{1,0:T(8,128)(2,1)}, bf16[48,4224]{1,0:T(8,128)(2,1)}, u32[]{:S(2)}, u32[]{:S(2)}) collective-permute-start(bf16[48,4224]{1,0:T(8,128)(2,1)} %get-tuple-element.58), channel_id=1, source_target_pairs={{64,0},{128,64},{192,128},{256,192},{320,256},{65,1},{129,65},{193... | collective-permute-start | bytes 1216520 | tf_op jit(solution)/shard_map/ppermute | solution.py:250
  144.7 16.2 %collective-permute-start.10 = (bf16[48,4224]{1,0:T(8,128)(2,1)}, bf16[48,4224]{1,0:T(8,128)(2,1)}, u32[]{:S(2)}, u32[]{:S(2)}) collective-permute-start(bf16[48,4224]{1,0:T(8,128)(2,1)} %get-tuple-element.55), channel_id=1, source_target_pairs={{128,192},{192,256},{256,320},{320,384},{384,448},{129,193},{193,2... | collective-permute-start | bytes 1216520 | tf_op jit(solution)/shard_map/ppermute | solution.py:249
  146.1 14.7 %collective-permute-start.11 = (bf16[48,4224]{1,0:T(8,128)(2,1)}, bf16[48,4224]{1,0:T(8,128)(2,1)}, u32[]{:S(2)}, u32[]{:S(2)}) collective-permute-start(bf16[48,4224]{1,0:T(8,128)(2,1)} %get-tuple-element.56), channel_id=1, source_target_pairs={{64,0},{128,64},{192,128},{256,192},{320,256},{65,1},{129,65},{193... | collective-permute-start | bytes 1216520 | tf_op jit(solution)/shard_map/ppermute | solution.py:250
  158.9 20.5 %collective-permute-start.14 = (bf16[48,4224]{1,0:T(8,128)(2,1)}, bf16[48,4224]{1,0:T(8,128)(2,1)S(1)}, u32[]{:S(2)}, u32[]{:S(2)}) collective-permute-start(bf16[48,4224]{1,0:T(8,128)(2,1)} %copy-done.1), channel_id=1, source_target_pairs={{192,256},{256,320},{320,384},{384,448},{193,257},{257,321},{321,3... | collective-permute-start | bytes 1216520 | tf_op jit(solution)/shard_map/ppermute | solution.py:249
  159.6 19.8 %collective-permute-start.15 = (bf16[48,4224]{1,0:T(8,128)(2,1)}, bf16[48,4224]{1,0:T(8,128)(2,1)}, u32[]{:S(2)}, u32[]{:S(2)}) collective-permute-start(bf16[48,4224]{1,0:T(8,128)(2,1)} %get-tuple-element.65), channel_id=1, source_target_pairs={{64,0},{128,64},{192,128},{256,192},{65,1},{129,65},{193,129},{257... | collective-permute-start | bytes 1216520 | tf_op jit(solution)/shard_map/ppermute | solution.py:250
  165.9 17.9 %collective-permute-start.18 = (bf16[48,4224]{1,0:T(8,128)(2,1)}, bf16[48,4224]{1,0:T(8,128)(2,1)}, u32[]{:S(2)}, u32[]{:S(2)}) collective-permute-start(bf16[48,4224]{1,0:T(8,128)(2,1)} %get-tuple-element.77), channel_id=1, source_target_pairs={{192,256},{256,320},{320,384},{384,448},{193,257},{257,321},{321,3... | collective-permute-start | bytes 1216520 | tf_op jit(solution)/shard_map/ppermute | solution.py:249
  167.4 16.5 %collective-permute-start.19 = (bf16[48,4224]{1,0:T(8,128)(2,1)}, bf16[48,4224]{1,0:T(8,128)(2,1)}, u32[]{:S(2)}, u32[]{:S(2)}) collective-permute-start(bf16[48,4224]{1,0:T(8,128)(2,1)} %get-tuple-element.78), channel_id=1, source_target_pairs={{64,0},{128,64},{192,128},{256,192},{65,1},{129,65},{193,129},{257... | collective-permute-start | bytes 1216520 | tf_op jit(solution)/shard_map/ppermute | solution.py:250
  182.6 11.0 %collective-permute-start.17 = (bf16[48,4224]{1,0:T(8,128)(2,1)}, bf16[48,4224]{1,0:T(8,128)(2,1)S(1)}, u32[]{:S(2)}, u32[]{:S(2)}) collective-permute-start(bf16[48,4224]{1,0:T(8,128)(2,1)} %get-tuple-element.76), channel_id=1, source_target_pairs={{64,0},{128,64},{192,128},{65,1},{129,65},{193,129},{66,2},{130,66... | collective-permute-start | bytes 1216520 | tf_op jit(solution)/shard_map/ppermute | solution.py:250
  186.3 11.7 %collective-permute-start.21 = (bf16[48,4224]{1,0:T(8,128)(2,1)}, bf16[48,4224]{1,0:T(8,128)(2,1)S(1)}, u32[]{:S(2)}, u32[]{:S(2)}) collective-permute-start(bf16[48,4224]{1,0:T(8,128)(2,1)} %get-tuple-element.85), channel_id=1, source_target_pairs={{64,0},{128,64},{192,128},{65,1},{129,65},{193,129},{66,2},{130,66... | collective-permute-start | bytes 1216520 | tf_op jit(solution)/shard_map/ppermute | solution.py:250
  200.4 29.6 %all-to-all-start.2 = ((bf16[8,192,128]{2,1,0:T(8,128)(2,1)}), bf16[8,192,128]{2,1,0:T(8,128)(2,1)S(1)}, u32[]{:S(2)}, u32[]{:S(2)}) async-start(bf16[8,192,128]{2,1,0:T(8,128)(2,1)} %broadcast_in_dim.435), calls=%async_computation.2 | async-start | bytes 786432 | tf_op jit(solution)/shard_map/all_to_all | solution.py:296
  279.2 30.6 %all-to-all-start.3 = ((bf16[16,16,8,512]{3,2,1,0:T(8,128)(2,1)}), bf16[16,16,8,512]{3,2,1,0:T(8,128)(2,1)S(1)}, u32[]{:S(2)}, u32[]{:S(2)}) async-start(bf16[16,16,8,512]{3,2,1,0:T(8,128)(2,1)} %bitcast.169), calls=%async_computation.3 | async-start | bytes 4194304 | tf_op jit(solution)/shard_map/all_to_all | solution.py:330
  (101 other events, 945.5 us)
Sparse Core Ops, SparseCore 0:
  179.5 85.8 all-gather.2

commit v6 on v5

--- a/solution.py
+++ b/solution.py
@@ -12,8 +12,8 @@
 LANES = 128
 ROWS = 48
 MOST = 2
-EARLY = 3
 STEPS = 5
+NEAR = 4
 HOME, HI, MID, ONE, POS = 0, 8, 16, 32, 33
 
 
@@ -34,12 +34,12 @@
     return jnp.pad(meta, ((0, 0), (0, LANES - meta.shape[-1])))
 
 
-def places(meta, me, columns, quad, tok, top):
+def places(meta, me, columns, quad, tok, top, sets=1):
     n = meta.shape[0]
-    box = jnp.arange(columns * quad * MOST, dtype=jnp.int32)[None, :]
+    box = jnp.arange(columns * sets * quad * MOST, dtype=jnp.int32)[None, :]
     row = jnp.arange(n, dtype=jnp.int32)[:, None]
-    target = (box // (quad * MOST) * quad + me).astype(BF)
-    same = (row // tok) % quad == (box // MOST) % quad
+    target = (box // (sets * quad * MOST) * quad + me).astype(BF)
+    same = (row // tok) % (sets * quad) == (box // MOST) % (sets * quad)
     hits = [(meta[:, HOME + k : HOME + k + 1] == target) & same for k in range(top)]
     match = hits[0]
     for hit in hits[1:]:
@@ -136,6 +136,36 @@
     )(my_dp.astype(jnp.int32).reshape(1), *flat)
 
 
+def down_kernel(places_of, n_dp, dp_ref, down_ref, *refs):
+    out_ref = refs[-1]
+    z = dp_ref[0]
+    total = None
+    for i in range(0, len(places_of), 2):
+        pair = range(i, min(i + 2, len(places_of)))
+        weights = [
+            down_ref[pl.ds(pl.multiple_of(places_of[p](z) * LANES, LANES), LANES), :] for p in pair
+        ]
+        part = jnp.dot(
+            jnp.concatenate([refs[p][...] for p in pair], axis=1),
+            jnp.concatenate(weights, axis=0),
+            preferred_element_type=F32,
+        )
+        total = part if total is None else total + part
+    out_ref[...] = total.astype(BF)
+
+
+def project_down(shards, places_of, down, n_dp, my_dp):
+    vmem = pl.BlockSpec(memory_space=pltpu.VMEM)
+    return pl.pallas_call(
+        functools.partial(down_kernel, places_of, n_dp),
+        out_shape=jax.ShapeDtypeStruct((shards[0].shape[0], down.shape[1]), BF),
+        in_specs=[pl.BlockSpec(memory_space=pltpu.SMEM), vmem] + [vmem] * len(shards),
+        out_specs=vmem,
+        compiler_params=pltpu.CompilerParams(vmem_limit_bytes=32 * 2**20),
+        cost_estimate=SMALL,
+    )(my_dp.astype(jnp.int32).reshape(1), down, *shards)
+
+
 def on_device(
     tokens, experts, replicas, route_weights, slot_tables, partners, slot_rows, gate_w, up_w, down_w
 ):
@@ -173,21 +203,19 @@
     line = jnp.arange(boxes, dtype=jnp.int32)
     lower = (line[:, None] < line[None, :]).astype(BF)
 
-    def exchange(sets, after=None):
-        send = []
-        for i, local in enumerate(sets):
-            place = places(local[:, model:], me, columns, quad, tok, top)[1]
-            if after is not None and i == len(sets) - 1:
-                place = place & after
-            send.append(
-                lax.dot_general(
-                    place.astype(BF), local, (((0,), (0,)), ((), ())), preferred_element_type=F32
-                )
-                .astype(BF)
-                .reshape(columns, quad * MOST, wide)
-            )
+    def exchange(local, sets, after=None):
+        place = places(local[:, model:], me, columns, quad, tok, top, sets)[1]
+        if after is not None:
+            place = place & after
+        send = lax.dot_general(
+            place.astype(BF), local, (((0,), (0,)), ((), ())), preferred_element_type=F32
+        ).astype(BF)
         return lax.all_to_all(
-            jnp.concatenate(send, axis=1), ("x", "y"), split_axis=0, concat_axis=0, tiled=True
+            send.reshape(columns, sets * quad * MOST, wide),
+            ("x", "y"),
+            split_axis=0,
+            concat_axis=0,
+            tiled=True,
         )
 
     def compacted(received, index, local, step, dp, after=None):
@@ -212,110 +240,77 @@
         side = jnp.where(lanes == POS, position.astype(BF), side)
         return jnp.concatenate([compact, side], axis=1)
 
-    received = exchange([held[step] for step in range(steps)])
-
-    beyond = list(range(STEPS + 1, n_dp))
-    half = lax.dynamic_index_in_dim(
-        held.reshape(steps, 2, 2, tok, wide), lax.axis_index("core"), 2, keepdims=False
-    )
-    half = half.reshape(steps * 2 * tok, wide)
-    distant = jnp.stack(
-        [
-            lax.ppermute(
-                half,
-                "dp",
-                [(i, i + k) for i in range(n_dp - k)] + [(i + k, i) for i in range(n_dp - k)],
-            )
-            for k in beyond
-        ]
-    ).reshape(len(beyond), steps, 2, tok, wide)
-    distant = lax.all_gather(distant, "core", axis=3, tiled=False).reshape(
-        len(beyond), steps, group, wide
-    )
+    held_rows = held.reshape(steps * group, wide)
+    received = exchange(held_rows, steps)
+
     both_w = jnp.concatenate([gate_w[0], up_w[0]], axis=1)
     batch = steps * n_dp
     own = [compacted(received, step, held[step], step, my_dp) for step in range(steps)]
-    ready = own[-1][0, 0] == own[-1][0, 0]
-    received_far = exchange(
-        [distant[i, step] for i in range(len(beyond)) for step in range(steps)], ready
-    )
+    beyond = list(range(STEPS + 1, n_dp))
+    apart = {
+        k: [(i, i + k) for i in range(n_dp - k)] + [(i + k, i) for i in range(n_dp - k)]
+        for k in range(NEAR + 1, n_dp)
+    }
+    leaving = jnp.where(own[-1][0, 0] == own[-1][0, 0], held_rows, jnp.zeros_like(held_rows))
+    distant = jnp.concatenate([lax.ppermute(leaving, "dp", apart[k]) for k in beyond], axis=0)
+
     to_right, to_left = list(own), list(own)
     done = [[[] for _ in range(n_dp)] for _ in range(steps)]
-    middle = [{} for _ in range(steps)]
     last = n_dp - 1
-    hidden = None
     for j in range(1, STEPS + 1):
         for s in range(steps):
             to_right[s] = lax.ppermute(to_right[s], "dp", right[j - 1])
             to_left[s] = lax.ppermute(to_left[s], "dp", left[j - 1])
             blocks = [to_right[s], to_left[s]] + ([own[s]] if j == 1 else [])
             passed = 2 if j < STEPS else 0
-            extra = [hidden] if j == EARLY + 1 and s == 0 else []
+            extra = [late[0]] if j == STEPS and s == 0 else []
             extra += [made[0]] if (j, s) != (1, 0) else []
             sent, made = project(both_w, blocks, passed, extra)
             if passed:
                 to_right[s], to_left[s] = sent
-            if j > EARLY:
-                middle[s][j] = made[0][:, :LANES] + made[1][:, :LANES]
             done[s][j].append((made[0], 0, last))
             done[s][n_dp - j].append((made[1], 0, last))
             if j == 1:
                 done[s][0].append((made[2], 0, last))
-        if j == EARLY:
+            if (j, s) == (1, steps - 1):
+                received_far = exchange(
+                    distant, len(beyond) * steps, made[0][0, 0] == made[0][0, 0]
+                )
+        if j == STEPS - 1:
             ready = made[0][0, 0] == made[0][0, 0]
-            blocks = [
-                compacted(
-                    received_far,
-                    i * steps + s,
-                    distant[i, s],
-                    s,
-                    jnp.where(my_dp >= k, my_dp - k, my_dp + k),
-                    ready,
-                )
-                for i, k in enumerate(beyond)
-                for s in range(steps)
-            ]
-            late = project(both_w, blocks, 0)[1]
+            late = project(
+                both_w,
+                [
+                    compacted(
+                        received_far,
+                        i * steps + s,
+                        distant[(i * steps + s) * group : (i * steps + s + 1) * group],
+                        s,
+                        jnp.where(my_dp >= k, my_dp - k, my_dp + k),
+                        ready,
+                    )
+                    for i, k in enumerate(beyond)
+                    for s in range(steps)
+                ],
+                0,
+            )[1]
             for i, k in enumerate(beyond):
                 for s in range(steps):
                     done[s][k].append((late[i * steps + s], k, last))
                     done[s][n_dp - k].append((late[i * steps + s], 0, last - k))
-            hidden = assemble(
-                [
-                    [parts if parts else [(done[s][0][0][0], n_dp, n_dp)] for parts in done[s]]
-                    for s in range(steps)
-                ],
-                0,
-                my_dp,
-            )
-    gathered = lax.all_gather(hidden, "dp", axis=0, tiled=False).reshape(
-        n_dp, steps, n_dp, ROWS, LANES
-    )
-    span = range(EARLY + 1, STEPS + 1)
-    rest = jnp.stack([jnp.stack([middle[s][k] for k in span]) for s in range(steps)])
-    rest = lax.all_to_all(
-        jnp.broadcast_to(
-            rest.reshape(1, steps * len(span) * ROWS, LANES),
-            (n_dp, steps * len(span) * ROWS, LANES),
-        ),
-        "dp",
-        split_axis=0,
-        concat_axis=0,
-        tiled=True,
-    ).reshape(n_dp, steps, len(span), ROWS, LANES)
-    for z in range(n_dp):
-        for i, k in enumerate(span):
-            for d in (z - k, z + k):
-                if 0 <= d < n_dp:
-                    gathered = lax.dynamic_update_slice(
-                        gathered, rest[z : z + 1, :, i : i + 1], (z, 0, d, 0, 0)
-                    )
-    output = jnp.einsum(
-        "zrh,zhf->rf",
-        gathered.reshape(n_dp, batch * ROWS, LANES),
-        down_w[0].reshape(n_dp, LANES, width),
-        preferred_element_type=F32,
-    ).astype(BF)
+    hidden = assemble(done, 0, my_dp)
+    shards, places_of = [hidden], [lambda z: z]
+    going_right, going_left = hidden, hidden
+    for k in range(NEAR + 1, n_dp):
+        shards.append(lax.ppermute(hidden, "dp", apart[k]))
+        places_of.append(lambda z, k=k: lax.rem(jnp.where(z >= k, z - k, z + k), n_dp))
+    for j in range(1, NEAR + 1):
+        going_right = lax.ppermute(going_right, "dp", right[j - 1])
+        going_left = lax.ppermute(going_left, "dp", left[j - 1])
+        shards += [going_right, going_left]
+        places_of.append(lambda z, j=j: lax.rem(z - j + n_dp, n_dp))
+        places_of.append(lambda z, j=j: lax.rem(z + j, n_dp))
+    output = project_down(shards, places_of, down_w[0], n_dp, my_dp)
 
     sides = assemble(done, LANES, my_dp).reshape(batch, ROWS, LANES)
 

time: 359 us -> 344 us (0.958)
  local copies, waits for them, and re-layouts: 53.9 us -> 19.5 us
  starting transfers between devices: 72.7 us -> 88.3 us
  waiting for transfers between devices: 97.4 us -> 111 us
  blocking collectives: 59.5 us -> 72.2 us
  between operations: 21.4 us -> 8.98 us
  other arithmetic: 14 us -> 8.13 us
  matrix products: 18.5 us -> 13.4 us
    ppermute x2 -> x13, waiting for transfers between devices: 0.01 us -> 46.9 us  [the longest x2 19.3 us: on_device(): lax.ppermute(leaving, 'dp', apart[k])]
    all_gather x1 -> x0, waiting for transfers between devices: 35.4 us -> none  [on_device(): lax.all_gather(hidden, 'dp', axis=0, tiled=False)]
    ppermute x2 -> x13, starting transfers between devices: 13 us -> 34.5 us  [the longest x2 12.1 us: on_device(): lax.ppermute(leaving, 'dp', apart[k])]
    unnamed x197 -> x72, local copies, waits for them, and re-layouts: 18.6 us -> 6.16 us
    all_to_all x3 -> x2, starting transfers between devices: 24 us -> 12 us  [exchange(): lax.all_to_all(send.reshape(columns, sets * quad * MOST, wide), ('x', 'y'...]
    all_to_all x1, blocking collectives: 10.3 us -> 22 us  [on_device(): lax.all_to_all(partial, 'core', split_axis=0, concat_axis=0, tiled=True)]
    dynamic_update_slice x14 -> x0, local copies, waits for them, and re-layouts: 8.53 us -> none  [on_device(): lax.dynamic_update_slice(gathered, rest[z:z + 1, :, i:i + 1], (z, 0, d, 0...]
    all_to_all x3 -> x2, waiting for transfers between devices: 18.5 us -> 26.3 us  [exchange(): lax.all_to_all(send.reshape(columns, sets * quad * MOST, wide), ('x', 'y'...]
  transfers between devices with their start and end apart: 27 -> 36, of which waited for: 10 -> 15; matrix products, arithmetic and copies ran while one was open for 11% -> 5% of each run, Pallas kernels for 5% -> 4%
where the time goes in v6:
time: 344 us; the launch traced here: 340 us
  waiting for transfers between devices  111 us (32%)
  starting transfers between devices  88.3 us (26%)
  blocking collectives  72.2 us (21%)
  local copies, waits for them, and re-layouts  19.5 us (6%)
  Pallas kernels  18.2 us (5%)
  matrix products  13.4 us (4%)
  between operations  8.98 us (3%)
  other arithmetic  8.13 us (2%)
    all_to_all x1, blocking collectives, on_device(): lax.all_to_all(halves.reshape(2 * n_dp, mine * width // LANES, LANES), ('...  28.6 us
    all_to_all x2, waiting for transfers between devices, exchange(): lax.all_to_all(send.reshape(columns, sets * quad * MOST, wide), ('x', 'y'...  26.3 us
    ppermute x10, waiting for transfers between devices, on_device(): to_left[s] = lax.ppermute(to_left[s], 'dp', left[j - 1])  24 us
    ppermute x10, starting transfers between devices, on_device(): to_right[s] = lax.ppermute(to_right[s], 'dp', right[j - 1])  22.1 us
    all_to_all x1, blocking collectives, on_device(): lax.all_to_all(partial, 'core', split_axis=0, concat_axis=0, tiled=True)  22 us
    all_gather x1, blocking collectives, on_device(): lax.all_gather(packed.reshape(steps, tok, wide), ('zh', 'core'), axis=1,...  21.7 us
    ppermute x2, waiting for transfers between devices, on_device(): lax.ppermute(leaving, 'dp', apart[k])  19.3 us
    pallas_call x11, Pallas kernels, project(): pl.pallas_call(functools.partial(project_kernel, count, passed, len(extra...  16.6 us
  transfers between devices with their start and end apart: 36, of which 15 were waited for; matrix products, arithmetic and copies ran while one was open for 5% of the time, Pallas kernels for 4%

profile of v6, /device:TPU:1, one launch (start us, length us, event | category | flops | bytes accessed | tf_op | source)
XLA Modules:
  0.0 340.0 jit_solution(8065347310564623122)
XLA Ops:
  4.8 21.7 %all_gather.3 = bf16[2,24,4224]{2,0,1:T(2,128)(2,1)S(1)} all-gather(bf16[2,6,4224]{2,0,1:T(2,128)(2,1)S(1)} %pad_maximum_fusion.7), channel_id=1, replica_groups=mesh['dp'=8,'x'=4,'y'=4,'zh'=2,'core'=2] {'zh','core'}, dimensions={1}, use_global_device_ids=true | all-gather | bytes 506880 | tf_op jit(solution)/shard_map/all_gather | solution.py:197
  29.1 5.7 %all-to-all-start = ((bf16[16,16,4224]{2,1,0:T(8,128)(2,1)}), bf16[16,16,4224]{2,1,0:T(8,128)(2,1)S(1)}, u32[]{:S(2)}, u32[]{:S(2)}) async-start(bf16[16,16,4224]{2,1,0:T(8,128)(2,1)} %bitcast.7), calls=%async_computation | async-start | bytes 4325376 | tf_op jit(solution)/shard_map/all_to_all | solution.py:213
  38.4 26.3 %all-to-all-done = bf16[16,16,4224]{2,1,0:T(8,128)(2,1)S(1)} async-done(((bf16[16,16,4224]{2,1,0:T(8,128)(2,1)}), bf16[16,16,4224]{2,1,0:T(8,128)(2,1)S(1)}, u32[]{:S(2)}, u32[]{:S(2)}) %all-to-all-start) | async-done | bytes 2162720 | tf_op jit(solution)/shard_map/all_to_all | solution.py:213
  67.9 9.6 %collective-permute-start = (bf16[48,4224]{1,0:T(8,128)(2,1)S(1)}, bf16[48,4224]{1,0:T(8,128)(2,1)S(1)}, u32[]{:S(2)}, u32[]{:S(2)}) collective-permute-start(bf16[48,4224]{1,0:T(8,128)(2,1)S(1)} %pad_maximum_fusion.1.refs_2_), channel_id=1, source_target_pairs={{0,64},{64,128},{128,192},{192,256},{256,320},{320,384},{384,448},... | collective-permute-start | bytes 1216520 | tf_op jit(solution)/shard_map/ppermute | solution.py:262
  79.3 4.0 %collective-permute-start.4 = (bf16[48,4224]{1,0:T(8,128)(2,1)S(1)}, bf16[48,4224]{1,0:T(8,128)(2,1)S(1)}, u32[]{:S(2)}, u32[]{:S(2)}) collective-permute-start(bf16[48,4224]{1,0:T(8,128)(2,1)S(1)} %pad_maximum_fusion.2.refs_2_), channel_id=1, source_target_pairs={{0,64},{64,128},{128,192},{192,256},{256,320},{320,384},{384,448},... | collective-permute-start | bytes 1216520 | tf_op jit(solution)/shard_map/ppermute | solution.py:262
  84.7 7.3 %collective-permute-start.2 = (bf16[48,4224]{1,0:T(8,128)(2,1)S(1)}, bf16[48,4224]{1,0:T(8,128)(2,1)S(1)}, u32[]{:S(2)}, u32[]{:S(2)}) collective-permute-start(bf16[48,4224]{1,0:T(8,128)(2,1)S(1)} %broadcast_select_fusion), channel_id=1, source_target_pairs={{0,384},{64,448},{384,0},{448,64},{1,385},{65,449},{385,1},{449,65... | collective-permute-start | bytes 1216520 | tf_op jit(solution)/shard_map/ppermute | solution.py:255
  92.3 4.8 %collective-permute-start.3 = (bf16[48,4224]{1,0:T(8,128)(2,1)S(1)}, bf16[48,4224]{1,0:T(8,128)(2,1)S(1)}, u32[]{:S(2)}, u32[]{:S(2)}) collective-permute-start(bf16[48,4224]{1,0:T(8,128)(2,1)S(1)} %broadcast_select_fusion), channel_id=1, source_target_pairs={{0,448},{448,0},{1,449},{449,1},{2,450},{450,2},{3,451},{451,3},{4... | collective-permute-start | bytes 1216520 | tf_op jit(solution)/shard_map/ppermute | solution.py:255
  102.6 19.3 %collective-permute-done.2 = bf16[48,4224]{1,0:T(8,128)(2,1)S(1)} collective-permute-done((bf16[48,4224]{1,0:T(8,128)(2,1)S(1)}, bf16[48,4224]{1,0:T(8,128)(2,1)S(1)}, u32[]{:S(2)}, u32[]{:S(2)}) %collective-permute-start.2) | collective-permute-done | bytes 405536 | tf_op jit(solution)/shard_map/ppermute | solution.py:255
  123.2 5.0 %convolution_convert_fusion = bf16[512,4224]{1,0:T(8,128)(2,1)} fusion(bf16[96,4224]{1,0:T(8,128)(2,1)} %copy-done.22, f32[512]{0:T(512)S(1)} %fusion.188, s32[512]{0:T(512)S(1)} %get-tuple-element.183, s32[96]{0:T(128)S(1)} %get-tuple-element.185, pred[]{:T(512)} %bitcast.17, bf16[512]{0:T(512)(128)(2,1)S(1)} %get-tuple-element.184, ...), kind=kOutput, calls=%fused_computation | convolution fusion | flops 430255104 | bytes 5143809 | tf_op jit(solution)/shard_map/dot_general | solution.py:210
  128.3 6.3 %all-to-all-start.1 = ((bf16[16,32,4224]{2,1,0:T(8,128)(2,1)}), bf16[16,32,4224]{2,1,0:T(8,128)(2,1)}, u32[]{:S(2)}, u32[]{:S(2)}) async-start(bf16[16,32,4224]{2,1,0:T(8,128)(2,1)} %bitcast.127), calls=%async_computation.1 | async-start | bytes 8650752 | tf_op jit(solution)/shard_map/all_to_all | solution.py:213
  140.0 6.4 %collective-permute-done.9.refs_1_ = bf16[48,4224]{1,0:T(8,128)(2,1)} collective-permute-done((bf16[48,4224]{1,0:T(8,128)(2,1)S(1)}, bf16[48,4224]{1,0:T(8,128)(2,1)}, u32[]{:S(2)}, u32[]{:S(2)}) %collective-permute-start.9) | collective-permute-done | bytes 405536 | tf_op jit(solution)/shard_map/ppermute | solution.py:263
  150.7 4.4 %collective-permute-done.7.refs_1_ = bf16[48,4224]{1,0:T(8,128)(2,1)} collective-permute-done((bf16[48,4224]{1,0:T(8,128)(2,1)S(1)}, bf16[48,4224]{1,0:T(8,128)(2,1)}, u32[]{:S(2)}, u32[]{:S(2)}) %collective-permute-start.7) | collective-permute-done | bytes 405536 | tf_op jit(solution)/shard_map/ppermute | solution.py:263
  168.8 3.6 %collective-permute-done.11.refs_1_ = bf16[48,4224]{1,0:T(8,128)(2,1)} collective-permute-done((bf16[48,4224]{1,0:T(8,128)(2,1)}, bf16[48,4224]{1,0:T(8,128)(2,1)}, u32[]{:S(2)}, u32[]{:S(2)}) %collective-permute-start.11) | collective-permute-done | bytes 405536 | tf_op jit(solution)/shard_map/ppermute | solution.py:263
  184.4 4.8 %collective-permute-done.15.refs_1_ = bf16[48,4224]{1,0:T(8,128)(2,1)} collective-permute-done((bf16[48,4224]{1,0:T(8,128)(2,1)}, bf16[48,4224]{1,0:T(8,128)(2,1)}, u32[]{:S(2)}, u32[]{:S(2)}) %collective-permute-start.15) | collective-permute-done | bytes 405536 | tf_op jit(solution)/shard_map/ppermute | solution.py:263
  208.9 4.0 %collective-permute-start.25 = (bf16[768,128]{1,0:T(8,128)(2,1)S(1)}, bf16[768,128]{1,0:T(8,128)(2,1)S(1)}, u32[]{:S(2)}, u32[]{:S(2)}) collective-permute-start(bf16[768,128]{1,0:T(8,128)(2,1)S(1)} %shard_map.112.refs_0_), channel_id=1, source_target_pairs={{0,64},{64,128},{128,192},{192,256},{256,320},{320,384},{384,448},... | collective-permute-start | bytes 589832 | tf_op jit(solution)/shard_map/ppermute | solution.py:308
  216.2 9.7 %collective-permute-done.28.refs_7_ = bf16[768,128]{1,0:T(8,128)(2,1)S(1)} collective-permute-done((bf16[768,128]{1,0:T(8,128)(2,1)S(1)}, bf16[768,128]{1,0:T(8,128)(2,1)S(1)}, u32[]{:S(2)}, u32[]{:S(2)}) %collective-permute-start.28) | collective-permute-done | bytes 196640 | tf_op jit(solution)/shard_map/ppermute | solution.py:309
  227.9 4.3 %collective-permute-start.24 = (bf16[768,128]{1,0:T(8,128)(2,1)S(1)}, bf16[768,128]{1,0:T(8,128)(2,1)S(1)}, u32[]{:S(2)}, u32[]{:S(2)}) collective-permute-start(bf16[768,128]{1,0:T(8,128)(2,1)S(1)} %shard_map.112.refs_0_), channel_id=1, source_target_pairs={{0,448},{448,0},{1,449},{449,1},{2,450},{450,2},{3,451},{451,3},{4... | collective-permute-start | bytes 589832 | tf_op jit(solution)/shard_map/ppermute | solution.py:305
  232.2 4.8 %collective-permute-start.23 = (bf16[768,128]{1,0:T(8,128)(2,1)S(1)}, bf16[768,128]{1,0:T(8,128)(2,1)S(1)}, u32[]{:S(2)}, u32[]{:S(2)}) collective-permute-start(bf16[768,128]{1,0:T(8,128)(2,1)S(1)} %shard_map.112.refs_0_), channel_id=1, source_target_pairs={{0,384},{64,448},{384,0},{448,64},{1,385},{65,449},{385,1},{449,65... | collective-permute-start | bytes 589832 | tf_op jit(solution)/shard_map/ppermute | solution.py:305
  241.5 6.1 %collective-permute-done.23.refs_2_ = bf16[768,128]{1,0:T(8,128)(2,1)S(1)} collective-permute-done((bf16[768,128]{1,0:T(8,128)(2,1)S(1)}, bf16[768,128]{1,0:T(8,128)(2,1)S(1)}, u32[]{:S(2)}, u32[]{:S(2)}) %collective-permute-start.23) | collective-permute-done | bytes 196640 | tf_op jit(solution)/shard_map/ppermute | solution.py:305
  247.6 10.5 %collective-permute-done.22.refs_1_ = bf16[768,128]{1,0:T(8,128)(2,1)S(1)} collective-permute-done((bf16[768,128]{1,0:T(8,128)(2,1)S(1)}, bf16[768,128]{1,0:T(8,128)(2,1)S(1)}, u32[]{:S(2)}, u32[]{:S(2)}) %collective-permute-start.22) | collective-permute-done | bytes 196640 | tf_op jit(solution)/shard_map/ppermute | solution.py:305
  262.4 6.6 %all-to-all-start.2 = ((bf16[16,16,8,512]{3,2,1,0:T(8,128)(2,1)}), bf16[16,16,8,512]{3,2,1,0:T(8,128)(2,1)S(1)}, u32[]{:S(2)}, u32[]{:S(2)}) async-start(bf16[16,16,8,512]{3,2,1,0:T(8,128)(2,1)} %bitcast.128), calls=%async_computation.2 | async-start | bytes 4194304 | tf_op jit(solution)/shard_map/all_to_all | solution.py:325
  273.1 14.2 %all-to-all-done.2 = bf16[16,16,8,512]{3,2,1,0:T(8,128)(2,1)S(1)} async-done(((bf16[16,16,8,512]{3,2,1,0:T(8,128)(2,1)}), bf16[16,16,8,512]{3,2,1,0:T(8,128)(2,1)S(1)}, u32[]{:S(2)}, u32[]{:S(2)}) %all-to-all-start.2) | async-done | bytes 2097184 | tf_op jit(solution)/shard_map/all_to_all | solution.py:325
  288.0 22.0 %all_to_all.25 = bf16[2,2,8,2,6,512]{5,2,3,4,1,0:T(8,128)(2,1)S(1)} all-to-all(bf16[2,2,8,2,6,512]{5,2,3,4,1,0:T(8,128)(2,1)S(1)} %copy.91), channel_id=1, replica_groups=mesh['dp'=8,'x'=4,'y'=4,'zh'=2,'core'=2] {'core'}, dimensions={0} | all-to-all | bytes 786432 | tf_op jit(solution)/shard_map/all_to_all | solution.py:351
  310.3 28.6 %all_to_all.26 = bf16[16,48,128]{2,1,0:T(8,128)(2,1)S(1)} all-to-all(bf16[16,48,128]{2,1,0:T(8,128)(2,1)S(1)} %reshape.755), channel_id=1, replica_groups=mesh['dp'=8,'x'=4,'y'=4,'zh'=2,'core'=2] {'zh','dp'}, dimensions={0} | all-to-all | bytes 393216 | tf_op jit(solution)/shard_map/all_to_all | solution.py:353
  (241 shorter events, 91.2 us)
Async XLA Ops:
  29.1 35.5 %all-to-all-start = ((bf16[16,16,4224]{2,1,0:T(8,128)(2,1)}), bf16[16,16,4224]{2,1,0:T(8,128)(2,1)S(1)}, u32[]{:S(2)}, u32[]{:S(2)}) async-start(bf16[16,16,4224]{2,1,0:T(8,128)(2,1)} %bitcast.7), calls=%async_computation | async-start | bytes 4325376 | tf_op jit(solution)/shard_map/all_to_all | solution.py:213
  66.4 25.9 %collective-permute-start.1 = (bf16[48,4224]{1,0:T(8,128)(2,1)S(1)}, bf16[48,4224]{1,0:T(8,128)(2,1)S(1)}, u32[]{:S(2)}, u32[]{:S(2)}) collective-permute-start(bf16[48,4224]{1,0:T(8,128)(2,1)S(1)} %pad_maximum_fusion.1.refs_2_), channel_id=1, source_target_pairs={{64,0},{128,64},{192,128},{256,192},{320,256},{384,320},{448,384},... | collective-permute-start | bytes 1216520 | tf_op jit(solution)/shard_map/ppermute | solution.py:263
  67.9 29.3 %collective-permute-start = (bf16[48,4224]{1,0:T(8,128)(2,1)S(1)}, bf16[48,4224]{1,0:T(8,128)(2,1)S(1)}, u32[]{:S(2)}, u32[]{:S(2)}) collective-permute-start(bf16[48,4224]{1,0:T(8,128)(2,1)S(1)} %pad_maximum_fusion.1.refs_2_), channel_id=1, source_target_pairs={{0,64},{64,128},{128,192},{192,256},{256,320},{320,384},{384,448},... | collective-permute-start | bytes 1216520 | tf_op jit(solution)/shard_map/ppermute | solution.py:262
  78.0 20.9 %collective-permute-start.5 = (bf16[48,4224]{1,0:T(8,128)(2,1)S(1)}, bf16[48,4224]{1,0:T(8,128)(2,1)S(1)}, u32[]{:S(2)}, u32[]{:S(2)}) collective-permute-start(bf16[48,4224]{1,0:T(8,128)(2,1)S(1)} %pad_maximum_fusion.2.refs_2_), channel_id=1, source_target_pairs={{64,0},{128,64},{192,128},{256,192},{320,256},{384,320},{448,384},... | collective-permute-start | bytes 1216520 | tf_op jit(solution)/shard_map/ppermute | solution.py:263
  79.3 19.6 %collective-permute-start.4 = (bf16[48,4224]{1,0:T(8,128)(2,1)S(1)}, bf16[48,4224]{1,0:T(8,128)(2,1)S(1)}, u32[]{:S(2)}, u32[]{:S(2)}) collective-permute-start(bf16[48,4224]{1,0:T(8,128)(2,1)S(1)} %pad_maximum_fusion.2.refs_2_), channel_id=1, source_target_pairs={{0,64},{64,128},{128,192},{192,256},{256,320},{320,384},{384,448},... | collective-permute-start | bytes 1216520 | tf_op jit(solution)/shard_map/ppermute | solution.py:262
  84.7 37.1 %collective-permute-start.2 = (bf16[48,4224]{1,0:T(8,128)(2,1)S(1)}, bf16[48,4224]{1,0:T(8,128)(2,1)S(1)}, u32[]{:S(2)}, u32[]{:S(2)}) collective-permute-start(bf16[48,4224]{1,0:T(8,128)(2,1)S(1)} %broadcast_select_fusion), channel_id=1, source_target_pairs={{0,384},{64,448},{384,0},{448,64},{1,385},{65,449},{385,1},{449,65... | collective-permute-start | bytes 1216520 | tf_op jit(solution)/shard_map/ppermute | solution.py:255
  92.3 29.6 %collective-permute-start.3 = (bf16[48,4224]{1,0:T(8,128)(2,1)S(1)}, bf16[48,4224]{1,0:T(8,128)(2,1)S(1)}, u32[]{:S(2)}, u32[]{:S(2)}) collective-permute-start(bf16[48,4224]{1,0:T(8,128)(2,1)S(1)} %broadcast_select_fusion), channel_id=1, source_target_pairs={{0,448},{448,0},{1,449},{449,1},{2,450},{450,2},{3,451},{451,3},{4... | collective-permute-start | bytes 1216520 | tf_op jit(solution)/shard_map/ppermute | solution.py:255
  128.3 67.1 %all-to-all-start.1 = ((bf16[16,32,4224]{2,1,0:T(8,128)(2,1)}), bf16[16,32,4224]{2,1,0:T(8,128)(2,1)}, u32[]{:S(2)}, u32[]{:S(2)}) async-start(bf16[16,32,4224]{2,1,0:T(8,128)(2,1)} %bitcast.127), calls=%async_computation.1 | async-start | bytes 8650752 | tf_op jit(solution)/shard_map/all_to_all | solution.py:213
  137.3 13.4 %collective-permute-start.6 = (bf16[48,4224]{1,0:T(8,128)(2,1)S(1)}, bf16[48,4224]{1,0:T(8,128)(2,1)}, u32[]{:S(2)}, u32[]{:S(2)}) collective-permute-start(bf16[48,4224]{1,0:T(8,128)(2,1)S(1)} %get-tuple-element.50), channel_id=1, source_target_pairs={{64,128},{128,192},{192,256},{256,320},{320,384},{384,448},{65,129... | collective-permute-start | bytes 1216520 | tf_op jit(solution)/shard_map/ppermute | solution.py:262
  138.7 16.4 %collective-permute-start.7 = (bf16[48,4224]{1,0:T(8,128)(2,1)S(1)}, bf16[48,4224]{1,0:T(8,128)(2,1)}, u32[]{:S(2)}, u32[]{:S(2)}) collective-permute-start(bf16[48,4224]{1,0:T(8,128)(2,1)S(1)} %get-tuple-element.51), channel_id=1, source_target_pairs={{64,0},{128,64},{192,128},{256,192},{320,256},{384,320},{65,1},{12... | collective-permute-start | bytes 1216520 | tf_op jit(solution)/shard_map/ppermute | solution.py:263
  148.7 13.3 %collective-permute-start.12 = (bf16[48,4224]{1,0:T(8,128)(2,1)}, bf16[48,4224]{1,0:T(8,128)(2,1)S(1)}, u32[]{:S(2)}, u32[]{:S(2)}) collective-permute-start(bf16[48,4224]{1,0:T(8,128)(2,1)} %get-tuple-element.57), channel_id=1, source_target_pairs={{128,192},{192,256},{256,320},{320,384},{384,448},{129,193},{193,2... | collective-permute-start | bytes 1216520 | tf_op jit(solution)/shard_map/ppermute | solution.py:262
  149.4 14.3 %collective-permute-start.13 = (bf16[48,4224]{1,0:T(8,128)(2,1)}, bf16[48,4224]{1,0:T(8,128)(2,1)}, u32[]{:S(2)}, u32[]{:S(2)}) collective-permute-start(bf16[48,4224]{1,0:T(8,128)(2,1)} %get-tuple-element.58), channel_id=1, source_target_pairs={{64,0},{128,64},{192,128},{256,192},{320,256},{65,1},{129,65},{193... | collective-permute-start | bytes 1216520 | tf_op jit(solution)/shard_map/ppermute | solution.py:263
  158.1 14.3 %collective-permute-start.11 = (bf16[48,4224]{1,0:T(8,128)(2,1)}, bf16[48,4224]{1,0:T(8,128)(2,1)}, u32[]{:S(2)}, u32[]{:S(2)}) collective-permute-start(bf16[48,4224]{1,0:T(8,128)(2,1)} %get-tuple-element.56), channel_id=1, source_target_pairs={{64,0},{128,64},{192,128},{256,192},{320,256},{65,1},{129,65},{193... | collective-permute-start | bytes 1216520 | tf_op jit(solution)/shard_map/ppermute | solution.py:263
  175.6 13.6 %collective-permute-start.15 = (bf16[48,4224]{1,0:T(8,128)(2,1)}, bf16[48,4224]{1,0:T(8,128)(2,1)}, u32[]{:S(2)}, u32[]{:S(2)}) collective-permute-start(bf16[48,4224]{1,0:T(8,128)(2,1)} %get-tuple-element.62), channel_id=1, source_target_pairs={{64,0},{128,64},{192,128},{256,192},{65,1},{129,65},{193,129},{257... | collective-permute-start | bytes 1216520 | tf_op jit(solution)/shard_map/ppermute | solution.py:263
  182.4 20.2 %collective-permute-start.18 = (bf16[48,4224]{1,0:T(8,128)(2,1)}, bf16[48,4224]{1,0:T(8,128)(2,1)S(1)}, u32[]{:S(2)}, u32[]{:S(2)}) collective-permute-start(bf16[48,4224]{1,0:T(8,128)(2,1)} %get-tuple-element.70), channel_id=1, source_target_pairs={{256,320},{320,384},{384,448},{257,321},{321,385},{385,449},{258,3... | collective-permute-start | bytes 1216520 | tf_op jit(solution)/shard_map/ppermute | solution.py:262
  183.1 19.5 %collective-permute-start.19 = (bf16[48,4224]{1,0:T(8,128)(2,1)}, bf16[48,4224]{1,0:T(8,128)(2,1)S(1)}, u32[]{:S(2)}, u32[]{:S(2)}) collective-permute-start(bf16[48,4224]{1,0:T(8,128)(2,1)} %get-tuple-element.71), channel_id=1, source_target_pairs={{64,0},{128,64},{192,128},{65,1},{129,65},{193,129},{66,2},{130,66... | collective-permute-start | bytes 1216520 | tf_op jit(solution)/shard_map/ppermute | solution.py:263
  225.9 13.1 %collective-permute-start.30 = (bf16[768,128]{1,0:T(8,128)(2,1)S(1)}, bf16[768,128]{1,0:T(8,128)(2,1)S(1)}, u32[]{:S(2)}, u32[]{:S(2)}) collective-permute-start(bf16[768,128]{1,0:T(8,128)(2,1)S(1)} %collective-permute-done.28.refs_7_), channel_id=1, source_target_pairs={{64,0},{128,64},{192,128},{256,192},{320,256},{65,1},{129,65},{193... | collective-permute-start | bytes 589832 | tf_op jit(solution)/shard_map/ppermute | solution.py:309
  227.2 13.1 %collective-permute-start.29 = (bf16[768,128]{1,0:T(8,128)(2,1)S(1)}, bf16[768,128]{1,0:T(8,128)(2,1)S(1)}, u32[]{:S(2)}, u32[]{:S(2)}) collective-permute-start(bf16[768,128]{1,0:T(8,128)(2,1)S(1)} %collective-permute-done.27.refs_6_), channel_id=1, source_target_pairs={{128,192},{192,256},{256,320},{320,384},{384,448},{129,193},{193,2... | collective-permute-start | bytes 589832 | tf_op jit(solution)/shard_map/ppermute | solution.py:308
  227.9 13.6 %collective-permute-start.24 = (bf16[768,128]{1,0:T(8,128)(2,1)S(1)}, bf16[768,128]{1,0:T(8,128)(2,1)S(1)}, u32[]{:S(2)}, u32[]{:S(2)}) collective-permute-start(bf16[768,128]{1,0:T(8,128)(2,1)S(1)} %shard_map.112.refs_0_), channel_id=1, source_target_pairs={{0,448},{448,0},{1,449},{449,1},{2,450},{450,2},{3,451},{451,3},{4... | collective-permute-start | bytes 589832 | tf_op jit(solution)/shard_map/ppermute | solution.py:305
  232.2 15.4 %collective-permute-start.23 = (bf16[768,128]{1,0:T(8,128)(2,1)S(1)}, bf16[768,128]{1,0:T(8,128)(2,1)S(1)}, u32[]{:S(2)}, u32[]{:S(2)}) collective-permute-start(bf16[768,128]{1,0:T(8,128)(2,1)S(1)} %shard_map.112.refs_0_), channel_id=1, source_target_pairs={{0,384},{64,448},{384,0},{448,64},{1,385},{65,449},{385,1},{449,65... | collective-permute-start | bytes 589832 | tf_op jit(solution)/shard_map/ppermute | solution.py:305
  237.0 21.1 %collective-permute-start.22 = (bf16[768,128]{1,0:T(8,128)(2,1)S(1)}, bf16[768,128]{1,0:T(8,128)(2,1)S(1)}, u32[]{:S(2)}, u32[]{:S(2)}) collective-permute-start(bf16[768,128]{1,0:T(8,128)(2,1)S(1)} %shard_map.112.refs_0_), channel_id=1, source_target_pairs={{0,320},{64,384},{128,448},{320,0},{384,64},{448,128},{1,321},{65,... | collective-permute-start | bytes 589832 | tf_op jit(solution)/shard_map/ppermute | solution.py:305
  239.0 19.1 %collective-permute-start.32 = (bf16[768,128]{1,0:T(8,128)(2,1)S(1)}, bf16[768,128]{1,0:T(8,128)(2,1)S(1)}, u32[]{:S(2)}, u32[]{:S(2)}) collective-permute-start(bf16[768,128]{1,0:T(8,128)(2,1)S(1)} %collective-permute-done.30.refs_9_), channel_id=1, source_target_pairs={{64,0},{128,64},{192,128},{256,192},{65,1},{129,65},{193,129},{257... | collective-permute-start | bytes 589832 | tf_op jit(solution)/shard_map/ppermute | solution.py:309
  240.3 17.8 %collective-permute-start.31 = (bf16[768,128]{1,0:T(8,128)(2,1)S(1)}, bf16[768,128]{1,0:T(8,128)(2,1)S(1)}, u32[]{:S(2)}, u32[]{:S(2)}) collective-permute-start(bf16[768,128]{1,0:T(8,128)(2,1)S(1)} %collective-permute-done.29.refs_8_), channel_id=1, source_target_pairs={{192,256},{256,320},{320,384},{384,448},{193,257},{257,321},{321,3... | collective-permute-start | bytes 589832 | tf_op jit(solution)/shard_map/ppermute | solution.py:308
  262.4 24.9 %all-to-all-start.2 = ((bf16[16,16,8,512]{3,2,1,0:T(8,128)(2,1)}), bf16[16,16,8,512]{3,2,1,0:T(8,128)(2,1)S(1)}, u32[]{:S(2)}, u32[]{:S(2)}) async-start(bf16[16,16,8,512]{3,2,1,0:T(8,128)(2,1)} %bitcast.128), calls=%async_computation.2 | async-start | bytes 4194304 | tf_op jit(solution)/shard_map/all_to_all | solution.py:325
  (47 other events, 404.8 us)

commit v7 on v6

--- a/solution.py
+++ b/solution.py
@@ -13,7 +13,7 @@
 ROWS = 48
 MOST = 2
 STEPS = 5
-NEAR = 4
+NEAR = 5
 HOME, HI, MID, ONE, POS = 0, 8, 16, 32, 33
 
 
@@ -263,8 +263,7 @@
             to_left[s] = lax.ppermute(to_left[s], "dp", left[j - 1])
             blocks = [to_right[s], to_left[s]] + ([own[s]] if j == 1 else [])
             passed = 2 if j < STEPS else 0
-            extra = [late[0]] if j == STEPS and s == 0 else []
-            extra += [made[0]] if (j, s) != (1, 0) else []
+            extra = [made[0]] if (j, s) != (1, 0) else []
             sent, made = project(both_w, blocks, passed, extra)
             if passed:
                 to_right[s], to_left[s] = sent
@@ -272,11 +271,11 @@
             done[s][n_dp - j].append((made[1], 0, last))
             if j == 1:
                 done[s][0].append((made[2], 0, last))
-            if (j, s) == (1, steps - 1):
+            if (j, s) == (2, steps - 1):
                 received_far = exchange(
                     distant, len(beyond) * steps, made[0][0, 0] == made[0][0, 0]
                 )
-        if j == STEPS - 1:
+        if j == STEPS:
             ready = made[0][0, 0] == made[0][0, 0]
             late = project(
                 both_w,

time: 344 us -> 350 us (1.017)
  waiting for transfers between devices: 111 us -> 120 us
  blocking collectives: 72.2 us -> 64.9 us
  starting transfers between devices: 88.3 us -> 94 us
    ppermute x10, waiting for transfers between devices: 24 us -> 38.4 us  [on_device(): to_left[s] = lax.ppermute(to_left[s], 'dp', left[j - 1])]
    all_to_all x1, blocking collectives: 22 us -> 14.3 us  [on_device(): lax.all_to_all(partial, 'core', split_axis=0, concat_axis=0, tiled=True)]
    ppermute x3 -> x2, waiting for transfers between devices: 16.6 us -> 12.1 us  [on_device(): shards.append(lax.ppermute(hidden, 'dp', apart[k]))]
    all_to_all x1, starting transfers between devices: 6.6 us -> 10.3 us  [on_device(): lax.all_to_all(spread.reshape(batch, columns, quad * MOST, width).transpo...]
    ppermute x4 -> x5, starting transfers between devices: 6.01 us -> 8.27 us  [on_device(): going_right = lax.ppermute(going_right, 'dp', right[j - 1])]
    ppermute x4 -> x5, waiting for transfers between devices: 10.8 us -> 9.89 us  [on_device(): going_left = lax.ppermute(going_left, 'dp', left[j - 1])]
    ppermute x3 -> x2, starting transfers between devices: 11.1 us -> 10.4 us  [on_device(): shards.append(lax.ppermute(hidden, 'dp', apart[k]))]
  transfers between devices with their start and end apart: 36 -> 37, of which waited for: 15 -> 16; matrix products, arithmetic and copies ran while one was open for 5% -> 4% of each run, Pallas kernels for 4% -> 3%
where the time goes in v7:
time: 350 us; the launch traced here: 346 us
  waiting for transfers between devices  120 us (34%)
  starting transfers between devices  94 us (27%)
  blocking collectives  64.9 us (19%)
  local copies, waits for them, and re-layouts  21.5 us (6%)
  Pallas kernels  15.1 us (4%)
  matrix products  13.4 us (4%)
  between operations  8.9 us (3%)
  other arithmetic  8.11 us (2%)
    ppermute x10, waiting for transfers between devices, on_device(): to_left[s] = lax.ppermute(to_left[s], 'dp', left[j - 1])  38.4 us
    all_to_all x1, blocking collectives, on_device(): lax.all_to_all(halves.reshape(2 * n_dp, mine * width // LANES, LANES), ('...  28.9 us
    all_to_all x2, waiting for transfers between devices, exchange(): lax.all_to_all(send.reshape(columns, sets * quad * MOST, wide), ('x', 'y'...  26.2 us
    all_gather x1, blocking collectives, on_device(): lax.all_gather(packed.reshape(steps, tok, wide), ('zh', 'core'), axis=1,...  21.7 us
    ppermute x10, starting transfers between devices, on_device(): to_right[s] = lax.ppermute(to_right[s], 'dp', right[j - 1])  20.6 us
    ppermute x2, waiting for transfers between devices, on_device(): lax.ppermute(leaving, 'dp', apart[k])  18.6 us
    all_to_all x1, waiting for transfers between devices, on_device(): lax.all_to_all(spread.reshape(batch, columns, quad * MOST, width).transpo...  14.7 us
    all_to_all x1, blocking collectives, on_device(): lax.all_to_all(partial, 'core', split_axis=0, concat_axis=0, tiled=True)  14.3 us
  transfers between devices with their start and end apart: 37, of which 16 were waited for; matrix products, arithmetic and copies ran while one was open for 4% of the time, Pallas kernels for 3%

profile of v7, /device:TPU:1, one launch (start us, length us, event | category | flops | bytes accessed | tf_op | source)
XLA Modules:
  0.0 346.0 jit_solution(359441157613394685)
XLA Ops:
  4.8 21.7 %all_gather.3 = bf16[2,24,4224]{2,0,1:T(2,128)(2,1)S(1)} all-gather(bf16[2,6,4224]{2,0,1:T(2,128)(2,1)S(1)} %pad_maximum_fusion.7), channel_id=1, replica_groups=mesh['dp'=8,'x'=4,'y'=4,'zh'=2,'core'=2] {'zh','core'}, dimensions={1}, use_global_device_ids=true | all-gather | bytes 506880 | tf_op jit(solution)/shard_map/all_gather | solution.py:197
  29.1 5.7 %all-to-all-start = ((bf16[16,16,4224]{2,1,0:T(8,128)(2,1)}), bf16[16,16,4224]{2,1,0:T(8,128)(2,1)S(1)}, u32[]{:S(2)}, u32[]{:S(2)}) async-start(bf16[16,16,4224]{2,1,0:T(8,128)(2,1)} %bitcast.7), calls=%async_computation | async-start | bytes 4325376 | tf_op jit(solution)/shard_map/all_to_all | solution.py:213
  38.4 26.2 %all-to-all-done = bf16[16,16,4224]{2,1,0:T(8,128)(2,1)S(1)} async-done(((bf16[16,16,4224]{2,1,0:T(8,128)(2,1)}), bf16[16,16,4224]{2,1,0:T(8,128)(2,1)S(1)}, u32[]{:S(2)}, u32[]{:S(2)}) %all-to-all-start) | async-done | bytes 2162720 | tf_op jit(solution)/shard_map/all_to_all | solution.py:213
  67.9 9.6 %collective-permute-start = (bf16[48,4224]{1,0:T(8,128)(2,1)S(1)}, bf16[48,4224]{1,0:T(8,128)(2,1)S(1)}, u32[]{:S(2)}, u32[]{:S(2)}) collective-permute-start(bf16[48,4224]{1,0:T(8,128)(2,1)S(1)} %pad_maximum_fusion.1.refs_2_), channel_id=1, source_target_pairs={{0,64},{64,128},{128,192},{192,256},{256,320},{320,384},{384,448},... | collective-permute-start | bytes 1216520 | tf_op jit(solution)/shard_map/ppermute | solution.py:262
  79.3 4.0 %collective-permute-start.4 = (bf16[48,4224]{1,0:T(8,128)(2,1)S(1)}, bf16[48,4224]{1,0:T(8,128)(2,1)S(1)}, u32[]{:S(2)}, u32[]{:S(2)}) collective-permute-start(bf16[48,4224]{1,0:T(8,128)(2,1)S(1)} %pad_maximum_fusion.2.refs_2_), channel_id=1, source_target_pairs={{0,64},{64,128},{128,192},{192,256},{256,320},{320,384},{384,448},... | collective-permute-start | bytes 1216520 | tf_op jit(solution)/shard_map/ppermute | solution.py:262
  84.7 7.3 %collective-permute-start.2 = (bf16[48,4224]{1,0:T(8,128)(2,1)S(1)}, bf16[48,4224]{1,0:T(8,128)(2,1)S(1)}, u32[]{:S(2)}, u32[]{:S(2)}) collective-permute-start(bf16[48,4224]{1,0:T(8,128)(2,1)S(1)} %broadcast_select_fusion), channel_id=1, source_target_pairs={{0,384},{64,448},{384,0},{448,64},{1,385},{65,449},{385,1},{449,65... | collective-permute-start | bytes 1216520 | tf_op jit(solution)/shard_map/ppermute | solution.py:255
  92.3 4.8 %collective-permute-start.3 = (bf16[48,4224]{1,0:T(8,128)(2,1)S(1)}, bf16[48,4224]{1,0:T(8,128)(2,1)S(1)}, u32[]{:S(2)}, u32[]{:S(2)}) collective-permute-start(bf16[48,4224]{1,0:T(8,128)(2,1)S(1)} %broadcast_select_fusion), channel_id=1, source_target_pairs={{0,448},{448,0},{1,449},{449,1},{2,450},{450,2},{3,451},{451,3},{4... | collective-permute-start | bytes 1216520 | tf_op jit(solution)/shard_map/ppermute | solution.py:255
  103.3 18.6 %collective-permute-done.2 = bf16[48,4224]{1,0:T(8,128)(2,1)S(1)} collective-permute-done((bf16[48,4224]{1,0:T(8,128)(2,1)S(1)}, bf16[48,4224]{1,0:T(8,128)(2,1)S(1)}, u32[]{:S(2)}, u32[]{:S(2)}) %collective-permute-start.2) | collective-permute-done | bytes 405536 | tf_op jit(solution)/shard_map/ppermute | solution.py:255
  128.0 5.5 %collective-permute-done.7.refs_1_ = bf16[48,4224]{1,0:T(8,128)(2,1)S(1)} collective-permute-done((bf16[48,4224]{1,0:T(8,128)(2,1)S(1)}, bf16[48,4224]{1,0:T(8,128)(2,1)S(1)}, u32[]{:S(2)}, u32[]{:S(2)}) %collective-permute-start.7) | collective-permute-done | bytes 405536 | tf_op jit(solution)/shard_map/ppermute | solution.py:263
  137.1 5.0 %convolution_convert_fusion = bf16[512,4224]{1,0:T(8,128)(2,1)} fusion(bf16[96,4224]{1,0:T(8,128)(2,1)} %constant_dynamic-update-slice_fusion, f32[512]{0:T(512)S(1)} %fusion.188, s32[512]{0:T(512)S(1)} %get-tuple-element.183, s32[96]{0:T(128)S(1)} %get-tuple-element.185, pred[]{:T(512)} %bitcast.17, bf16[512]{0:T(512)(128)(2,1)S(1)} %get-tuple-element.184, ...), kind=kOutput, calls=%fused_computation | convolution fusion | flops 430255104 | bytes 5143809 | tf_op jit(solution)/shard_map/dot_general | solution.py:210
  142.1 7.0 %all-to-all-start.1 = ((bf16[16,32,4224]{2,1,0:T(8,128)(2,1)}), bf16[16,32,4224]{2,1,0:T(8,128)(2,1)}, u32[]{:S(2)}, u32[]{:S(2)}) async-start(bf16[16,32,4224]{2,1,0:T(8,128)(2,1)} %bitcast.127), calls=%async_computation.1 | async-start | bytes 8650752 | tf_op jit(solution)/shard_map/all_to_all | solution.py:213
  154.6 12.0 %collective-permute-done.13.refs_1_ = bf16[48,4224]{1,0:T(8,128)(2,1)} collective-permute-done((bf16[48,4224]{1,0:T(8,128)(2,1)S(1)}, bf16[48,4224]{1,0:T(8,128)(2,1)}, u32[]{:S(2)}, u32[]{:S(2)}) %collective-permute-start.13) | collective-permute-done | bytes 405536 | tf_op jit(solution)/shard_map/ppermute | solution.py:263
  170.9 4.5 %collective-permute-done.11.refs_1_ = bf16[48,4224]{1,0:T(8,128)(2,1)} collective-permute-done((bf16[48,4224]{1,0:T(8,128)(2,1)}, bf16[48,4224]{1,0:T(8,128)(2,1)}, u32[]{:S(2)}, u32[]{:S(2)}) %collective-permute-start.11) | collective-permute-done | bytes 405536 | tf_op jit(solution)/shard_map/ppermute | solution.py:263
  187.4 4.4 %collective-permute-done.15.refs_1_ = bf16[48,4224]{1,0:T(8,128)(2,1)S(1)} collective-permute-done((bf16[48,4224]{1,0:T(8,128)(2,1)}, bf16[48,4224]{1,0:T(8,128)(2,1)S(1)}, u32[]{:S(2)}, u32[]{:S(2)}) %collective-permute-start.15) | collective-permute-done | bytes 405536 | tf_op jit(solution)/shard_map/ppermute | solution.py:263
  201.3 7.7 %collective-permute-done.19.refs_1_ = bf16[48,4224]{1,0:T(8,128)(2,1)S(1)} collective-permute-done((bf16[48,4224]{1,0:T(8,128)(2,1)S(1)}, bf16[48,4224]{1,0:T(8,128)(2,1)S(1)}, u32[]{:S(2)}, u32[]{:S(2)}) %collective-permute-start.19) | collective-permute-done | bytes 405536 | tf_op jit(solution)/shard_map/ppermute | solution.py:263
  220.5 5.6 %collective-permute-start.24 = (bf16[768,128]{1,0:T(8,128)(2,1)S(1)}, bf16[768,128]{1,0:T(8,128)(2,1)S(1)}, u32[]{:S(2)}, u32[]{:S(2)}) collective-permute-start(bf16[768,128]{1,0:T(8,128)(2,1)S(1)} %shard_map.112.refs_0_), channel_id=1, source_target_pairs={{0,64},{64,128},{128,192},{192,256},{256,320},{320,384},{384,448},... | collective-permute-start | bytes 589832 | tf_op jit(solution)/shard_map/ppermute | solution.py:307
  229.3 4.3 %collective-permute-done.27.refs_6_ = bf16[768,128]{1,0:T(8,128)(2,1)S(1)} collective-permute-done((bf16[768,128]{1,0:T(8,128)(2,1)S(1)}, bf16[768,128]{1,0:T(8,128)(2,1)S(1)}, u32[]{:S(2)}, u32[]{:S(2)}) %collective-permute-start.27) | collective-permute-done | bytes 196640 | tf_op jit(solution)/shard_map/ppermute | solution.py:308
  235.6 4.5 %collective-permute-done.29.refs_8_ = bf16[768,128]{1,0:T(8,128)(2,1)S(1)} collective-permute-done((bf16[768,128]{1,0:T(8,128)(2,1)S(1)}, bf16[768,128]{1,0:T(8,128)(2,1)S(1)}, u32[]{:S(2)}, u32[]{:S(2)}) %collective-permute-start.29) | collective-permute-done | bytes 196640 | tf_op jit(solution)/shard_map/ppermute | solution.py:308
  242.1 8.4 %collective-permute-start.23 = (bf16[768,128]{1,0:T(8,128)(2,1)S(1)}, bf16[768,128]{1,0:T(8,128)(2,1)S(1)}, u32[]{:S(2)}, u32[]{:S(2)}) collective-permute-start(bf16[768,128]{1,0:T(8,128)(2,1)S(1)} %shard_map.112.refs_0_), channel_id=1, source_target_pairs={{0,448},{448,0},{1,449},{449,1},{2,450},{450,2},{3,451},{451,3},{4... | collective-permute-start | bytes 589832 | tf_op jit(solution)/shard_map/ppermute | solution.py:304
  255.3 11.8 %collective-permute-done.22.refs_1_ = bf16[768,128]{1,0:T(8,128)(2,1)S(1)} collective-permute-done((bf16[768,128]{1,0:T(8,128)(2,1)S(1)}, bf16[768,128]{1,0:T(8,128)(2,1)S(1)}, u32[]{:S(2)}, u32[]{:S(2)}) %collective-permute-start.22) | collective-permute-done | bytes 196640 | tf_op jit(solution)/shard_map/ppermute | solution.py:304
  271.6 10.3 %all-to-all-start.2 = ((bf16[16,16,8,512]{3,2,1,0:T(8,128)(2,1)}), bf16[16,16,8,512]{3,2,1,0:T(8,128)(2,1)S(1)}, u32[]{:S(2)}, u32[]{:S(2)}) async-start(bf16[16,16,8,512]{3,2,1,0:T(8,128)(2,1)} %bitcast.128), calls=%async_computation.2 | async-start | bytes 4194304 | tf_op jit(solution)/shard_map/all_to_all | solution.py:324
  286.0 14.7 %all-to-all-done.2 = bf16[16,16,8,512]{3,2,1,0:T(8,128)(2,1)S(1)} async-done(((bf16[16,16,8,512]{3,2,1,0:T(8,128)(2,1)}), bf16[16,16,8,512]{3,2,1,0:T(8,128)(2,1)S(1)}, u32[]{:S(2)}, u32[]{:S(2)}) %all-to-all-start.2) | async-done | bytes 2097184 | tf_op jit(solution)/shard_map/all_to_all | solution.py:324
  301.3 14.3 %all_to_all.25 = bf16[2,2,8,2,6,512]{5,2,3,4,1,0:T(8,128)(2,1)S(1)} all-to-all(bf16[2,2,8,2,6,512]{5,2,3,4,1,0:T(8,128)(2,1)S(1)} %copy.91), channel_id=1, replica_groups=mesh['dp'=8,'x'=4,'y'=4,'zh'=2,'core'=2] {'core'}, dimensions={0} | all-to-all | bytes 786432 | tf_op jit(solution)/shard_map/all_to_all | solution.py:350
  316.0 28.9 %all_to_all.26 = bf16[16,48,128]{2,1,0:T(8,128)(2,1)S(1)} all-to-all(bf16[16,48,128]{2,1,0:T(8,128)(2,1)S(1)} %reshape.755), channel_id=1, replica_groups=mesh['dp'=8,'x'=4,'y'=4,'zh'=2,'core'=2] {'zh','dp'}, dimensions={0} | all-to-all | bytes 393216 | tf_op jit(solution)/shard_map/all_to_all | solution.py:352
  (237 shorter events, 90.4 us)
Async XLA Ops:
  29.1 35.5 %all-to-all-start = ((bf16[16,16,4224]{2,1,0:T(8,128)(2,1)}), bf16[16,16,4224]{2,1,0:T(8,128)(2,1)S(1)}, u32[]{:S(2)}, u32[]{:S(2)}) async-start(bf16[16,16,4224]{2,1,0:T(8,128)(2,1)} %bitcast.7), calls=%async_computation | async-start | bytes 4325376 | tf_op jit(solution)/shard_map/all_to_all | solution.py:213
  66.4 25.8 %collective-permute-start.1 = (bf16[48,4224]{1,0:T(8,128)(2,1)S(1)}, bf16[48,4224]{1,0:T(8,128)(2,1)S(1)}, u32[]{:S(2)}, u32[]{:S(2)}) collective-permute-start(bf16[48,4224]{1,0:T(8,128)(2,1)S(1)} %pad_maximum_fusion.1.refs_2_), channel_id=1, source_target_pairs={{64,0},{128,64},{192,128},{256,192},{320,256},{384,320},{448,384},... | collective-permute-start | bytes 1216520 | tf_op jit(solution)/shard_map/ppermute | solution.py:263
  67.9 29.3 %collective-permute-start = (bf16[48,4224]{1,0:T(8,128)(2,1)S(1)}, bf16[48,4224]{1,0:T(8,128)(2,1)S(1)}, u32[]{:S(2)}, u32[]{:S(2)}) collective-permute-start(bf16[48,4224]{1,0:T(8,128)(2,1)S(1)} %pad_maximum_fusion.1.refs_2_), channel_id=1, source_target_pairs={{0,64},{64,128},{128,192},{192,256},{256,320},{320,384},{384,448},... | collective-permute-start | bytes 1216520 | tf_op jit(solution)/shard_map/ppermute | solution.py:262
  78.0 21.5 %collective-permute-start.5 = (bf16[48,4224]{1,0:T(8,128)(2,1)S(1)}, bf16[48,4224]{1,0:T(8,128)(2,1)S(1)}, u32[]{:S(2)}, u32[]{:S(2)}) collective-permute-start(bf16[48,4224]{1,0:T(8,128)(2,1)S(1)} %pad_maximum_fusion.2.refs_2_), channel_id=1, source_target_pairs={{64,0},{128,64},{192,128},{256,192},{320,256},{384,320},{448,384},... | collective-permute-start | bytes 1216520 | tf_op jit(solution)/shard_map/ppermute | solution.py:263
  79.3 21.6 %collective-permute-start.4 = (bf16[48,4224]{1,0:T(8,128)(2,1)S(1)}, bf16[48,4224]{1,0:T(8,128)(2,1)S(1)}, u32[]{:S(2)}, u32[]{:S(2)}) collective-permute-start(bf16[48,4224]{1,0:T(8,128)(2,1)S(1)} %pad_maximum_fusion.2.refs_2_), channel_id=1, source_target_pairs={{0,64},{64,128},{128,192},{192,256},{256,320},{320,384},{384,448},... | collective-permute-start | bytes 1216520 | tf_op jit(solution)/shard_map/ppermute | solution.py:262
  84.7 37.2 %collective-permute-start.2 = (bf16[48,4224]{1,0:T(8,128)(2,1)S(1)}, bf16[48,4224]{1,0:T(8,128)(2,1)S(1)}, u32[]{:S(2)}, u32[]{:S(2)}) collective-permute-start(bf16[48,4224]{1,0:T(8,128)(2,1)S(1)} %broadcast_select_fusion), channel_id=1, source_target_pairs={{0,384},{64,448},{384,0},{448,64},{1,385},{65,449},{385,1},{449,65... | collective-permute-start | bytes 1216520 | tf_op jit(solution)/shard_map/ppermute | solution.py:255
  92.3 31.7 %collective-permute-start.3 = (bf16[48,4224]{1,0:T(8,128)(2,1)S(1)}, bf16[48,4224]{1,0:T(8,128)(2,1)S(1)}, u32[]{:S(2)}, u32[]{:S(2)}) collective-permute-start(bf16[48,4224]{1,0:T(8,128)(2,1)S(1)} %broadcast_select_fusion), channel_id=1, source_target_pairs={{0,448},{448,0},{1,449},{449,1},{2,450},{450,2},{3,451},{451,3},{4... | collective-permute-start | bytes 1216520 | tf_op jit(solution)/shard_map/ppermute | solution.py:255
  98.9 27.6 %collective-permute-start.8 = (bf16[48,4224]{1,0:T(8,128)(2,1)S(1)}, bf16[48,4224]{1,0:T(8,128)(2,1)S(1)}, u32[]{:S(2)}, u32[]{:S(2)}) collective-permute-start(bf16[48,4224]{1,0:T(8,128)(2,1)S(1)} %get-tuple-element.51), channel_id=1, source_target_pairs={{64,128},{128,192},{192,256},{256,320},{320,384},{384,448},{65,129... | collective-permute-start | bytes 1216520 | tf_op jit(solution)/shard_map/ppermute | solution.py:262
  99.6 26.9 %collective-permute-start.9 = (bf16[48,4224]{1,0:T(8,128)(2,1)S(1)}, bf16[48,4224]{1,0:T(8,128)(2,1)S(1)}, u32[]{:S(2)}, u32[]{:S(2)}) collective-permute-start(bf16[48,4224]{1,0:T(8,128)(2,1)S(1)} %get-tuple-element.52), channel_id=1, source_target_pairs={{64,0},{128,64},{192,128},{256,192},{320,256},{384,320},{65,1},{12... | collective-permute-start | bytes 1216520 | tf_op jit(solution)/shard_map/ppermute | solution.py:263
  102.6 25.4 %collective-permute-start.6 = (bf16[48,4224]{1,0:T(8,128)(2,1)S(1)}, bf16[48,4224]{1,0:T(8,128)(2,1)S(1)}, u32[]{:S(2)}, u32[]{:S(2)}) collective-permute-start(bf16[48,4224]{1,0:T(8,128)(2,1)S(1)} %get-tuple-element.49), channel_id=1, source_target_pairs={{64,128},{128,192},{192,256},{256,320},{320,384},{384,448},{65,129... | collective-permute-start | bytes 1216520 | tf_op jit(solution)/shard_map/ppermute | solution.py:262
  142.1 69.4 %all-to-all-start.1 = ((bf16[16,32,4224]{2,1,0:T(8,128)(2,1)}), bf16[16,32,4224]{2,1,0:T(8,128)(2,1)}, u32[]{:S(2)}, u32[]{:S(2)}) async-start(bf16[16,32,4224]{2,1,0:T(8,128)(2,1)} %bitcast.127), calls=%async_computation.1 | async-start | bytes 8650752 | tf_op jit(solution)/shard_map/all_to_all | solution.py:213
  150.6 16.1 %collective-permute-start.13 = (bf16[48,4224]{1,0:T(8,128)(2,1)S(1)}, bf16[48,4224]{1,0:T(8,128)(2,1)}, u32[]{:S(2)}, u32[]{:S(2)}) collective-permute-start(bf16[48,4224]{1,0:T(8,128)(2,1)S(1)} %get-tuple-element.59), channel_id=1, source_target_pairs={{64,0},{128,64},{192,128},{256,192},{320,256},{65,1},{129,65},{193... | collective-permute-start | bytes 1216520 | tf_op jit(solution)/shard_map/ppermute | solution.py:263
  151.9 19.0 %collective-permute-start.10 = (bf16[48,4224]{1,0:T(8,128)(2,1)S(1)}, bf16[48,4224]{1,0:T(8,128)(2,1)}, u32[]{:S(2)}, u32[]{:S(2)}) collective-permute-start(bf16[48,4224]{1,0:T(8,128)(2,1)S(1)} %get-tuple-element.56), channel_id=1, source_target_pairs={{128,192},{192,256},{256,320},{320,384},{384,448},{129,193},{193,2... | collective-permute-start | bytes 1216520 | tf_op jit(solution)/shard_map/ppermute | solution.py:262
  153.3 22.0 %collective-permute-start.11 = (bf16[48,4224]{1,0:T(8,128)(2,1)}, bf16[48,4224]{1,0:T(8,128)(2,1)}, u32[]{:S(2)}, u32[]{:S(2)}) collective-permute-start(bf16[48,4224]{1,0:T(8,128)(2,1)} %copy-done.1), channel_id=1, source_target_pairs={{64,0},{128,64},{192,128},{256,192},{320,256},{65,1},{129,65},{193... | collective-permute-start | bytes 1216520 | tf_op jit(solution)/shard_map/ppermute | solution.py:263
  168.9 13.3 %collective-permute-start.16 = (bf16[48,4224]{1,0:T(8,128)(2,1)}, bf16[48,4224]{1,0:T(8,128)(2,1)S(1)}, u32[]{:S(2)}, u32[]{:S(2)}) collective-permute-start(bf16[48,4224]{1,0:T(8,128)(2,1)} %get-tuple-element.63), channel_id=1, source_target_pairs={{192,256},{256,320},{320,384},{384,448},{193,257},{257,321},{321,3... | collective-permute-start | bytes 1216520 | tf_op jit(solution)/shard_map/ppermute | solution.py:262
  169.6 13.5 %collective-permute-start.17 = (bf16[48,4224]{1,0:T(8,128)(2,1)}, bf16[48,4224]{1,0:T(8,128)(2,1)}, u32[]{:S(2)}, u32[]{:S(2)}) collective-permute-start(bf16[48,4224]{1,0:T(8,128)(2,1)} %get-tuple-element.64), channel_id=1, source_target_pairs={{64,0},{128,64},{192,128},{256,192},{65,1},{129,65},{193,129},{257... | collective-permute-start | bytes 1216520 | tf_op jit(solution)/shard_map/ppermute | solution.py:263
  178.3 13.5 %collective-permute-start.15 = (bf16[48,4224]{1,0:T(8,128)(2,1)}, bf16[48,4224]{1,0:T(8,128)(2,1)S(1)}, u32[]{:S(2)}, u32[]{:S(2)}) collective-permute-start(bf16[48,4224]{1,0:T(8,128)(2,1)} %get-tuple-element.62), channel_id=1, source_target_pairs={{64,0},{128,64},{192,128},{256,192},{65,1},{129,65},{193,129},{257... | collective-permute-start | bytes 1216520 | tf_op jit(solution)/shard_map/ppermute | solution.py:263
  186.1 14.2 %collective-permute-start.21 = (bf16[48,4224]{1,0:T(8,128)(2,1)}, bf16[48,4224]{1,0:T(8,128)(2,1)S(1)}, u32[]{:S(2)}, u32[]{:S(2)}) collective-permute-start(bf16[48,4224]{1,0:T(8,128)(2,1)} %get-tuple-element.70), channel_id=1, source_target_pairs={{64,0},{128,64},{192,128},{65,1},{129,65},{193,129},{66,2},{130,66... | collective-permute-start | bytes 1216520 | tf_op jit(solution)/shard_map/ppermute | solution.py:263
  193.4 15.5 %collective-permute-start.19 = (bf16[48,4224]{1,0:T(8,128)(2,1)S(1)}, bf16[48,4224]{1,0:T(8,128)(2,1)S(1)}, u32[]{:S(2)}, u32[]{:S(2)}) collective-permute-start(bf16[48,4224]{1,0:T(8,128)(2,1)S(1)} %get-tuple-element.68), channel_id=1, source_target_pairs={{64,0},{128,64},{192,128},{65,1},{129,65},{193,129},{66,2},{130,66... | collective-permute-start | bytes 1216520 | tf_op jit(solution)/shard_map/ppermute | solution.py:263
  242.1 13.2 %collective-permute-start.23 = (bf16[768,128]{1,0:T(8,128)(2,1)S(1)}, bf16[768,128]{1,0:T(8,128)(2,1)S(1)}, u32[]{:S(2)}, u32[]{:S(2)}) collective-permute-start(bf16[768,128]{1,0:T(8,128)(2,1)S(1)} %shard_map.112.refs_0_), channel_id=1, source_target_pairs={{0,448},{448,0},{1,449},{449,1},{2,450},{450,2},{3,451},{451,3},{4... | collective-permute-start | bytes 589832 | tf_op jit(solution)/shard_map/ppermute | solution.py:304
  250.5 16.6 %collective-permute-start.22 = (bf16[768,128]{1,0:T(8,128)(2,1)S(1)}, bf16[768,128]{1,0:T(8,128)(2,1)S(1)}, u32[]{:S(2)}, u32[]{:S(2)}) collective-permute-start(bf16[768,128]{1,0:T(8,128)(2,1)S(1)} %shard_map.112.refs_0_), channel_id=1, source_target_pairs={{0,384},{64,448},{384,0},{448,64},{1,385},{65,449},{385,1},{449,65... | collective-permute-start | bytes 589832 | tf_op jit(solution)/shard_map/ppermute | solution.py:304
  252.4 14.7 %collective-permute-start.33 = (bf16[768,128]{1,0:T(8,128)(2,1)S(1)}, bf16[768,128]{1,0:T(8,128)(2,1)S(1)}, u32[]{:S(2)}, u32[]{:S(2)}) collective-permute-start(bf16[768,128]{1,0:T(8,128)(2,1)S(1)} %collective-permute-done.31.refs_10_), channel_id=1, source_target_pairs={{64,0},{128,64},{192,128},{65,1},{129,65},{193,129},{66,2},{130,66... | collective-permute-start | bytes 589832 | tf_op jit(solution)/shard_map/ppermute | solution.py:308
  253.8 13.3 %collective-permute-start.32 = (bf16[768,128]{1,0:T(8,128)(2,1)S(1)}, bf16[768,128]{1,0:T(8,128)(2,1)S(1)}, u32[]{:S(2)}, u32[]{:S(2)}) collective-permute-start(bf16[768,128]{1,0:T(8,128)(2,1)S(1)} %collective-permute-done.30.refs_9_), channel_id=1, source_target_pairs={{256,320},{320,384},{384,448},{257,321},{321,385},{385,449},{258,3... | collective-permute-start | bytes 589832 | tf_op jit(solution)/shard_map/ppermute | solution.py:307
  271.6 29.0 %all-to-all-start.2 = ((bf16[16,16,8,512]{3,2,1,0:T(8,128)(2,1)}), bf16[16,16,8,512]{3,2,1,0:T(8,128)(2,1)S(1)}, u32[]{:S(2)}, u32[]{:S(2)}) async-start(bf16[16,16,8,512]{3,2,1,0:T(8,128)(2,1)} %bitcast.128), calls=%async_computation.2 | async-start | bytes 4194304 | tf_op jit(solution)/shard_map/all_to_all | solution.py:324
  (45 other events, 362.2 us)

commit v8 on v7

--- a/solution.py
+++ b/solution.py
@@ -12,8 +12,6 @@
 LANES = 128
 ROWS = 48
 MOST = 2
-STEPS = 5
-NEAR = 5
 HOME, HI, MID, ONE, POS = 0, 8, 16, 32, 33
 
 
@@ -203,26 +201,25 @@
     line = jnp.arange(boxes, dtype=jnp.int32)
     lower = (line[:, None] < line[None, :]).astype(BF)
 
-    def exchange(local, sets, after=None):
-        place = places(local[:, model:], me, columns, quad, tok, top, sets)[1]
+    def exchange(local, after=None):
+        place = places(local[:, model:], me, columns, quad, tok, top)[1]
         if after is not None:
             place = place & after
         send = lax.dot_general(
             place.astype(BF), local, (((0,), (0,)), ((), ())), preferred_element_type=F32
         ).astype(BF)
         return lax.all_to_all(
-            send.reshape(columns, sets * quad * MOST, wide),
+            send.reshape(columns, quad * MOST, wide),
             ("x", "y"),
             split_axis=0,
             concat_axis=0,
             tiled=True,
-        )
-
-    def compacted(received, index, local, step, dp, after=None):
-        arrived = received[:, index * quad * MOST : (index + 1) * quad * MOST].reshape(boxes, wide)
+        ).reshape(boxes, wide)
+
+    def compacted(arrived, local, step, after=None):
         valid = arrived[:, model + ONE]
         rank = jnp.dot(valid[None, :], lower, preferred_element_type=F32)
-        which = (jnp.arange(n_dp, dtype=jnp.int32)[:, None] == dp) & (
+        which = (jnp.arange(n_dp, dtype=jnp.int32)[:, None] == my_dp) & (
             labels[None, :] == owners[step]
         )
         limit = jnp.sum(jnp.where(which, slot_rows[step], 0)).astype(F32)
@@ -240,112 +237,81 @@
         side = jnp.where(lanes == POS, position.astype(BF), side)
         return jnp.concatenate([compact, side], axis=1)
 
-    held_rows = held.reshape(steps * group, wide)
-    received = exchange(held_rows, steps)
-
     both_w = jnp.concatenate([gate_w[0], up_w[0]], axis=1)
-    batch = steps * n_dp
-    own = [compacted(received, step, held[step], step, my_dp) for step in range(steps)]
-    beyond = list(range(STEPS + 1, n_dp))
-    apart = {
-        k: [(i, i + k) for i in range(n_dp - k)] + [(i + k, i) for i in range(n_dp - k)]
-        for k in range(NEAR + 1, n_dp)
-    }
-    leaving = jnp.where(own[-1][0, 0] == own[-1][0, 0], held_rows, jnp.zeros_like(held_rows))
-    distant = jnp.concatenate([lax.ppermute(leaving, "dp", apart[k]) for k in beyond], axis=0)
-
-    to_right, to_left = list(own), list(own)
+    last = n_dp - 1
+    own = [None] * steps
+    to_right, to_left = [None] * steps, [None] * steps
     done = [[[] for _ in range(n_dp)] for _ in range(steps)]
-    last = n_dp - 1
-    for j in range(1, STEPS + 1):
-        for s in range(steps):
-            to_right[s] = lax.ppermute(to_right[s], "dp", right[j - 1])
-            to_left[s] = lax.ppermute(to_left[s], "dp", left[j - 1])
-            blocks = [to_right[s], to_left[s]] + ([own[s]] if j == 1 else [])
-            passed = 2 if j < STEPS else 0
-            extra = [made[0]] if (j, s) != (1, 0) else []
-            sent, made = project(both_w, blocks, passed, extra)
-            if passed:
-                to_right[s], to_left[s] = sent
-            done[s][j].append((made[0], 0, last))
-            done[s][n_dp - j].append((made[1], 0, last))
-            if j == 1:
-                done[s][0].append((made[2], 0, last))
-            if (j, s) == (2, steps - 1):
-                received_far = exchange(
-                    distant, len(beyond) * steps, made[0][0, 0] == made[0][0, 0]
+    own[0] = compacted(exchange(held[0]), held[0], 0)
+    to_right[0], to_left[0] = own[0], own[0]
+    arrived = exchange(held[1], own[0][0, 0] == own[0][0, 0])
+    order = [(1, 0)]
+    for j in range(2, n_dp):
+        order += [(j, 0), (j - 1, 1)]
+    order.append((last, 1))
+    made = None
+    for j, s in order:
+        if (j, s) == (2, 0):
+            own[1] = compacted(arrived, held[1], 1, made[0][0, 0] == made[0][0, 0])
+            to_right[1], to_left[1] = own[1], own[1]
+        to_right[s] = lax.ppermute(to_right[s], "dp", right[j - 1])
+        to_left[s] = lax.ppermute(to_left[s], "dp", left[j - 1])
+        blocks = [to_right[s], to_left[s]] + ([own[s]] if j == 1 else [])
+        passed = 2 if j < last else 0
+        sent, made = project(both_w, blocks, passed, [] if made is None else [made[0]])
+        if passed:
+            to_right[s], to_left[s] = sent
+        done[s][j].append((made[0], 0, last))
+        done[s][n_dp - j].append((made[1], 0, last))
+        if j == 1:
+            done[s][0].append((made[2], 0, last))
+
+    partials = []
+    for s in range(steps):
+        hidden = assemble([done[s]], 0, my_dp)
+        shards, places_of = [hidden], [lambda z: z]
+        going_right, going_left = hidden, hidden
+        for j in range(1, n_dp):
+            going_right = lax.ppermute(going_right, "dp", right[j - 1])
+            going_left = lax.ppermute(going_left, "dp", left[j - 1])
+            shards += [going_right, going_left]
+            places_of.append(lambda z, j=j: lax.rem(z - j + n_dp, n_dp))
+            places_of.append(lambda z, j=j: lax.rem(z + j, n_dp))
+        output = project_down(shards, places_of, down_w[0], n_dp, my_dp)
+        sides = assemble([done[s]], LANES, my_dp).reshape(n_dp, ROWS, LANES)
+        positions = sides[:, :, POS].astype(jnp.int32) - 1
+        unpick = (line[None, :, None] == positions[:, None, :]).astype(BF)
+        spread = jnp.einsum(
+            "bpr,brf->bpf",
+            unpick,
+            output.reshape(n_dp, ROWS, width),
+            preferred_element_type=F32,
+        ).astype(BF)
+        back = lax.all_to_all(
+            spread.reshape(n_dp, columns, quad * MOST, width).transpose(1, 0, 2, 3),
+            ("x", "y"),
+            split_axis=0,
+            concat_axis=0,
+            tiled=True,
+        )
+        token_meta = sides[:, :group].reshape(n_dp * group, LANES)
+        hits, place = places(token_meta, me, columns, quad, tok, top)
+        parts = []
+        for lane in (HI, MID):
+            weight = jnp.zeros((n_dp * group, boxes), F32)
+            for k in range(top):
+                weight = jnp.where(
+                    hits[k], token_meta[:, lane + k : lane + k + 1].astype(F32), weight
                 )
-        if j == STEPS:
-            ready = made[0][0, 0] == made[0][0, 0]
-            late = project(
-                both_w,
-                [
-                    compacted(
-                        received_far,
-                        i * steps + s,
-                        distant[(i * steps + s) * group : (i * steps + s + 1) * group],
-                        s,
-                        jnp.where(my_dp >= k, my_dp - k, my_dp + k),
-                        ready,
-                    )
-                    for i, k in enumerate(beyond)
-                    for s in range(steps)
-                ],
-                0,
-            )[1]
-            for i, k in enumerate(beyond):
-                for s in range(steps):
-                    done[s][k].append((late[i * steps + s], k, last))
-                    done[s][n_dp - k].append((late[i * steps + s], 0, last - k))
-    hidden = assemble(done, 0, my_dp)
-    shards, places_of = [hidden], [lambda z: z]
-    going_right, going_left = hidden, hidden
-    for k in range(NEAR + 1, n_dp):
-        shards.append(lax.ppermute(hidden, "dp", apart[k]))
-        places_of.append(lambda z, k=k: lax.rem(jnp.where(z >= k, z - k, z + k), n_dp))
-    for j in range(1, NEAR + 1):
-        going_right = lax.ppermute(going_right, "dp", right[j - 1])
-        going_left = lax.ppermute(going_left, "dp", left[j - 1])
-        shards += [going_right, going_left]
-        places_of.append(lambda z, j=j: lax.rem(z - j + n_dp, n_dp))
-        places_of.append(lambda z, j=j: lax.rem(z + j, n_dp))
-    output = project_down(shards, places_of, down_w[0], n_dp, my_dp)
-
-    sides = assemble(done, LANES, my_dp).reshape(batch, ROWS, LANES)
-
-    positions = sides[:, :, POS].astype(jnp.int32) - 1
-    unpick = (line[None, :, None] == positions[:, None, :]).astype(BF)
-    spread = jnp.einsum(
-        "bpr,brf->bpf",
-        unpick,
-        output.reshape(batch, ROWS, width),
-        preferred_element_type=F32,
-    ).astype(BF)
-    back = lax.all_to_all(
-        spread.reshape(batch, columns, quad * MOST, width).transpose(1, 0, 2, 3),
-        ("x", "y"),
-        split_axis=0,
-        concat_axis=0,
-        tiled=True,
-    )
-
-    token_meta = sides[:, :group].reshape(batch * group, LANES)
-    hits, place = places(token_meta, me, columns, quad, tok, top)
-    parts = []
-    for lane in (HI, MID):
-        weight = jnp.zeros((batch * group, boxes), F32)
-        for k in range(top):
-            weight = jnp.where(
-                hits[k], token_meta[:, lane + k : lane + k + 1].astype(F32), weight
-            )
-        parts.append(jnp.where(place, weight, 0.0).astype(BF).reshape(batch, group, boxes))
-    sums = jnp.einsum(
-        "btp,bpf->btf",
-        jnp.concatenate(parts, axis=1),
-        back.transpose(1, 0, 2, 3).reshape(batch, boxes, width),
-        preferred_element_type=F32,
-    )
-    partial = (sums[:, :group] + sums[:, group:]).astype(BF)
+            parts.append(jnp.where(place, weight, 0.0).astype(BF).reshape(n_dp, group, boxes))
+        sums = jnp.einsum(
+            "btp,bpf->btf",
+            jnp.concatenate(parts, axis=1),
+            back.transpose(1, 0, 2, 3).reshape(n_dp, boxes, width),
+            preferred_element_type=F32,
+        )
+        partials.append((sums[:, :group] + sums[:, group:]).astype(BF))
+    partial = jnp.stack(partials)
     partial = partial.reshape(steps, n_dp, 2, 2, tok, width).transpose(3, 2, 1, 0, 4, 5)
     swapped = lax.all_to_all(partial, "core", split_axis=0, concat_axis=0, tiled=True)
     halves = jnp.sum(swapped.astype(F32), axis=0).astype(BF)

time: 350 us -> 351 us (level)
  local copies, waits for them, and re-layouts: 21.5 us -> 10.8 us
  waiting for transfers between devices: 120 us -> 128 us
  Pallas kernels: 15.1 us -> 22.5 us
  between operations: 8.9 us -> 5.2 us
  matrix products: 13.4 us -> 9.78 us
    ppermute x5 -> x14, waiting for transfers between devices: 9.89 us -> 49.9 us  [on_device(): going_left = lax.ppermute(going_left, 'dp', left[j - 1])]
    ppermute x4 -> x0, waiting for transfers between devices: 30.7 us -> none  [the longest x2 18.6 us: on_device(): lax.ppermute(leaving, 'dp', apart[k])]
    ppermute x4 -> x0, starting transfers between devices: 22.5 us -> none  [the longest x2 12.1 us: on_device(): lax.ppermute(leaving, 'dp', apart[k])]
    all_to_all x3 -> x4, waiting for transfers between devices: 40.9 us -> 22.4 us  [the longest x2 12.7 us: exchange(): lax.all_to_all(send.reshape(columns, quad * MOST, wide), ('x', 'y'), spli...]
    ppermute x10 -> x14, waiting for transfers between devices: 38.4 us -> 52.7 us  [on_device(): to_left[s] = lax.ppermute(to_left[s], 'dp', left[j - 1])]
    ppermute x5 -> x14, starting transfers between devices: 6.56 us -> 18 us  [on_device(): going_left = lax.ppermute(going_left, 'dp', left[j - 1])]
    all_to_all x1, blocking collectives: 14.3 us -> 23.2 us  [on_device(): lax.all_to_all(partial, 'core', split_axis=0, concat_axis=0, tiled=True)]
    pallas_call x11 -> x14, Pallas kernels: 13.3 us -> 20.4 us  [project(): pl.pallas_call(functools.partial(project_kernel, count, passed, len(extra...]
  transfers between devices with their start and end apart: 37 -> 60, of which waited for: 16 -> 28; matrix products, arithmetic and copies ran while one was open for 4% -> 5% of each run, Pallas kernels for 3% -> 6%
where the time goes in v8:
time: 351 us; the launch traced here: 346 us
  waiting for transfers between devices  128 us (36%)
  starting transfers between devices  92.4 us (26%)
  blocking collectives  66.8 us (19%)
  Pallas kernels  22.5 us (6%)
  local copies, waits for them, and re-layouts  10.8 us (3%)
  other arithmetic  10.3 us (3%)
  matrix products  9.78 us (3%)
  between operations  5.2 us (1%)
    ppermute x14, waiting for transfers between devices, on_device(): to_left[s] = lax.ppermute(to_left[s], 'dp', left[j - 1])  52.7 us
    ppermute x14, waiting for transfers between devices, on_device(): going_left = lax.ppermute(going_left, 'dp', left[j - 1])  49.9 us
    all_to_all x1, blocking collectives, on_device(): lax.all_to_all(partial, 'core', split_axis=0, concat_axis=0, tiled=True)  23.2 us
    all_to_all x1, blocking collectives, on_device(): lax.all_to_all(halves.reshape(2 * n_dp, mine * width // LANES, LANES), ('...  21.8 us
    all_gather x1, blocking collectives, on_device(): lax.all_gather(packed.reshape(steps, tok, wide), ('zh', 'core'), axis=1,...  21.7 us
    ppermute x14, starting transfers between devices, on_device(): to_right[s] = lax.ppermute(to_right[s], 'dp', right[j - 1])  21.2 us
    pallas_call x14, Pallas kernels, project(): pl.pallas_call(functools.partial(project_kernel, count, passed, len(extra...  20.4 us
    ppermute x14, starting transfers between devices, on_device(): to_left[s] = lax.ppermute(to_left[s], 'dp', left[j - 1])  18.1 us
  transfers between devices with their start and end apart: 60, of which 28 were waited for; matrix products, arithmetic and copies ran while one was open for 5% of the time, Pallas kernels for 6%

profile of v8, /device:TPU:1, one launch (start us, length us, event | category | flops | bytes accessed | tf_op | source)
XLA Modules:
  0.0 346.0 jit_solution(7803193090057169565)
XLA Ops:
  4.8 21.7 %all_gather.3 = bf16[2,24,4224]{2,0,1:T(2,128)(2,1)S(1)} all-gather(bf16[2,6,4224]{2,0,1:T(2,128)(2,1)S(1)} %pad_maximum_fusion.3), channel_id=1, replica_groups=mesh['dp'=8,'x'=4,'y'=4,'zh'=2,'core'=2] {'zh','core'}, dimensions={1}, use_global_device_ids=true | all-gather | bytes 506880 | tf_op jit(solution)/shard_map/all_gather | solution.py:195
  29.0 5.7 %all-to-all-start = ((bf16[16,8,4224]{2,1,0:T(8,128)(2,1)}), bf16[16,8,4224]{2,1,0:T(8,128)(2,1)S(1)}, u32[]{:S(2)}, u32[]{:S(2)}) async-start(bf16[16,8,4224]{2,1,0:T(8,128)(2,1)} %fusion), calls=%async_computation | async-start | bytes 2162688 | tf_op jit(solution)/shard_map/all_to_all | solution.py:211
  38.3 12.7 %all-to-all-done = bf16[16,8,4224]{2,1,0:T(8,128)(2,1)S(1)} async-done(((bf16[16,8,4224]{2,1,0:T(8,128)(2,1)}), bf16[16,8,4224]{2,1,0:T(8,128)(2,1)S(1)}, u32[]{:S(2)}, u32[]{:S(2)}) %all-to-all-start) | async-done | bytes 1081376 | tf_op jit(solution)/shard_map/all_to_all | solution.py:211
  55.3 4.4 %all-to-all-start.1 = ((bf16[16,8,4224]{2,1,0:T(8,128)(2,1)}), bf16[16,8,4224]{2,1,0:T(8,128)(2,1)}, u32[]{:S(2)}, u32[]{:S(2)}) async-start(bf16[16,8,4224]{2,1,0:T(8,128)(2,1)} %fusion.1), calls=%async_computation.1 | async-start | bytes 2162688 | tf_op jit(solution)/shard_map/all_to_all | solution.py:211
  60.0 9.0 %collective-permute-start = (bf16[48,4224]{1,0:T(8,128)(2,1)S(1)}, bf16[48,4224]{1,0:T(8,128)(2,1)S(1)}, u32[]{:S(2)}, u32[]{:S(2)}) collective-permute-start(bf16[48,4224]{1,0:T(8,128)(2,1)S(1)} %pad_maximum_fusion.1.refs_2_), channel_id=1, source_target_pairs={{0,64},{64,128},{128,192},{192,256},{256,320},{320,384},{384,448},... | collective-permute-start | bytes 1216520 | tf_op jit(solution)/shard_map/ppermute | solution.py:257
  95.8 4.0 %collective-permute-done.7.refs_1_ = bf16[48,4224]{1,0:T(8,128)(2,1)S(1)} collective-permute-done((bf16[48,4224]{1,0:T(8,128)(2,1)S(1)}, bf16[48,4224]{1,0:T(8,128)(2,1)S(1)}, u32[]{:S(2)}, u32[]{:S(2)}) %collective-permute-start.7) | collective-permute-done | bytes 405536 | tf_op jit(solution)/shard_map/ppermute | solution.py:258
  103.0 6.0 %collective-permute-done.5.refs_1_ = bf16[48,4224]{1,0:T(8,128)(2,1)S(1)} collective-permute-done((bf16[48,4224]{1,0:T(8,128)(2,1)}, bf16[48,4224]{1,0:T(8,128)(2,1)S(1)}, u32[]{:S(2)}, u32[]{:S(2)}) %collective-permute-start.5) | collective-permute-done | bytes 405536 | tf_op jit(solution)/shard_map/ppermute | solution.py:258
  112.0 6.7 %collective-permute-done.11.refs_1_ = bf16[48,4224]{1,0:T(8,128)(2,1)} collective-permute-done((bf16[48,4224]{1,0:T(8,128)(2,1)S(1)}, bf16[48,4224]{1,0:T(8,128)(2,1)}, u32[]{:S(2)}, u32[]{:S(2)}) %collective-permute-start.11) | collective-permute-done | bytes 405536 | tf_op jit(solution)/shard_map/ppermute | solution.py:258
  122.4 5.0 %collective-permute-done.9.refs_1_ = bf16[48,4224]{1,0:T(8,128)(2,1)} collective-permute-done((bf16[48,4224]{1,0:T(8,128)(2,1)S(1)}, bf16[48,4224]{1,0:T(8,128)(2,1)}, u32[]{:S(2)}, u32[]{:S(2)}) %collective-permute-start.9) | collective-permute-done | bytes 405536 | tf_op jit(solution)/shard_map/ppermute | solution.py:258
  131.1 4.1 %collective-permute-done.15.refs_1_ = bf16[48,4224]{1,0:T(8,128)(2,1)} collective-permute-done((bf16[48,4224]{1,0:T(8,128)(2,1)}, bf16[48,4224]{1,0:T(8,128)(2,1)}, u32[]{:S(2)}, u32[]{:S(2)}) %collective-permute-start.15) | collective-permute-done | bytes 405536 | tf_op jit(solution)/shard_map/ppermute | solution.py:258
  139.0 5.0 %collective-permute-done.13.refs_1_ = bf16[48,4224]{1,0:T(8,128)(2,1)} collective-permute-done((bf16[48,4224]{1,0:T(8,128)(2,1)}, bf16[48,4224]{1,0:T(8,128)(2,1)}, u32[]{:S(2)}, u32[]{:S(2)}) %collective-permute-start.13) | collective-permute-done | bytes 405536 | tf_op jit(solution)/shard_map/ppermute | solution.py:258
  147.7 4.9 %collective-permute-done.19.refs_1_ = bf16[48,4224]{1,0:T(8,128)(2,1)} collective-permute-done((bf16[48,4224]{1,0:T(8,128)(2,1)}, bf16[48,4224]{1,0:T(8,128)(2,1)}, u32[]{:S(2)}, u32[]{:S(2)}) %collective-permute-start.19) | collective-permute-done | bytes 405536 | tf_op jit(solution)/shard_map/ppermute | solution.py:258
  162.1 5.0 %collective-permute-done.23.refs_1_ = bf16[48,4224]{1,0:T(8,128)(2,1)} collective-permute-done((bf16[48,4224]{1,0:T(8,128)(2,1)}, bf16[48,4224]{1,0:T(8,128)(2,1)}, u32[]{:S(2)}, u32[]{:S(2)}) %collective-permute-start.23) | collective-permute-done | bytes 405536 | tf_op jit(solution)/shard_map/ppermute | solution.py:258
  170.8 6.0 %collective-permute-done.21.refs_1_ = bf16[48,4224]{1,0:T(8,128)(2,1)} collective-permute-done((bf16[48,4224]{1,0:T(8,128)(2,1)}, bf16[48,4224]{1,0:T(8,128)(2,1)}, u32[]{:S(2)}, u32[]{:S(2)}) %collective-permute-start.21) | collective-permute-done | bytes 405536 | tf_op jit(solution)/shard_map/ppermute | solution.py:258
  183.1 5.4 %collective-permute-done.25.refs_2_ = bf16[384,128]{1,0:T(8,128)(2,1)S(1)} collective-permute-done((bf16[384,128]{1,0:T(8,128)(2,1)S(1)}, bf16[384,128]{1,0:T(8,128)(2,1)S(1)}, u32[]{:S(2)}, u32[]{:S(2)}) %collective-permute-start.25) | collective-permute-done | bytes 98336 | tf_op jit(solution)/shard_map/ppermute | solution.py:276
  207.4 5.6 %collective-permute-done.33.refs_10_ = bf16[384,128]{1,0:T(8,128)(2,1)S(1)} collective-permute-done((bf16[384,128]{1,0:T(8,128)(2,1)S(1)}, bf16[384,128]{1,0:T(8,128)(2,1)S(1)}, u32[]{:S(2)}, u32[]{:S(2)}) %collective-permute-start.33) | collective-permute-done | bytes 98336 | tf_op jit(solution)/shard_map/ppermute | solution.py:276
  220.5 5.2 %collective-permute-done.37.refs_14_ = bf16[384,128]{1,0:T(8,128)(2,1)S(1)} collective-permute-done((bf16[384,128]{1,0:T(8,128)(2,1)S(1)}, bf16[384,128]{1,0:T(8,128)(2,1)S(1)}, u32[]{:S(2)}, u32[]{:S(2)}) %collective-permute-start.37) | collective-permute-done | bytes 98336 | tf_op jit(solution)/shard_map/ppermute | solution.py:276
  232.1 7.3 %all-to-all-start.2 = ((bf16[16,8,8,512]{3,2,1,0:T(8,128)(2,1)}), bf16[16,8,8,512]{3,2,1,0:T(8,128)(2,1)S(1)}, u32[]{:S(2)}, u32[]{:S(2)}) async-start(bf16[16,8,8,512]{3,2,1,0:T(8,128)(2,1)} %bitcast.88), calls=%async_computation.2 | async-start | bytes 2097152 | tf_op jit(solution)/shard_map/all_to_all | solution.py:290
  242.7 4.5 %collective-permute-done.45.refs_4_ = bf16[384,128]{1,0:T(8,128)(2,1)S(1)} collective-permute-done((bf16[384,128]{1,0:T(8,128)(2,1)S(1)}, bf16[384,128]{1,0:T(8,128)(2,1)S(1)}, u32[]{:S(2)}, u32[]{:S(2)}) %collective-permute-start.45) | collective-permute-done | bytes 98336 | tf_op jit(solution)/shard_map/ppermute | solution.py:276
  266.9 6.0 %collective-permute-done.53.refs_12_ = bf16[384,128]{1,0:T(8,128)(2,1)S(1)} collective-permute-done((bf16[384,128]{1,0:T(8,128)(2,1)S(1)}, bf16[384,128]{1,0:T(8,128)(2,1)S(1)}, u32[]{:S(2)}, u32[]{:S(2)}) %collective-permute-start.53) | collective-permute-done | bytes 98336 | tf_op jit(solution)/shard_map/ppermute | solution.py:276
  281.1 6.1 %all-to-all-start.3 = ((bf16[16,8,8,512]{3,2,1,0:T(8,128)(2,1)}), bf16[16,8,8,512]{3,2,1,0:T(8,128)(2,1)S(1)}, u32[]{:S(2)}, u32[]{:S(2)}) async-start(bf16[16,8,8,512]{3,2,1,0:T(8,128)(2,1)} %bitcast.87), calls=%async_computation.3 | async-start | bytes 2097152 | tf_op jit(solution)/shard_map/all_to_all | solution.py:290
  289.3 9.7 %all-to-all-done.3 = bf16[16,8,8,512]{3,2,1,0:T(8,128)(2,1)S(1)} async-done(((bf16[16,8,8,512]{3,2,1,0:T(8,128)(2,1)}), bf16[16,8,8,512]{3,2,1,0:T(8,128)(2,1)S(1)}, u32[]{:S(2)}, u32[]{:S(2)}) %all-to-all-start.3) | async-done | bytes 1048608 | tf_op jit(solution)/shard_map/all_to_all | solution.py:290
  299.5 23.2 %all_to_all.30 = bf16[2,2,8,2,6,512]{5,2,4,1,3,0:T(8,128)(2,1)S(1)} all-to-all(bf16[2,2,8,2,6,512]{5,2,4,1,3,0:T(8,128)(2,1)S(1)} %copy.103), channel_id=1, replica_groups=mesh['dp'=8,'x'=4,'y'=4,'zh'=2,'core'=2] {'core'}, dimensions={0} | all-to-all | bytes 786432 | tf_op jit(solution)/shard_map/all_to_all | solution.py:316
  323.0 21.8 %all_to_all.31 = bf16[16,48,128]{2,1,0:T(8,128)(2,1)S(1)} all-to-all(bf16[16,48,128]{2,1,0:T(8,128)(2,1)S(1)} %reshape.428), channel_id=1, replica_groups=mesh['dp'=8,'x'=4,'y'=4,'zh'=2,'core'=2] {'zh','dp'}, dimensions={0} | all-to-all | bytes 393216 | tf_op jit(solution)/shard_map/all_to_all | solution.py:318
  (228 shorter events, 145.7 us)
Async XLA Ops:
  29.0 22.1 %all-to-all-start = ((bf16[16,8,4224]{2,1,0:T(8,128)(2,1)}), bf16[16,8,4224]{2,1,0:T(8,128)(2,1)S(1)}, u32[]{:S(2)}, u32[]{:S(2)}) async-start(bf16[16,8,4224]{2,1,0:T(8,128)(2,1)} %fusion), calls=%async_computation | async-start | bytes 2162688 | tf_op jit(solution)/shard_map/all_to_all | solution.py:211
  55.3 28.5 %all-to-all-start.1 = ((bf16[16,8,4224]{2,1,0:T(8,128)(2,1)}), bf16[16,8,4224]{2,1,0:T(8,128)(2,1)}, u32[]{:S(2)}, u32[]{:S(2)}) async-start(bf16[16,8,4224]{2,1,0:T(8,128)(2,1)} %fusion.1), calls=%async_computation.1 | async-start | bytes 2162688 | tf_op jit(solution)/shard_map/all_to_all | solution.py:211
  60.0 15.0 %collective-permute-start = (bf16[48,4224]{1,0:T(8,128)(2,1)S(1)}, bf16[48,4224]{1,0:T(8,128)(2,1)S(1)}, u32[]{:S(2)}, u32[]{:S(2)}) collective-permute-start(bf16[48,4224]{1,0:T(8,128)(2,1)S(1)} %pad_maximum_fusion.1.refs_2_), channel_id=1, source_target_pairs={{0,64},{64,128},{128,192},{192,256},{256,320},{320,384},{384,448},... | collective-permute-start | bytes 1216520 | tf_op jit(solution)/shard_map/ppermute | solution.py:257
  94.5 14.5 %collective-permute-start.5 = (bf16[48,4224]{1,0:T(8,128)(2,1)}, bf16[48,4224]{1,0:T(8,128)(2,1)S(1)}, u32[]{:S(2)}, u32[]{:S(2)}) collective-permute-start(bf16[48,4224]{1,0:T(8,128)(2,1)} %get-tuple-element.64), channel_id=1, source_target_pairs={{64,0},{128,64},{192,128},{256,192},{320,256},{65,1},{129,65},{193... | collective-permute-start | bytes 1216520 | tf_op jit(solution)/shard_map/ppermute | solution.py:258
  101.0 11.0 %collective-permute-start.10 = (bf16[48,4224]{1,0:T(8,128)(2,1)S(1)}, bf16[48,4224]{1,0:T(8,128)(2,1)S(1)}, u32[]{:S(2)}, u32[]{:S(2)}) collective-permute-start(bf16[48,4224]{1,0:T(8,128)(2,1)S(1)} %get-tuple-element.69), channel_id=1, source_target_pairs={{64,128},{128,192},{192,256},{256,320},{320,384},{384,448},{65,129... | collective-permute-start | bytes 1216520 | tf_op jit(solution)/shard_map/ppermute | solution.py:257
  101.7 17.0 %collective-permute-start.11 = (bf16[48,4224]{1,0:T(8,128)(2,1)S(1)}, bf16[48,4224]{1,0:T(8,128)(2,1)}, u32[]{:S(2)}, u32[]{:S(2)}) collective-permute-start(bf16[48,4224]{1,0:T(8,128)(2,1)S(1)} %get-tuple-element.70), channel_id=1, source_target_pairs={{64,0},{128,64},{192,128},{256,192},{320,256},{384,320},{65,1},{12... | collective-permute-start | bytes 1216520 | tf_op jit(solution)/shard_map/ppermute | solution.py:258
  110.0 12.4 %collective-permute-start.8 = (bf16[48,4224]{1,0:T(8,128)(2,1)S(1)}, bf16[48,4224]{1,0:T(8,128)(2,1)S(1)}, u32[]{:S(2)}, u32[]{:S(2)}) collective-permute-start(bf16[48,4224]{1,0:T(8,128)(2,1)S(1)} %get-tuple-element.67), channel_id=1, source_target_pairs={{192,256},{256,320},{320,384},{384,448},{193,257},{257,321},{321,3... | collective-permute-start | bytes 1216520 | tf_op jit(solution)/shard_map/ppermute | solution.py:257
  110.7 16.7 %collective-permute-start.9 = (bf16[48,4224]{1,0:T(8,128)(2,1)S(1)}, bf16[48,4224]{1,0:T(8,128)(2,1)}, u32[]{:S(2)}, u32[]{:S(2)}) collective-permute-start(bf16[48,4224]{1,0:T(8,128)(2,1)S(1)} %get-tuple-element.68), channel_id=1, source_target_pairs={{64,0},{128,64},{192,128},{256,192},{65,1},{129,65},{193,129},{257... | collective-permute-start | bytes 1216520 | tf_op jit(solution)/shard_map/ppermute | solution.py:258
  120.4 10.7 %collective-permute-start.14 = (bf16[48,4224]{1,0:T(8,128)(2,1)S(1)}, bf16[48,4224]{1,0:T(8,128)(2,1)S(1)}, u32[]{:S(2)}, u32[]{:S(2)}) collective-permute-start(bf16[48,4224]{1,0:T(8,128)(2,1)S(1)} %get-tuple-element.75), channel_id=1, source_target_pairs={{128,192},{192,256},{256,320},{320,384},{384,448},{129,193},{193,2... | collective-permute-start | bytes 1216520 | tf_op jit(solution)/shard_map/ppermute | solution.py:257
  121.1 14.1 %collective-permute-start.15 = (bf16[48,4224]{1,0:T(8,128)(2,1)}, bf16[48,4224]{1,0:T(8,128)(2,1)}, u32[]{:S(2)}, u32[]{:S(2)}) collective-permute-start(bf16[48,4224]{1,0:T(8,128)(2,1)} %get-tuple-element.76), channel_id=1, source_target_pairs={{64,0},{128,64},{192,128},{256,192},{320,256},{65,1},{129,65},{193... | collective-permute-start | bytes 1216520 | tf_op jit(solution)/shard_map/ppermute | solution.py:258
  129.8 14.1 %collective-permute-start.13 = (bf16[48,4224]{1,0:T(8,128)(2,1)}, bf16[48,4224]{1,0:T(8,128)(2,1)}, u32[]{:S(2)}, u32[]{:S(2)}) collective-permute-start(bf16[48,4224]{1,0:T(8,128)(2,1)} %get-tuple-element.74), channel_id=1, source_target_pairs={{64,0},{128,64},{192,128},{65,1},{129,65},{193,129},{66,2},{130,66... | collective-permute-start | bytes 1216520 | tf_op jit(solution)/shard_map/ppermute | solution.py:258
  137.7 14.9 %collective-permute-start.19 = (bf16[48,4224]{1,0:T(8,128)(2,1)}, bf16[48,4224]{1,0:T(8,128)(2,1)}, u32[]{:S(2)}, u32[]{:S(2)}) collective-permute-start(bf16[48,4224]{1,0:T(8,128)(2,1)} %get-tuple-element.82), channel_id=1, source_target_pairs={{64,0},{128,64},{192,128},{256,192},{65,1},{129,65},{193,129},{257... | collective-permute-start | bytes 1216520 | tf_op jit(solution)/shard_map/ppermute | solution.py:258
  146.3 12.1 %collective-permute-start.17 = (bf16[48,4224]{1,0:T(8,128)(2,1)}, bf16[48,4224]{1,0:T(8,128)(2,1)}, u32[]{:S(2)}, u32[]{:S(2)}) collective-permute-start(bf16[48,4224]{1,0:T(8,128)(2,1)} %get-tuple-element.80), channel_id=1, source_target_pairs={{64,0},{128,64},{65,1},{129,65},{66,2},{130,66},{67,3},{131,67},{6... | collective-permute-start | bytes 1216520 | tf_op jit(solution)/shard_map/ppermute | solution.py:258
  155.0 12.1 %collective-permute-start.23 = (bf16[48,4224]{1,0:T(8,128)(2,1)}, bf16[48,4224]{1,0:T(8,128)(2,1)}, u32[]{:S(2)}, u32[]{:S(2)}) collective-permute-start(bf16[48,4224]{1,0:T(8,128)(2,1)} %get-tuple-element.88), channel_id=1, source_target_pairs={{64,0},{128,64},{192,128},{65,1},{129,65},{193,129},{66,2},{130,66... | collective-permute-start | bytes 1216520 | tf_op jit(solution)/shard_map/ppermute | solution.py:258
  160.1 10.7 %collective-permute-start.20 = (bf16[48,4224]{1,0:T(8,128)(2,1)S(1)}, bf16[48,4224]{1,0:T(8,128)(2,1)S(1)}, u32[]{:S(2)}, u32[]{:S(2)}) collective-permute-start(bf16[48,4224]{1,0:T(8,128)(2,1)S(1)} %get-tuple-element.85), channel_id=1, source_target_pairs={{384,448},{385,449},{386,450},{387,451},{388,452},{389,453},{390,4... | collective-permute-start | bytes 1216520 | tf_op jit(solution)/shard_map/ppermute | solution.py:257
  160.8 16.0 %collective-permute-start.21 = (bf16[48,4224]{1,0:T(8,128)(2,1)}, bf16[48,4224]{1,0:T(8,128)(2,1)}, u32[]{:S(2)}, u32[]{:S(2)}) collective-permute-start(bf16[48,4224]{1,0:T(8,128)(2,1)} %get-tuple-element.86), channel_id=1, source_target_pairs={{64,0},{65,1},{66,2},{67,3},{68,4},{69,5},{70,6},{71,7},{72,8},{73... | collective-permute-start | bytes 1216520 | tf_op jit(solution)/shard_map/ppermute | solution.py:258
  168.8 31.7 %collective-permute-start.38 = (bf16[48,4224]{1,0:T(8,128)(2,1)S(1)}, bf16[48,4224]{1,0:T(8,128)(2,1)S(1)}, u32[]{:S(2)}, u32[]{:S(2)}) collective-permute-start(bf16[48,4224]{1,0:T(8,128)(2,1)S(1)} %get-tuple-element.100), channel_id=1, source_target_pairs={{320,384},{384,448},{321,385},{385,449},{322,386},{386,450},{323,3... | collective-permute-start | bytes 1216520 | tf_op jit(solution)/shard_map/ppermute | solution.py:257
  169.5 31.0 %collective-permute-start.39 = (bf16[48,4224]{1,0:T(8,128)(2,1)}, bf16[48,4224]{1,0:T(8,128)(2,1)S(1)}, u32[]{:S(2)}, u32[]{:S(2)}) collective-permute-start(bf16[48,4224]{1,0:T(8,128)(2,1)} %get-tuple-element.101), channel_id=1, source_target_pairs={{64,0},{128,64},{65,1},{129,65},{66,2},{130,66},{67,3},{131,67},{6... | collective-permute-start | bytes 1216520 | tf_op jit(solution)/shard_map/ppermute | solution.py:258
  201.4 25.2 %collective-permute-start.40 = (bf16[48,4224]{1,0:T(8,128)(2,1)S(1)}, bf16[48,4224]{1,0:T(8,128)(2,1)S(1)}, u32[]{:S(2)}, u32[]{:S(2)}) collective-permute-start(bf16[48,4224]{1,0:T(8,128)(2,1)S(1)} %get-tuple-element.102), channel_id=1, source_target_pairs={{384,448},{385,449},{386,450},{387,451},{388,452},{389,453},{390,4... | collective-permute-start | bytes 1216520 | tf_op jit(solution)/shard_map/ppermute | solution.py:257
  202.1 24.5 %collective-permute-start.41 = (bf16[48,4224]{1,0:T(8,128)(2,1)S(1)}, bf16[48,4224]{1,0:T(8,128)(2,1)S(1)}, u32[]{:S(2)}, u32[]{:S(2)}) collective-permute-start(bf16[48,4224]{1,0:T(8,128)(2,1)S(1)} %get-tuple-element.103), channel_id=1, source_target_pairs={{64,0},{65,1},{66,2},{67,3},{68,4},{69,5},{70,6},{71,7},{72,8},{73... | collective-permute-start | bytes 1216520 | tf_op jit(solution)/shard_map/ppermute | solution.py:258
  227.7 11.8 %collective-permute-start.42 = (bf16[384,128]{1,0:T(8,128)(2,1)S(1)}, bf16[384,128]{1,0:T(8,128)(2,1)S(1)}, u32[]{:S(2)}, u32[]{:S(2)}) collective-permute-start(bf16[384,128]{1,0:T(8,128)(2,1)S(1)} %shard_map.118.refs_0_), channel_id=1, source_target_pairs={{0,64},{64,128},{128,192},{192,256},{256,320},{320,384},{384,448},... | collective-permute-start | bytes 294920 | tf_op jit(solution)/shard_map/ppermute | solution.py:275
  229.0 11.1 %collective-permute-start.43 = (bf16[384,128]{1,0:T(8,128)(2,1)S(1)}, bf16[384,128]{1,0:T(8,128)(2,1)S(1)}, u32[]{:S(2)}, u32[]{:S(2)}) collective-permute-start(bf16[384,128]{1,0:T(8,128)(2,1)S(1)} %shard_map.118.refs_0_), channel_id=1, source_target_pairs={{64,0},{128,64},{192,128},{256,192},{320,256},{384,320},{448,384},... | collective-permute-start | bytes 294920 | tf_op jit(solution)/shard_map/ppermute | solution.py:276
  232.1 49.0 %all-to-all-start.2 = ((bf16[16,8,8,512]{3,2,1,0:T(8,128)(2,1)}), bf16[16,8,8,512]{3,2,1,0:T(8,128)(2,1)S(1)}, u32[]{:S(2)}, u32[]{:S(2)}) async-start(bf16[16,8,8,512]{3,2,1,0:T(8,128)(2,1)} %bitcast.88), calls=%async_computation.2 | async-start | bytes 2097152 | tf_op jit(solution)/shard_map/all_to_all | solution.py:290
  281.1 17.9 %all-to-all-start.3 = ((bf16[16,8,8,512]{3,2,1,0:T(8,128)(2,1)}), bf16[16,8,8,512]{3,2,1,0:T(8,128)(2,1)S(1)}, u32[]{:S(2)}, u32[]{:S(2)}) async-start(bf16[16,8,8,512]{3,2,1,0:T(8,128)(2,1)} %bitcast.87), calls=%async_computation.3 | async-start | bytes 2097152 | tf_op jit(solution)/shard_map/all_to_all | solution.py:290
  (46 other events, 426.3 us)

commit v9 on v8

--- a/solution.py
+++ b/solution.py
@@ -249,7 +249,7 @@
     for j in range(2, n_dp):
         order += [(j, 0), (j - 1, 1)]
     order.append((last, 1))
-    made = None
+    made, made_at = None, {}
     for j, s in order:
         if (j, s) == (2, 0):
             own[1] = compacted(arrived, held[1], 1, made[0][0, 0] == made[0][0, 0])
@@ -259,6 +259,7 @@
         blocks = [to_right[s], to_left[s]] + ([own[s]] if j == 1 else [])
         passed = 2 if j < last else 0
         sent, made = project(both_w, blocks, passed, [] if made is None else [made[0]])
+        made_at[j, s] = made[0]
         if passed:
             to_right[s], to_left[s] = sent
         done[s][j].append((made[0], 0, last))
@@ -266,18 +267,39 @@
         if j == 1:
             done[s][0].append((made[2], 0, last))
 
+    def behind(block, others):
+        there = others[0][0, 0] == others[0][0, 0]
+        for other in others[1:]:
+            there = there & (other[0, 0] == other[0, 0])
+        return jnp.where(there, block, jnp.zeros_like(block))
+
+    hidden = [assemble([done[s]], 0, my_dp) for s in range(steps)]
+    shards = [[hidden[s]] for s in range(steps)]
+    places_of = [lambda z: z]
+    for j in range(1, n_dp):
+        places_of.append(lambda z, j=j: lax.rem(z - j + n_dp, n_dp))
+        places_of.append(lambda z, j=j: lax.rem(z + j, n_dp))
+
+    def pass_on(s, j, after=None):
+        going = shards[s][-2:] if j > 1 else [hidden[s], hidden[s]]
+        if after is not None:
+            going = [behind(going[0], after), behind(going[1], after)]
+        shards[s].append(lax.ppermute(going[0], "dp", right[j - 1]))
+        shards[s].append(lax.ppermute(going[1], "dp", left[j - 1]))
+
+    pass_on(0, 1)
+    pass_on(0, 2, [made_at[last - 1, 1]])
+    pass_on(0, 3)
+    pass_on(0, 4, [made_at[last, 1]])
+    for j in range(5, n_dp):
+        pass_on(1, j - 4)
+        pass_on(0, j, shards[1][-2:])
+    for j in range(n_dp - 4, n_dp):
+        pass_on(1, j)
+
     partials = []
     for s in range(steps):
-        hidden = assemble([done[s]], 0, my_dp)
-        shards, places_of = [hidden], [lambda z: z]
-        going_right, going_left = hidden, hidden
-        for j in range(1, n_dp):
-            going_right = lax.ppermute(going_right, "dp", right[j - 1])
-            going_left = lax.ppermute(going_left, "dp", left[j - 1])
-            shards += [going_right, going_left]
-            places_of.append(lambda z, j=j: lax.rem(z - j + n_dp, n_dp))
-            places_of.append(lambda z, j=j: lax.rem(z + j, n_dp))
-        output = project_down(shards, places_of, down_w[0], n_dp, my_dp)
+        output = project_down(shards[s], places_of, down_w[0], n_dp, my_dp)
         sides = assemble([done[s]], LANES, my_dp).reshape(n_dp, ROWS, LANES)
         positions = sides[:, :, POS].astype(jnp.int32) - 1
         unpick = (line[None, :, None] == positions[:, None, :]).astype(BF)

time: 351 us -> 356 us (1.014)
  waiting for transfers between devices: 128 us -> 117 us
  between operations: 5.2 us -> 16.2 us
  local copies, waits for them, and re-layouts: 10.8 us -> 15 us
    ppermute x28, waiting for transfers between devices: 50.2 us -> 35.9 us  [the longest x14 35.9 us: pass_on(): shards[s].append(lax.ppermute(going[1], 'dp', left[j - 1]))]
    slice x0 -> x8, local copies, waits for them, and re-layouts: none -> 4.74 us  [the longest x5 2.96 us: behind(): there = others[0][0, 0] == others[0][0, 0]]
    ppermute x14, waiting for transfers between devices: 52.7 us -> 57.2 us  [on_device(): to_left[s] = lax.ppermute(to_left[s], 'dp', left[j - 1])]
  transfers between devices with their start and end apart: 60 -> 60, of which waited for: 28 -> 23; matrix products, arithmetic and copies ran while one was open for 5% -> 6% of each run, Pallas kernels for 6% -> 6%
where the time goes in v9:
time: 356 us; the launch traced here: 351 us
  waiting for transfers between devices  117 us (33%)
  starting transfers between devices  94.3 us (26%)
  blocking collectives  65.6 us (18%)
  Pallas kernels  22.5 us (6%)
  between operations  16.2 us (5%)
  local copies, waits for them, and re-layouts  15 us (4%)
  matrix products  10.4 us (3%)
  other arithmetic  9.83 us (3%)
    ppermute x14, waiting for transfers between devices, on_device(): to_left[s] = lax.ppermute(to_left[s], 'dp', left[j - 1])  57.2 us
    ppermute x14, waiting for transfers between devices, pass_on(): shards[s].append(lax.ppermute(going[1], 'dp', left[j - 1]))  35.9 us
    all_to_all x1, blocking collectives, on_device(): lax.all_to_all(partial, 'core', split_axis=0, concat_axis=0, tiled=True)  22 us
    all_to_all x1, blocking collectives, on_device(): lax.all_to_all(halves.reshape(2 * n_dp, mine * width // LANES, LANES), ('...  21.9 us
    all_gather x1, blocking collectives, on_device(): lax.all_gather(packed.reshape(steps, tok, wide), ('zh', 'core'), axis=1,...  21.7 us
    ppermute x14, starting transfers between devices, on_device(): to_right[s] = lax.ppermute(to_right[s], 'dp', right[j - 1])  21.2 us
    pallas_call x14, Pallas kernels, project(): pl.pallas_call(functools.partial(project_kernel, count, passed, len(extra...  20.4 us
    ppermute x14, starting transfers between devices, pass_on(): shards[s].append(lax.ppermute(going[1], 'dp', left[j - 1]))  18.2 us
  transfers between devices with their start and end apart: 60, of which 23 were waited for; matrix products, arithmetic and copies ran while one was open for 6% of the time, Pallas kernels for 6%

profile of v9, /device:TPU:1, one launch (start us, length us, event | category | flops | bytes accessed | tf_op | source)
XLA Modules:
  0.0 351.1 jit_solution(15251010286699700479)
XLA Ops:
  4.8 21.7 %all_gather.3 = bf16[2,24,4224]{2,0,1:T(2,128)(2,1)S(1)} all-gather(bf16[2,6,4224]{2,0,1:T(2,128)(2,1)S(1)} %pad_maximum_fusion.3), channel_id=1, replica_groups=mesh['dp'=8,'x'=4,'y'=4,'zh'=2,'core'=2] {'zh','core'}, dimensions={1}, use_global_device_ids=true | all-gather | bytes 506880 | tf_op jit(solution)/shard_map/all_gather | solution.py:195
  29.0 5.7 %all-to-all-start = ((bf16[16,8,4224]{2,1,0:T(8,128)(2,1)}), bf16[16,8,4224]{2,1,0:T(8,128)(2,1)S(1)}, u32[]{:S(2)}, u32[]{:S(2)}) async-start(bf16[16,8,4224]{2,1,0:T(8,128)(2,1)} %fusion), calls=%async_computation | async-start | bytes 2162688 | tf_op jit(solution)/shard_map/all_to_all | solution.py:211
  38.4 12.7 %all-to-all-done = bf16[16,8,4224]{2,1,0:T(8,128)(2,1)S(1)} async-done(((bf16[16,8,4224]{2,1,0:T(8,128)(2,1)}), bf16[16,8,4224]{2,1,0:T(8,128)(2,1)S(1)}, u32[]{:S(2)}, u32[]{:S(2)}) %all-to-all-start) | async-done | bytes 1081376 | tf_op jit(solution)/shard_map/all_to_all | solution.py:211
  55.1 4.4 %all-to-all-start.1 = ((bf16[16,8,4224]{2,1,0:T(8,128)(2,1)}), bf16[16,8,4224]{2,1,0:T(8,128)(2,1)}, u32[]{:S(2)}, u32[]{:S(2)}) async-start(bf16[16,8,4224]{2,1,0:T(8,128)(2,1)} %fusion.1), calls=%async_computation.1 | async-start | bytes 2162688 | tf_op jit(solution)/shard_map/all_to_all | solution.py:211
  59.9 9.0 %collective-permute-start = (bf16[48,4224]{1,0:T(8,128)(2,1)S(1)}, bf16[48,4224]{1,0:T(8,128)(2,1)S(1)}, u32[]{:S(2)}, u32[]{:S(2)}) collective-permute-start(bf16[48,4224]{1,0:T(8,128)(2,1)S(1)} %pad_maximum_fusion.1.refs_2_), channel_id=1, source_target_pairs={{0,64},{64,128},{128,192},{192,256},{256,320},{320,384},{384,448},... | collective-permute-start | bytes 1216520 | tf_op jit(solution)/shard_map/ppermute | solution.py:257
  102.8 6.0 %collective-permute-done.5.refs_1_ = bf16[48,4224]{1,0:T(8,128)(2,1)S(1)} collective-permute-done((bf16[48,4224]{1,0:T(8,128)(2,1)}, bf16[48,4224]{1,0:T(8,128)(2,1)S(1)}, u32[]{:S(2)}, u32[]{:S(2)}) %collective-permute-start.5) | collective-permute-done | bytes 405536 | tf_op jit(solution)/shard_map/ppermute | solution.py:258
  111.8 6.7 %collective-permute-done.11.refs_1_ = bf16[48,4224]{1,0:T(8,128)(2,1)} collective-permute-done((bf16[48,4224]{1,0:T(8,128)(2,1)S(1)}, bf16[48,4224]{1,0:T(8,128)(2,1)}, u32[]{:S(2)}, u32[]{:S(2)}) %collective-permute-start.11) | collective-permute-done | bytes 405536 | tf_op jit(solution)/shard_map/ppermute | solution.py:258
  122.2 5.0 %collective-permute-done.9.refs_1_ = bf16[48,4224]{1,0:T(8,128)(2,1)} collective-permute-done((bf16[48,4224]{1,0:T(8,128)(2,1)S(1)}, bf16[48,4224]{1,0:T(8,128)(2,1)}, u32[]{:S(2)}, u32[]{:S(2)}) %collective-permute-start.9) | collective-permute-done | bytes 405536 | tf_op jit(solution)/shard_map/ppermute | solution.py:258
  138.8 5.0 %collective-permute-done.13.refs_1_ = bf16[48,4224]{1,0:T(8,128)(2,1)} collective-permute-done((bf16[48,4224]{1,0:T(8,128)(2,1)}, bf16[48,4224]{1,0:T(8,128)(2,1)}, u32[]{:S(2)}, u32[]{:S(2)}) %collective-permute-start.13) | collective-permute-done | bytes 405536 | tf_op jit(solution)/shard_map/ppermute | solution.py:258
  147.5 4.9 %collective-permute-done.19.refs_1_ = bf16[48,4224]{1,0:T(8,128)(2,1)} collective-permute-done((bf16[48,4224]{1,0:T(8,128)(2,1)}, bf16[48,4224]{1,0:T(8,128)(2,1)}, u32[]{:S(2)}, u32[]{:S(2)}) %collective-permute-start.19) | collective-permute-done | bytes 405536 | tf_op jit(solution)/shard_map/ppermute | solution.py:258
  162.0 5.0 %collective-permute-done.23.refs_1_ = bf16[48,4224]{1,0:T(8,128)(2,1)} collective-permute-done((bf16[48,4224]{1,0:T(8,128)(2,1)}, bf16[48,4224]{1,0:T(8,128)(2,1)}, u32[]{:S(2)}, u32[]{:S(2)}) %collective-permute-start.23) | collective-permute-done | bytes 405536 | tf_op jit(solution)/shard_map/ppermute | solution.py:258
  170.6 6.0 %collective-permute-done.21.refs_1_ = bf16[48,4224]{1,0:T(8,128)(2,1)} collective-permute-done((bf16[48,4224]{1,0:T(8,128)(2,1)}, bf16[48,4224]{1,0:T(8,128)(2,1)}, u32[]{:S(2)}, u32[]{:S(2)}) %collective-permute-start.21) | collective-permute-done | bytes 405536 | tf_op jit(solution)/shard_map/ppermute | solution.py:258
  181.8 4.5 %collective-permute-done.27.refs_1_ = bf16[48,4224]{1,0:T(8,128)(2,1)S(1)} collective-permute-done((bf16[48,4224]{1,0:T(8,128)(2,1)}, bf16[48,4224]{1,0:T(8,128)(2,1)S(1)}, u32[]{:S(2)}, u32[]{:S(2)}) %collective-permute-start.27) | collective-permute-done | bytes 405536 | tf_op jit(solution)/shard_map/ppermute | solution.py:258
  194.0 4.7 %collective-permute-done.29.refs_4_ = bf16[384,128]{1,0:T(8,128)(2,1)S(1)} collective-permute-done((bf16[384,128]{1,0:T(8,128)(2,1)S(1)}, bf16[384,128]{1,0:T(8,128)(2,1)S(1)}, u32[]{:S(2)}, u32[]{:S(2)}) %collective-permute-start.29) | collective-permute-done | bytes 98336 | tf_op jit(solution)/shard_map/ppermute | solution.py:288
  201.0 4.2 %collective-permute-start.36 = (bf16[384,128]{1,0:T(8,128)(2,1)S(1)}, bf16[384,128]{1,0:T(8,128)(2,1)S(1)}, u32[]{:S(2)}, u32[]{:S(2)}) collective-permute-start(bf16[384,128]{1,0:T(8,128)(2,1)S(1)} %shard_map.116.refs_0_), channel_id=1, source_target_pairs={{0,64},{64,128},{128,192},{192,256},{256,320},{320,384},{384,448},... | collective-permute-start | bytes 294920 | tf_op jit(solution)/shard_map/ppermute | solution.py:287
  220.5 4.7 %collective-permute-done.41.refs_4_ = bf16[384,128]{1,0:T(8,128)(2,1)S(1)} collective-permute-done((bf16[384,128]{1,0:T(8,128)(2,1)S(1)}, bf16[384,128]{1,0:T(8,128)(2,1)S(1)}, u32[]{:S(2)}, u32[]{:S(2)}) %collective-permute-start.41) | collective-permute-done | bytes 98336 | tf_op jit(solution)/shard_map/ppermute | solution.py:288
  233.2 4.9 %collective-permute-done.45.refs_6_ = bf16[384,128]{1,0:T(8,128)(2,1)S(1)} collective-permute-done((bf16[384,128]{1,0:T(8,128)(2,1)S(1)}, bf16[384,128]{1,0:T(8,128)(2,1)S(1)}, u32[]{:S(2)}, u32[]{:S(2)}) %collective-permute-start.45) | collective-permute-done | bytes 98336 | tf_op jit(solution)/shard_map/ppermute | solution.py:288
  242.4 8.9 %collective-permute-done.47.refs_14_ = bf16[384,128]{1,0:T(8,128)(2,1)S(1)} collective-permute-done((bf16[384,128]{1,0:T(8,128)(2,1)S(1)}, bf16[384,128]{1,0:T(8,128)(2,1)S(1)}, u32[]{:S(2)}, u32[]{:S(2)}) %collective-permute-start.47) | collective-permute-done | bytes 98336 | tf_op jit(solution)/shard_map/ppermute | solution.py:288
  254.1 6.4 %all-to-all-start.2 = ((bf16[16,8,8,512]{3,2,1,0:T(8,128)(2,1)}), bf16[16,8,8,512]{3,2,1,0:T(8,128)(2,1)}, u32[]{:S(2)}, u32[]{:S(2)}) async-start(bf16[16,8,8,512]{3,2,1,0:T(8,128)(2,1)} %bitcast.110), calls=%async_computation.2 | async-start | bytes 2097152 | tf_op jit(solution)/shard_map/all_to_all | solution.py:312
  280.2 4.2 %collective-permute-done.55.refs_14_ = bf16[384,128]{1,0:T(8,128)(2,1)S(1)} collective-permute-done((bf16[384,128]{1,0:T(8,128)(2,1)S(1)}, bf16[384,128]{1,0:T(8,128)(2,1)S(1)}, u32[]{:S(2)}, u32[]{:S(2)}) %collective-permute-start.55) | collective-permute-done | bytes 98336 | tf_op jit(solution)/shard_map/ppermute | solution.py:288
  287.2 6.2 %all-to-all-start.3 = ((bf16[16,8,8,512]{3,2,1,0:T(8,128)(2,1)}), bf16[16,8,8,512]{3,2,1,0:T(8,128)(2,1)S(1)}, u32[]{:S(2)}, u32[]{:S(2)}) async-start(bf16[16,8,8,512]{3,2,1,0:T(8,128)(2,1)} %bitcast.92), calls=%async_computation.3 | async-start | bytes 2097152 | tf_op jit(solution)/shard_map/all_to_all | solution.py:312
  296.7 8.5 %all-to-all-done.3 = bf16[16,8,8,512]{3,2,1,0:T(8,128)(2,1)S(1)} async-done(((bf16[16,8,8,512]{3,2,1,0:T(8,128)(2,1)}), bf16[16,8,8,512]{3,2,1,0:T(8,128)(2,1)S(1)}, u32[]{:S(2)}, u32[]{:S(2)}) %all-to-all-start.3) | async-done | bytes 1048608 | tf_op jit(solution)/shard_map/all_to_all | solution.py:312
  305.7 22.0 %all_to_all.30 = bf16[2,2,8,2,6,512]{5,2,4,1,3,0:T(8,128)(2,1)S(1)} all-to-all(bf16[2,2,8,2,6,512]{5,2,4,1,3,0:T(8,128)(2,1)S(1)} %copy.103), channel_id=1, replica_groups=mesh['dp'=8,'x'=4,'y'=4,'zh'=2,'core'=2] {'core'}, dimensions={0} | all-to-all | bytes 786432 | tf_op jit(solution)/shard_map/all_to_all | solution.py:338
  328.0 21.9 %all_to_all.31 = bf16[16,48,128]{2,1,0:T(8,128)(2,1)S(1)} all-to-all(bf16[16,48,128]{2,1,0:T(8,128)(2,1)S(1)} %reshape.439), channel_id=1, replica_groups=mesh['dp'=8,'x'=4,'y'=4,'zh'=2,'core'=2] {'zh','dp'}, dimensions={0} | all-to-all | bytes 393216 | tf_op jit(solution)/shard_map/all_to_all | solution.py:340
  (232 shorter events, 141.9 us)
Async XLA Ops:
  29.0 22.1 %all-to-all-start = ((bf16[16,8,4224]{2,1,0:T(8,128)(2,1)}), bf16[16,8,4224]{2,1,0:T(8,128)(2,1)S(1)}, u32[]{:S(2)}, u32[]{:S(2)}) async-start(bf16[16,8,4224]{2,1,0:T(8,128)(2,1)} %fusion), calls=%async_computation | async-start | bytes 2162688 | tf_op jit(solution)/shard_map/all_to_all | solution.py:211
  55.1 28.5 %all-to-all-start.1 = ((bf16[16,8,4224]{2,1,0:T(8,128)(2,1)}), bf16[16,8,4224]{2,1,0:T(8,128)(2,1)}, u32[]{:S(2)}, u32[]{:S(2)}) async-start(bf16[16,8,4224]{2,1,0:T(8,128)(2,1)} %fusion.1), calls=%async_computation.1 | async-start | bytes 2162688 | tf_op jit(solution)/shard_map/all_to_all | solution.py:211
  59.9 15.0 %collective-permute-start = (bf16[48,4224]{1,0:T(8,128)(2,1)S(1)}, bf16[48,4224]{1,0:T(8,128)(2,1)S(1)}, u32[]{:S(2)}, u32[]{:S(2)}) collective-permute-start(bf16[48,4224]{1,0:T(8,128)(2,1)S(1)} %pad_maximum_fusion.1.refs_2_), channel_id=1, source_target_pairs={{0,64},{64,128},{128,192},{192,256},{256,320},{320,384},{384,448},... | collective-permute-start | bytes 1216520 | tf_op jit(solution)/shard_map/ppermute | solution.py:257
  94.4 14.5 %collective-permute-start.5 = (bf16[48,4224]{1,0:T(8,128)(2,1)}, bf16[48,4224]{1,0:T(8,128)(2,1)S(1)}, u32[]{:S(2)}, u32[]{:S(2)}) collective-permute-start(bf16[48,4224]{1,0:T(8,128)(2,1)} %get-tuple-element.64), channel_id=1, source_target_pairs={{64,0},{128,64},{192,128},{256,192},{320,256},{65,1},{129,65},{193... | collective-permute-start | bytes 1216520 | tf_op jit(solution)/shard_map/ppermute | solution.py:258
  101.5 17.0 %collective-permute-start.11 = (bf16[48,4224]{1,0:T(8,128)(2,1)S(1)}, bf16[48,4224]{1,0:T(8,128)(2,1)}, u32[]{:S(2)}, u32[]{:S(2)}) collective-permute-start(bf16[48,4224]{1,0:T(8,128)(2,1)S(1)} %get-tuple-element.70), channel_id=1, source_target_pairs={{64,0},{128,64},{192,128},{256,192},{320,256},{384,320},{65,1},{12... | collective-permute-start | bytes 1216520 | tf_op jit(solution)/shard_map/ppermute | solution.py:258
  109.8 12.5 %collective-permute-start.8 = (bf16[48,4224]{1,0:T(8,128)(2,1)S(1)}, bf16[48,4224]{1,0:T(8,128)(2,1)S(1)}, u32[]{:S(2)}, u32[]{:S(2)}) collective-permute-start(bf16[48,4224]{1,0:T(8,128)(2,1)S(1)} %get-tuple-element.67), channel_id=1, source_target_pairs={{192,256},{256,320},{320,384},{384,448},{193,257},{257,321},{321,3... | collective-permute-start | bytes 1216520 | tf_op jit(solution)/shard_map/ppermute | solution.py:257
  110.5 16.7 %collective-permute-start.9 = (bf16[48,4224]{1,0:T(8,128)(2,1)S(1)}, bf16[48,4224]{1,0:T(8,128)(2,1)}, u32[]{:S(2)}, u32[]{:S(2)}) collective-permute-start(bf16[48,4224]{1,0:T(8,128)(2,1)S(1)} %get-tuple-element.68), channel_id=1, source_target_pairs={{64,0},{128,64},{192,128},{256,192},{65,1},{129,65},{193,129},{257... | collective-permute-start | bytes 1216520 | tf_op jit(solution)/shard_map/ppermute | solution.py:258
  120.9 14.1 %collective-permute-start.15 = (bf16[48,4224]{1,0:T(8,128)(2,1)}, bf16[48,4224]{1,0:T(8,128)(2,1)}, u32[]{:S(2)}, u32[]{:S(2)}) collective-permute-start(bf16[48,4224]{1,0:T(8,128)(2,1)} %get-tuple-element.76), channel_id=1, source_target_pairs={{64,0},{128,64},{192,128},{256,192},{320,256},{65,1},{129,65},{193... | collective-permute-start | bytes 1216520 | tf_op jit(solution)/shard_map/ppermute | solution.py:258
  129.6 14.1 %collective-permute-start.13 = (bf16[48,4224]{1,0:T(8,128)(2,1)}, bf16[48,4224]{1,0:T(8,128)(2,1)}, u32[]{:S(2)}, u32[]{:S(2)}) collective-permute-start(bf16[48,4224]{1,0:T(8,128)(2,1)} %get-tuple-element.74), channel_id=1, source_target_pairs={{64,0},{128,64},{192,128},{65,1},{129,65},{193,129},{66,2},{130,66... | collective-permute-start | bytes 1216520 | tf_op jit(solution)/shard_map/ppermute | solution.py:258
  137.5 14.9 %collective-permute-start.19 = (bf16[48,4224]{1,0:T(8,128)(2,1)}, bf16[48,4224]{1,0:T(8,128)(2,1)}, u32[]{:S(2)}, u32[]{:S(2)}) collective-permute-start(bf16[48,4224]{1,0:T(8,128)(2,1)} %get-tuple-element.82), channel_id=1, source_target_pairs={{64,0},{128,64},{192,128},{256,192},{65,1},{129,65},{193,129},{257... | collective-permute-start | bytes 1216520 | tf_op jit(solution)/shard_map/ppermute | solution.py:258
  146.2 12.1 %collective-permute-start.17 = (bf16[48,4224]{1,0:T(8,128)(2,1)}, bf16[48,4224]{1,0:T(8,128)(2,1)}, u32[]{:S(2)}, u32[]{:S(2)}) collective-permute-start(bf16[48,4224]{1,0:T(8,128)(2,1)} %get-tuple-element.80), channel_id=1, source_target_pairs={{64,0},{128,64},{65,1},{129,65},{66,2},{130,66},{67,3},{131,67},{6... | collective-permute-start | bytes 1216520 | tf_op jit(solution)/shard_map/ppermute | solution.py:258
  154.8 12.1 %collective-permute-start.23 = (bf16[48,4224]{1,0:T(8,128)(2,1)}, bf16[48,4224]{1,0:T(8,128)(2,1)}, u32[]{:S(2)}, u32[]{:S(2)}) collective-permute-start(bf16[48,4224]{1,0:T(8,128)(2,1)} %get-tuple-element.88), channel_id=1, source_target_pairs={{64,0},{128,64},{192,128},{65,1},{129,65},{193,129},{66,2},{130,66... | collective-permute-start | bytes 1216520 | tf_op jit(solution)/shard_map/ppermute | solution.py:258
  160.6 16.0 %collective-permute-start.21 = (bf16[48,4224]{1,0:T(8,128)(2,1)}, bf16[48,4224]{1,0:T(8,128)(2,1)}, u32[]{:S(2)}, u32[]{:S(2)}) collective-permute-start(bf16[48,4224]{1,0:T(8,128)(2,1)} %get-tuple-element.86), channel_id=1, source_target_pairs={{64,0},{65,1},{66,2},{67,3},{68,4},{69,5},{70,6},{71,7},{72,8},{73... | collective-permute-start | bytes 1216520 | tf_op jit(solution)/shard_map/ppermute | solution.py:258
  168.6 13.2 %collective-permute-start.26 = (bf16[48,4224]{1,0:T(8,128)(2,1)S(1)}, bf16[48,4224]{1,0:T(8,128)(2,1)S(1)}, u32[]{:S(2)}, u32[]{:S(2)}) collective-permute-start(bf16[48,4224]{1,0:T(8,128)(2,1)S(1)} %get-tuple-element.99), channel_id=1, source_target_pairs={{320,384},{384,448},{321,385},{385,449},{322,386},{386,450},{323,3... | collective-permute-start | bytes 1216520 | tf_op jit(solution)/shard_map/ppermute | solution.py:257
  169.3 17.0 %collective-permute-start.27 = (bf16[48,4224]{1,0:T(8,128)(2,1)}, bf16[48,4224]{1,0:T(8,128)(2,1)S(1)}, u32[]{:S(2)}, u32[]{:S(2)}) collective-permute-start(bf16[48,4224]{1,0:T(8,128)(2,1)} %get-tuple-element.100), channel_id=1, source_target_pairs={{64,0},{128,64},{65,1},{129,65},{66,2},{130,66},{67,3},{131,67},{6... | collective-permute-start | bytes 1216520 | tf_op jit(solution)/shard_map/ppermute | solution.py:258
  178.4 12.8 %collective-permute-start.24 = (bf16[384,128]{1,0:T(8,128)(2,1)S(1)}, bf16[384,128]{1,0:T(8,128)(2,1)S(1)}, u32[]{:S(2)}, u32[]{:S(2)}) collective-permute-start(bf16[384,128]{1,0:T(8,128)(2,1)S(1)} %shard_map.113.refs_0_), channel_id=1, source_target_pairs={{0,64},{64,128},{128,192},{192,256},{256,320},{320,384},{384,448},... | collective-permute-start | bytes 294920 | tf_op jit(solution)/shard_map/ppermute | solution.py:287
  187.2 12.7 %collective-permute-start.32 = (bf16[48,4224]{1,0:T(8,128)(2,1)S(1)}, bf16[48,4224]{1,0:T(8,128)(2,1)S(1)}, u32[]{:S(2)}, u32[]{:S(2)}) collective-permute-start(bf16[48,4224]{1,0:T(8,128)(2,1)S(1)} %get-tuple-element.102), channel_id=1, source_target_pairs={{384,448},{385,449},{386,450},{387,451},{388,452},{389,453},{390,4... | collective-permute-start | bytes 1216520 | tf_op jit(solution)/shard_map/ppermute | solution.py:257
  187.9 12.1 %collective-permute-start.33 = (bf16[48,4224]{1,0:T(8,128)(2,1)S(1)}, bf16[48,4224]{1,0:T(8,128)(2,1)S(1)}, u32[]{:S(2)}, u32[]{:S(2)}) collective-permute-start(bf16[48,4224]{1,0:T(8,128)(2,1)S(1)} %get-tuple-element.103), channel_id=1, source_target_pairs={{64,0},{65,1},{66,2},{67,3},{68,4},{69,5},{70,6},{71,7},{72,8},{73... | collective-permute-start | bytes 1216520 | tf_op jit(solution)/shard_map/ppermute | solution.py:258
  193.3 15.2 %collective-permute-start.30 = (bf16[384,128]{1,0:T(8,128)(2,1)S(1)}, bf16[384,128]{1,0:T(8,128)(2,1)S(1)}, u32[]{:S(2)}, u32[]{:S(2)}) collective-permute-start(bf16[384,128]{1,0:T(8,128)(2,1)S(1)} %collective-permute-done.28.refs_3_), channel_id=1, source_target_pairs={{128,192},{192,256},{256,320},{320,384},{384,448},{129,193},{193,2... | collective-permute-start | bytes 294920 | tf_op jit(solution)/shard_map/ppermute | solution.py:287
  214.5 12.7 %collective-permute-start.38 = (bf16[384,128]{1,0:T(8,128)(2,1)S(1)}, bf16[384,128]{1,0:T(8,128)(2,1)S(1)}, u32[]{:S(2)}, u32[]{:S(2)}) collective-permute-start(bf16[384,128]{1,0:T(8,128)(2,1)S(1)} %broadcast_select_fusion.5), channel_id=1, source_target_pairs={{256,320},{320,384},{384,448},{257,321},{321,385},{385,449},{258,3... | collective-permute-start | bytes 294920 | tf_op jit(solution)/shard_map/ppermute | solution.py:287
  217.2 12.7 %collective-permute-start.39 = (bf16[384,128]{1,0:T(8,128)(2,1)S(1)}, bf16[384,128]{1,0:T(8,128)(2,1)S(1)}, u32[]{:S(2)}, u32[]{:S(2)}) collective-permute-start(bf16[384,128]{1,0:T(8,128)(2,1)S(1)} %broadcast_select_fusion.4), channel_id=1, source_target_pairs={{64,0},{128,64},{192,128},{65,1},{129,65},{193,129},{66,2},{130,66... | collective-permute-start | bytes 294920 | tf_op jit(solution)/shard_map/ppermute | solution.py:288
  227.2 12.8 %collective-permute-start.42 = (bf16[384,128]{1,0:T(8,128)(2,1)S(1)}, bf16[384,128]{1,0:T(8,128)(2,1)S(1)}, u32[]{:S(2)}, u32[]{:S(2)}) collective-permute-start(bf16[384,128]{1,0:T(8,128)(2,1)S(1)} %broadcast_select_fusion.3), channel_id=1, source_target_pairs={{320,384},{384,448},{321,385},{385,449},{322,386},{386,450},{323,3... | collective-permute-start | bytes 294920 | tf_op jit(solution)/shard_map/ppermute | solution.py:287
  254.1 33.1 %all-to-all-start.2 = ((bf16[16,8,8,512]{3,2,1,0:T(8,128)(2,1)}), bf16[16,8,8,512]{3,2,1,0:T(8,128)(2,1)}, u32[]{:S(2)}, u32[]{:S(2)}) async-start(bf16[16,8,8,512]{3,2,1,0:T(8,128)(2,1)} %bitcast.110), calls=%async_computation.2 | async-start | bytes 2097152 | tf_op jit(solution)/shard_map/all_to_all | solution.py:312
  287.2 18.0 %all-to-all-start.3 = ((bf16[16,8,8,512]{3,2,1,0:T(8,128)(2,1)}), bf16[16,8,8,512]{3,2,1,0:T(8,128)(2,1)S(1)}, u32[]{:S(2)}, u32[]{:S(2)}) async-start(bf16[16,8,8,512]{3,2,1,0:T(8,128)(2,1)} %bitcast.92), calls=%async_computation.3 | async-start | bytes 2097152 | tf_op jit(solution)/shard_map/all_to_all | solution.py:312
  (39 other events, 343.1 us)

commit v10 on v4

--- a/solution.py
+++ b/solution.py
@@ -163,23 +163,22 @@
     line = jnp.arange(boxes, dtype=jnp.int32)
     lower = (line[:, None] < line[None, :]).astype(BF)
 
-    send = []
-    for step in range(steps):
-        local = held[step]
+    def exchange(local, after=None):
         place = places(local[:, model:], me, columns, quad, tok, top)[1]
-        send.append(
-            lax.dot_general(
-                place.astype(BF), local, (((0,), (0,)), ((), ())), preferred_element_type=F32
-            )
-            .astype(BF)
-            .reshape(columns, quad * MOST, wide)
-        )
-    received = lax.all_to_all(
-        jnp.concatenate(send, axis=1), ("x", "y"), split_axis=0, concat_axis=0, tiled=True
-    )
-
-    def compacted(step):
-        arrived = received[:, step * quad * MOST : (step + 1) * quad * MOST].reshape(boxes, wide)
+        if after is not None:
+            place = place & after
+        send = lax.dot_general(
+            place.astype(BF), local, (((0,), (0,)), ((), ())), preferred_element_type=F32
+        ).astype(BF)
+        return lax.all_to_all(
+            send.reshape(columns, quad * MOST, wide),
+            ("x", "y"),
+            split_axis=0,
+            concat_axis=0,
+            tiled=True,
+        ).reshape(boxes, wide)
+
+    def compacted(step, arrived, after=None):
         valid = arrived[:, model + ONE]
         rank = jnp.dot(valid[None, :], lower, preferred_element_type=F32)
         which = (jnp.arange(n_dp, dtype=jnp.int32)[:, None] == my_dp) & (
@@ -187,6 +186,8 @@
         )
         limit = jnp.sum(jnp.where(which, slot_rows[step], 0)).astype(F32)
         kept = (valid[None, :] > 0) & (rank < limit)
+        if after is not None:
+            kept = kept & after
         slot_row = jnp.arange(ROWS, dtype=jnp.int32).astype(F32)[:, None]
         chosen = kept & (rank == slot_row)
         pick = chosen.astype(BF)
@@ -200,29 +201,42 @@
 
     both_w = jnp.concatenate([gate_w[0], up_w[0]], axis=1)
     batch = steps * n_dp
-    own = [compacted(step) for step in range(steps)]
-    to_right, to_left = list(own), list(own)
+    last = n_dp - 1
+    own = [None] * steps
+    to_right, to_left = [None] * steps, [None] * steps
     done = [[[] for _ in range(n_dp)] for _ in range(steps)]
     far = [[None] * n_dp for _ in range(steps)]
-    hidden = None
-    for j in range(1, n_dp):
-        for s in range(steps):
-            to_right[s] = lax.ppermute(to_right[s], "dp", right[j - 1])
-            to_left[s] = lax.ppermute(to_left[s], "dp", left[j - 1])
-            blocks = [to_right[s], to_left[s]] + ([own[s]] if j == 1 else [])
-            passed = 2 if j < n_dp - 1 else 0
-            extra = [hidden] if j == EARLY + 1 and s == 0 else []
-            sent, made = project(both_w, blocks, passed, extra)
-            if passed:
-                to_right[s], to_left[s] = sent
-            if j > EARLY:
-                far[s][j] = made[0][:, :LANES] + made[1][:, :LANES]
-            done[s][j].append(made[0])
-            done[s][n_dp - j].append(made[1])
-            if j == 1:
-                done[s][0].append(made[2])
-        if j == EARLY:
-            hidden = assemble(done, 0, my_dp)
+    own[0] = compacted(0, exchange(held[0]))
+    to_right[0], to_left[0] = own[0], own[0]
+    arrived = exchange(held[1], own[0][0, 0] == own[0][0, 0])
+    order = [(1, 0)]
+    for j in range(2, n_dp):
+        order += [(j, 0), (j - 1, 1)]
+    order.append((last, 1))
+    hidden, made, extra = None, None, []
+    for j, s in order:
+        if (j, s) == (2, 0):
+            own[1] = compacted(1, arrived, made[0][0, 0] == made[0][0, 0])
+            to_right[1], to_left[1] = own[1], own[1]
+        to_right[s] = lax.ppermute(to_right[s], "dp", right[j - 1])
+        to_left[s] = lax.ppermute(to_left[s], "dp", left[j - 1])
+        blocks = [to_right[s], to_left[s]] + ([own[s]] if j == 1 else [])
+        passed = 2 if j < last else 0
+        sent, made = project(both_w, blocks, passed, extra)
+        extra = [made[0]]
+        if passed:
+            to_right[s], to_left[s] = sent
+        if j > EARLY:
+            far[s][j] = made[0][:, :LANES] + made[1][:, :LANES]
+        done[s][j].append(made[0])
+        done[s][n_dp - j].append(made[1])
+        if j == 1:
+            done[s][0].append(made[2])
+        if (j, s) == (EARLY, 0):
+            near = [list(parts) for parts in done[0]]
+        if (j, s) == (EARLY, 1):
+            hidden = assemble([near, done[1]], 0, my_dp)
+            extra = [made[0], hidden]
     gathered = lax.all_gather(hidden, "dp", axis=0, tiled=False).reshape(
         n_dp, steps, n_dp, ROWS, LANES
     )

time: 343 us -> 349 us (1.017)
  waiting for transfers between devices: 143 us -> 129 us
  local copies, waits for them, and re-layouts: 24.6 us -> 30.6 us
    all_to_all x1 -> x2, waiting for transfers between devices: 25.7 us -> 12.2 us  [exchange(): lax.all_to_all(send.reshape(columns, quad * MOST, wide), ('x', 'y'), spli...]
    ppermute x14, waiting for transfers between devices: 8.05 us -> 2.94 us  [on_device(): to_right[s] = lax.ppermute(to_right[s], 'dp', right[j - 1])]
    unnamed x141 -> x149, local copies, waits for them, and re-layouts: 12.5 us -> 17 us
    all_to_all x1 -> x2, starting transfers between devices: 5.66 us -> 9.94 us  [exchange(): lax.all_to_all(send.reshape(columns, quad * MOST, wide), ('x', 'y'), spli...]
    ppermute x14, starting transfers between devices: 28.1 us -> 24.3 us  [on_device(): to_right[s] = lax.ppermute(to_right[s], 'dp', right[j - 1])]
    all_to_all x1, waiting for transfers between devices: 14.9 us -> 18.4 us  [on_device(): lax.all_to_all(jnp.broadcast_to(rest.reshape(1, steps * len(beyond) * ROW...]
  transfers between devices with their start and end apart: 32 -> 33, of which waited for: 18 -> 18; matrix products, arithmetic and copies ran while one was open for 3% -> 5% of each run, Pallas kernels for 6% -> 6%
where the time goes in v10:
time: 349 us; the launch traced here: 343 us
  waiting for transfers between devices  129 us (37%)
  starting transfers between devices  63.6 us (18%)
  blocking collectives  56.3 us (16%)
  local copies, waits for them, and re-layouts  30.6 us (9%)
  Pallas kernels  22.3 us (6%)
  between operations  18.8 us (5%)
  other arithmetic  11.3 us (3%)
  matrix products  11.2 us (3%)
    ppermute x14, waiting for transfers between devices, on_device(): to_left[s] = lax.ppermute(to_left[s], 'dp', left[j - 1])  61.1 us
    ppermute x14, starting transfers between devices, on_device(): to_right[s] = lax.ppermute(to_right[s], 'dp', right[j - 1])  24.3 us
    all_to_all x1, blocking collectives, on_device(): lax.all_to_all(halves.reshape(2 * n_dp, mine * width // LANES, LANES), ('...  23.9 us
    all_gather x1, blocking collectives, on_device(): lax.all_gather(packed.reshape(steps, tok, wide), ('zh', 'core'), axis=1,...  21.7 us
    pallas_call x14, Pallas kernels, project(): pl.pallas_call(functools.partial(project_kernel, count, passed, len(extra...  21.5 us
    all_to_all x1, waiting for transfers between devices, on_device(): lax.all_to_all(spread.reshape(batch, columns, quad * MOST, width).transpo...  19.2 us
    all_to_all x1, waiting for transfers between devices, on_device(): lax.all_to_all(jnp.broadcast_to(rest.reshape(1, steps * len(beyond) * ROW...  18.4 us
    ppermute x14, starting transfers between devices, on_device(): to_left[s] = lax.ppermute(to_left[s], 'dp', left[j - 1])  18.2 us
  transfers between devices with their start and end apart: 33, of which 18 were waited for; matrix products, arithmetic and copies ran while one was open for 5% of the time, Pallas kernels for 6%

profile of v10, /device:TPU:1, one launch (start us, length us, event | category | flops | bytes accessed | tf_op | source)
XLA Modules:
  0.0 343.4 jit_solution(13308732756586228749)
XLA Ops:
  11.4 21.7 %all_gather.9 = bf16[2,24,4224]{2,0,1:T(2,128)(2,1)S(1)} all-gather(bf16[2,6,4224]{2,0,1:T(2,128)(2,1)S(1)} %pad_maximum_fusion.3), channel_id=1, replica_groups=mesh['dp'=8,'x'=4,'y'=4,'zh'=2,'core'=2] {'zh','core'}, dimensions={1}, use_global_device_ids=true | all-gather | bytes 506880 | tf_op jit(solution)/shard_map/all_gather | solution.py:157
  35.6 5.5 %all-to-all-start = ((bf16[16,8,4224]{2,1,0:T(8,128)(2,1)}), bf16[16,8,4224]{2,1,0:T(8,128)(2,1)S(1)}, u32[]{:S(2)}, u32[]{:S(2)}) async-start(bf16[16,8,4224]{2,1,0:T(8,128)(2,1)} %fusion), calls=%async_computation | async-start | bytes 2162688 | tf_op jit(solution)/shard_map/all_to_all | solution.py:173
  45.4 12.2 %all-to-all-done = bf16[16,8,4224]{2,1,0:T(8,128)(2,1)S(1)} async-done(((bf16[16,8,4224]{2,1,0:T(8,128)(2,1)}), bf16[16,8,4224]{2,1,0:T(8,128)(2,1)S(1)}, u32[]{:S(2)}, u32[]{:S(2)}) %all-to-all-start) | async-done | bytes 1081376 | tf_op jit(solution)/shard_map/all_to_all | solution.py:173
  62.1 4.4 %all-to-all-start.1 = ((bf16[16,8,4224]{2,1,0:T(8,128)(2,1)}), bf16[16,8,4224]{2,1,0:T(8,128)(2,1)}, u32[]{:S(2)}, u32[]{:S(2)}) async-start(bf16[16,8,4224]{2,1,0:T(8,128)(2,1)} %fusion.1), calls=%async_computation.1 | async-start | bytes 2162688 | tf_op jit(solution)/shard_map/all_to_all | solution.py:173
  66.7 9.0 %collective-permute-start = (bf16[48,4224]{1,0:T(8,128)(2,1)S(1)}, bf16[48,4224]{1,0:T(8,128)(2,1)S(1)}, u32[]{:S(2)}, u32[]{:S(2)}) collective-permute-start(bf16[48,4224]{1,0:T(8,128)(2,1)S(1)} %pad_maximum_fusion.1.refs_2_), channel_id=1, source_target_pairs={{0,64},{64,128},{128,192},{192,256},{256,320},{320,384},{384,448},... | collective-permute-start | bytes 1216520 | tf_op jit(solution)/shard_map/ppermute | solution.py:221
  81.6 4.0 %collective-permute-done.1.refs_1_ = bf16[48,4224]{1,0:T(8,128)(2,1)} collective-permute-done((bf16[48,4224]{1,0:T(8,128)(2,1)S(1)}, bf16[48,4224]{1,0:T(8,128)(2,1)}, u32[]{:S(2)}, u32[]{:S(2)}) %collective-permute-start.1) | collective-permute-done | bytes 405536 | tf_op jit(solution)/shard_map/ppermute | solution.py:222
  97.9 4.0 %collective-permute-start.6 = (bf16[48,4224]{1,0:T(8,128)(2,1)S(1)}, bf16[48,4224]{1,0:T(8,128)(2,1)S(1)}, u32[]{:S(2)}, u32[]{:S(2)}) collective-permute-start(bf16[48,4224]{1,0:T(8,128)(2,1)S(1)} %pad_maximum_fusion.2.refs_2_), channel_id=1, source_target_pairs={{0,64},{64,128},{128,192},{192,256},{256,320},{320,384},{384,448},... | collective-permute-start | bytes 1216520 | tf_op jit(solution)/shard_map/ppermute | solution.py:221
  106.9 3.7 %collective-permute-done.7.refs_1_ = bf16[48,4224]{1,0:T(8,128)(2,1)S(1)} collective-permute-done((bf16[48,4224]{1,0:T(8,128)(2,1)S(1)}, bf16[48,4224]{1,0:T(8,128)(2,1)S(1)}, u32[]{:S(2)}, u32[]{:S(2)}) %collective-permute-start.7) | collective-permute-done | bytes 405536 | tf_op jit(solution)/shard_map/ppermute | solution.py:222
  113.8 5.6 %collective-permute-done.5.refs_1_ = bf16[48,4224]{1,0:T(8,128)(2,1)S(1)} collective-permute-done((bf16[48,4224]{1,0:T(8,128)(2,1)}, bf16[48,4224]{1,0:T(8,128)(2,1)S(1)}, u32[]{:S(2)}, u32[]{:S(2)}) %collective-permute-start.5) | collective-permute-done | bytes 405536 | tf_op jit(solution)/shard_map/ppermute | solution.py:222
  122.4 7.1 %collective-permute-done.11.refs_1_ = bf16[48,4224]{1,0:T(8,128)(2,1)} collective-permute-done((bf16[48,4224]{1,0:T(8,128)(2,1)S(1)}, bf16[48,4224]{1,0:T(8,128)(2,1)}, u32[]{:S(2)}, u32[]{:S(2)}) %collective-permute-start.11) | collective-permute-done | bytes 405536 | tf_op jit(solution)/shard_map/ppermute | solution.py:222
  133.2 4.9 %collective-permute-done.9.refs_1_ = bf16[48,4224]{1,0:T(8,128)(2,1)} collective-permute-done((bf16[48,4224]{1,0:T(8,128)(2,1)S(1)}, bf16[48,4224]{1,0:T(8,128)(2,1)}, u32[]{:S(2)}, u32[]{:S(2)}) %collective-permute-start.9) | collective-permute-done | bytes 405536 | tf_op jit(solution)/shard_map/ppermute | solution.py:222
  141.9 4.3 %collective-permute-done.15.refs_1_ = bf16[48,4224]{1,0:T(8,128)(2,1)} collective-permute-done((bf16[48,4224]{1,0:T(8,128)(2,1)}, bf16[48,4224]{1,0:T(8,128)(2,1)}, u32[]{:S(2)}, u32[]{:S(2)}) %collective-permute-start.15) | collective-permute-done | bytes 405536 | tf_op jit(solution)/shard_map/ppermute | solution.py:222
  150.0 4.9 %collective-permute-done.13.refs_1_ = bf16[48,4224]{1,0:T(8,128)(2,1)} collective-permute-done((bf16[48,4224]{1,0:T(8,128)(2,1)}, bf16[48,4224]{1,0:T(8,128)(2,1)}, u32[]{:S(2)}, u32[]{:S(2)}) %collective-permute-start.13) | collective-permute-done | bytes 405536 | tf_op jit(solution)/shard_map/ppermute | solution.py:222
  159.4 3.6 %collective-permute-done.19.refs_1_ = bf16[48,4224]{1,0:T(8,128)(2,1)} collective-permute-done((bf16[48,4224]{1,0:T(8,128)(2,1)}, bf16[48,4224]{1,0:T(8,128)(2,1)}, u32[]{:S(2)}, u32[]{:S(2)}) %collective-permute-start.19) | collective-permute-done | bytes 405536 | tf_op jit(solution)/shard_map/ppermute | solution.py:222
  173.9 3.6 %collective-permute-done.23.refs_1_ = bf16[48,4224]{1,0:T(8,128)(2,1)} collective-permute-done((bf16[48,4224]{1,0:T(8,128)(2,1)}, bf16[48,4224]{1,0:T(8,128)(2,1)}, u32[]{:S(2)}, u32[]{:S(2)}) %collective-permute-start.23) | collective-permute-done | bytes 405536 | tf_op jit(solution)/shard_map/ppermute | solution.py:222
  190.1 7.3 %collective-permute-done.25.refs_1_ = bf16[48,4224]{1,0:T(8,128)(2,1)} collective-permute-done((bf16[48,4224]{1,0:T(8,128)(2,1)}, bf16[48,4224]{1,0:T(8,128)(2,1)}, u32[]{:S(2)}, u32[]{:S(2)}) %collective-permute-start.25) | collective-permute-done | bytes 405536 | tf_op jit(solution)/shard_map/ppermute | solution.py:222
  201.3 7.4 %collective-permute-done.27.refs_1_ = bf16[48,4224]{1,0:T(8,128)(2,1)S(1)} collective-permute-done((bf16[48,4224]{1,0:T(8,128)(2,1)}, bf16[48,4224]{1,0:T(8,128)(2,1)S(1)}, u32[]{:S(2)}, u32[]{:S(2)}) %collective-permute-start.27) | collective-permute-done | bytes 405536 | tf_op jit(solution)/shard_map/ppermute | solution.py:222
  211.5 5.2 %all-to-all-start.2 = ((bf16[8,192,128]{2,1,0:T(8,128)(2,1)}), bf16[8,192,128]{2,1,0:T(8,128)(2,1)S(1)}, u32[]{:S(2)}, u32[]{:S(2)}) async-start(bf16[8,192,128]{2,1,0:T(8,128)(2,1)} %broadcast_in_dim.331), calls=%async_computation.2 | async-start | bytes 786432 | tf_op jit(solution)/shard_map/all_to_all | solution.py:245
  227.8 18.4 %all-to-all-done.2 = bf16[8,192,128]{2,1,0:T(8,128)(2,1)S(1)} async-done(((bf16[8,192,128]{2,1,0:T(8,128)(2,1)}), bf16[8,192,128]{2,1,0:T(8,128)(2,1)S(1)}, u32[]{:S(2)}, u32[]{:S(2)}) %all-to-all-start.2) | async-done | bytes 393248 | tf_op jit(solution)/shard_map/all_to_all | solution.py:245
  246.2 15.5 %all-gather.3.cloned.1.call-done = bf16[6144,128]{1,0:T(8,128)(2,1)} async-done(((bf16[768,128]{1,0:T(8,128)(2,1)}), bf16[6144,128]{1,0:T(8,128)(2,1)}) %all-gather.3.cloned.1.call-update) | async-done | bytes 1572880 | tf_op jit(solution)/shard_map/all_gather | solution.py:240
  270.6 5.9 %all-to-all-start.3 = ((bf16[16,16,8,512]{3,2,1,0:T(8,128)(2,1)}), bf16[16,16,8,512]{3,2,1,0:T(8,128)(2,1)S(1)}, u32[]{:S(2)}, u32[]{:S(2)}) async-start(bf16[16,16,8,512]{3,2,1,0:T(8,128)(2,1)} %bitcast.97), calls=%async_computation.3 | async-start | bytes 4194304 | tf_op jit(solution)/shard_map/all_to_all | solution.py:279
  280.6 19.2 %all-to-all-done.3 = bf16[16,16,8,512]{3,2,1,0:T(8,128)(2,1)S(1)} async-done(((bf16[16,16,8,512]{3,2,1,0:T(8,128)(2,1)}), bf16[16,16,8,512]{3,2,1,0:T(8,128)(2,1)S(1)}, u32[]{:S(2)}, u32[]{:S(2)}) %all-to-all-start.3) | async-done | bytes 2097184 | tf_op jit(solution)/shard_map/all_to_all | solution.py:279
  300.4 10.7 %all_to_all.30 = bf16[2,2,8,2,6,512]{5,2,3,4,1,0:T(8,128)(2,1)S(1)} all-to-all(bf16[2,2,8,2,6,512]{5,2,3,4,1,0:T(8,128)(2,1)S(1)} %copy.93), channel_id=1, replica_groups=mesh['dp'=8,'x'=4,'y'=4,'zh'=2,'core'=2] {'core'}, dimensions={0} | all-to-all | bytes 786432 | tf_op jit(solution)/shard_map/all_to_all | solution.py:305
  311.4 23.9 %all_to_all.31 = bf16[16,48,128]{2,1,0:T(8,128)(2,1)S(1)} all-to-all(bf16[16,48,128]{2,1,0:T(8,128)(2,1)S(1)} %reshape.400), channel_id=1, replica_groups=mesh['dp'=8,'x'=4,'y'=4,'zh'=2,'core'=2] {'zh','dp'}, dimensions={0} | all-to-all | bytes 393216 | tf_op jit(solution)/shard_map/all_to_all | solution.py:307
  (299 shorter events, 112.6 us)
Async XLA Ops:
  35.6 22.0 %all-to-all-start = ((bf16[16,8,4224]{2,1,0:T(8,128)(2,1)}), bf16[16,8,4224]{2,1,0:T(8,128)(2,1)S(1)}, u32[]{:S(2)}, u32[]{:S(2)}) async-start(bf16[16,8,4224]{2,1,0:T(8,128)(2,1)} %fusion), calls=%async_computation | async-start | bytes 2162688 | tf_op jit(solution)/shard_map/all_to_all | solution.py:173
  62.1 31.6 %all-to-all-start.1 = ((bf16[16,8,4224]{2,1,0:T(8,128)(2,1)}), bf16[16,8,4224]{2,1,0:T(8,128)(2,1)}, u32[]{:S(2)}, u32[]{:S(2)}) async-start(bf16[16,8,4224]{2,1,0:T(8,128)(2,1)} %fusion.1), calls=%async_computation.1 | async-start | bytes 2162688 | tf_op jit(solution)/shard_map/all_to_all | solution.py:173
  66.5 195.2 %all-gather.3.cloned.1.call-start = ((), (), s32[]{:S(2)}) async-start(), calls=%async_computation.6 | async-start | bytes 1769472 | tf_op jit(solution)/shard_map/all_gather | solution.py:240
  66.7 15.0 %collective-permute-start = (bf16[48,4224]{1,0:T(8,128)(2,1)S(1)}, bf16[48,4224]{1,0:T(8,128)(2,1)S(1)}, u32[]{:S(2)}, u32[]{:S(2)}) collective-permute-start(bf16[48,4224]{1,0:T(8,128)(2,1)S(1)} %pad_maximum_fusion.1.refs_2_), channel_id=1, source_target_pairs={{0,64},{64,128},{128,192},{192,256},{256,320},{320,384},{384,448},... | collective-permute-start | bytes 1216520 | tf_op jit(solution)/shard_map/ppermute | solution.py:221
  88.5 14.7 %collective-permute-start.2 = (bf16[48,4224]{1,0:T(8,128)(2,1)S(1)}, bf16[48,4224]{1,0:T(8,128)(2,1)}, u32[]{:S(2)}, u32[]{:S(2)}) collective-permute-start(bf16[48,4224]{1,0:T(8,128)(2,1)S(1)} %get-tuple-element.61), channel_id=1, source_target_pairs={{64,128},{128,192},{192,256},{256,320},{320,384},{384,448},{65,129... | collective-permute-start | bytes 1216520 | tf_op jit(solution)/shard_map/ppermute | solution.py:221
  89.9 13.3 %collective-permute-start.3 = (bf16[48,4224]{1,0:T(8,128)(2,1)}, bf16[48,4224]{1,0:T(8,128)(2,1)}, u32[]{:S(2)}, u32[]{:S(2)}) collective-permute-start(bf16[48,4224]{1,0:T(8,128)(2,1)} %get-tuple-element.62), channel_id=1, source_target_pairs={{64,0},{128,64},{192,128},{256,192},{320,256},{384,320},{65,1},{12... | collective-permute-start | bytes 1216520 | tf_op jit(solution)/shard_map/ppermute | solution.py:222
  105.6 13.8 %collective-permute-start.5 = (bf16[48,4224]{1,0:T(8,128)(2,1)}, bf16[48,4224]{1,0:T(8,128)(2,1)S(1)}, u32[]{:S(2)}, u32[]{:S(2)}) collective-permute-start(bf16[48,4224]{1,0:T(8,128)(2,1)} %get-tuple-element.64), channel_id=1, source_target_pairs={{64,0},{128,64},{192,128},{256,192},{320,256},{65,1},{129,65},{193... | collective-permute-start | bytes 1216520 | tf_op jit(solution)/shard_map/ppermute | solution.py:222
  111.8 10.6 %collective-permute-start.10 = (bf16[48,4224]{1,0:T(8,128)(2,1)S(1)}, bf16[48,4224]{1,0:T(8,128)(2,1)S(1)}, u32[]{:S(2)}, u32[]{:S(2)}) collective-permute-start(bf16[48,4224]{1,0:T(8,128)(2,1)S(1)} %get-tuple-element.69), channel_id=1, source_target_pairs={{64,128},{128,192},{192,256},{256,320},{320,384},{384,448},{65,129... | collective-permute-start | bytes 1216520 | tf_op jit(solution)/shard_map/ppermute | solution.py:221
  112.5 17.0 %collective-permute-start.11 = (bf16[48,4224]{1,0:T(8,128)(2,1)S(1)}, bf16[48,4224]{1,0:T(8,128)(2,1)}, u32[]{:S(2)}, u32[]{:S(2)}) collective-permute-start(bf16[48,4224]{1,0:T(8,128)(2,1)S(1)} %get-tuple-element.70), channel_id=1, source_target_pairs={{64,0},{128,64},{192,128},{256,192},{320,256},{384,320},{65,1},{12... | collective-permute-start | bytes 1216520 | tf_op jit(solution)/shard_map/ppermute | solution.py:222
  120.4 12.9 %collective-permute-start.8 = (bf16[48,4224]{1,0:T(8,128)(2,1)S(1)}, bf16[48,4224]{1,0:T(8,128)(2,1)S(1)}, u32[]{:S(2)}, u32[]{:S(2)}) collective-permute-start(bf16[48,4224]{1,0:T(8,128)(2,1)S(1)} %get-tuple-element.67), channel_id=1, source_target_pairs={{192,256},{256,320},{320,384},{384,448},{193,257},{257,321},{321,3... | collective-permute-start | bytes 1216520 | tf_op jit(solution)/shard_map/ppermute | solution.py:221
  121.1 17.1 %collective-permute-start.9 = (bf16[48,4224]{1,0:T(8,128)(2,1)S(1)}, bf16[48,4224]{1,0:T(8,128)(2,1)}, u32[]{:S(2)}, u32[]{:S(2)}) collective-permute-start(bf16[48,4224]{1,0:T(8,128)(2,1)S(1)} %get-tuple-element.68), channel_id=1, source_target_pairs={{64,0},{128,64},{192,128},{256,192},{65,1},{129,65},{193,129},{257... | collective-permute-start | bytes 1216520 | tf_op jit(solution)/shard_map/ppermute | solution.py:222
  131.2 10.7 %collective-permute-start.14 = (bf16[48,4224]{1,0:T(8,128)(2,1)S(1)}, bf16[48,4224]{1,0:T(8,128)(2,1)S(1)}, u32[]{:S(2)}, u32[]{:S(2)}) collective-permute-start(bf16[48,4224]{1,0:T(8,128)(2,1)S(1)} %get-tuple-element.75), channel_id=1, source_target_pairs={{128,192},{192,256},{256,320},{320,384},{384,448},{129,193},{193,2... | collective-permute-start | bytes 1216520 | tf_op jit(solution)/shard_map/ppermute | solution.py:221
  131.9 14.3 %collective-permute-start.15 = (bf16[48,4224]{1,0:T(8,128)(2,1)}, bf16[48,4224]{1,0:T(8,128)(2,1)}, u32[]{:S(2)}, u32[]{:S(2)}) collective-permute-start(bf16[48,4224]{1,0:T(8,128)(2,1)} %get-tuple-element.76), channel_id=1, source_target_pairs={{64,0},{128,64},{192,128},{256,192},{320,256},{65,1},{129,65},{193... | collective-permute-start | bytes 1216520 | tf_op jit(solution)/shard_map/ppermute | solution.py:222
  140.6 14.3 %collective-permute-start.13 = (bf16[48,4224]{1,0:T(8,128)(2,1)}, bf16[48,4224]{1,0:T(8,128)(2,1)}, u32[]{:S(2)}, u32[]{:S(2)}) collective-permute-start(bf16[48,4224]{1,0:T(8,128)(2,1)} %get-tuple-element.74), channel_id=1, source_target_pairs={{64,0},{128,64},{192,128},{65,1},{129,65},{193,129},{66,2},{130,66... | collective-permute-start | bytes 1216520 | tf_op jit(solution)/shard_map/ppermute | solution.py:222
  148.0 11.4 %collective-permute-start.18 = (bf16[48,4224]{1,0:T(8,128)(2,1)S(1)}, bf16[48,4224]{1,0:T(8,128)(2,1)S(1)}, u32[]{:S(2)}, u32[]{:S(2)}) collective-permute-start(bf16[48,4224]{1,0:T(8,128)(2,1)S(1)} %get-tuple-element.81), channel_id=1, source_target_pairs={{192,256},{256,320},{320,384},{384,448},{193,257},{257,321},{321,3... | collective-permute-start | bytes 1216520 | tf_op jit(solution)/shard_map/ppermute | solution.py:221
  148.7 14.3 %collective-permute-start.19 = (bf16[48,4224]{1,0:T(8,128)(2,1)}, bf16[48,4224]{1,0:T(8,128)(2,1)}, u32[]{:S(2)}, u32[]{:S(2)}) collective-permute-start(bf16[48,4224]{1,0:T(8,128)(2,1)} %get-tuple-element.82), channel_id=1, source_target_pairs={{64,0},{128,64},{192,128},{256,192},{65,1},{129,65},{193,129},{257... | collective-permute-start | bytes 1216520 | tf_op jit(solution)/shard_map/ppermute | solution.py:222
  156.7 10.8 %collective-permute-start.16 = (bf16[48,4224]{1,0:T(8,128)(2,1)S(1)}, bf16[48,4224]{1,0:T(8,128)(2,1)}, u32[]{:S(2)}, u32[]{:S(2)}) collective-permute-start(bf16[48,4224]{1,0:T(8,128)(2,1)S(1)} %get-tuple-element.79), channel_id=1, source_target_pairs={{320,384},{384,448},{321,385},{385,449},{322,386},{386,450},{323,3... | collective-permute-start | bytes 1216520 | tf_op jit(solution)/shard_map/ppermute | solution.py:221
  158.1 11.4 %collective-permute-start.17 = (bf16[48,4224]{1,0:T(8,128)(2,1)}, bf16[48,4224]{1,0:T(8,128)(2,1)}, u32[]{:S(2)}, u32[]{:S(2)}) collective-permute-start(bf16[48,4224]{1,0:T(8,128)(2,1)} %get-tuple-element.80), channel_id=1, source_target_pairs={{64,0},{128,64},{65,1},{129,65},{66,2},{130,66},{67,3},{131,67},{6... | collective-permute-start | bytes 1216520 | tf_op jit(solution)/shard_map/ppermute | solution.py:222
  166.2 11.3 %collective-permute-start.23 = (bf16[48,4224]{1,0:T(8,128)(2,1)}, bf16[48,4224]{1,0:T(8,128)(2,1)}, u32[]{:S(2)}, u32[]{:S(2)}) collective-permute-start(bf16[48,4224]{1,0:T(8,128)(2,1)} %get-tuple-element.88), channel_id=1, source_target_pairs={{64,0},{128,64},{192,128},{65,1},{129,65},{193,129},{66,2},{130,66... | collective-permute-start | bytes 1216520 | tf_op jit(solution)/shard_map/ppermute | solution.py:222
  171.8 13.2 %collective-permute-start.20 = (bf16[48,4224]{1,0:T(8,128)(2,1)}, bf16[48,4224]{1,0:T(8,128)(2,1)S(1)}, u32[]{:S(2)}, u32[]{:S(2)}) collective-permute-start(bf16[48,4224]{1,0:T(8,128)(2,1)} %get-tuple-element.85), channel_id=1, source_target_pairs={{384,448},{385,449},{386,450},{387,451},{388,452},{389,453},{390,4... | collective-permute-start | bytes 1216520 | tf_op jit(solution)/shard_map/ppermute | solution.py:221
  172.6 15.1 %collective-permute-start.21 = (bf16[48,4224]{1,0:T(8,128)(2,1)}, bf16[48,4224]{1,0:T(8,128)(2,1)}, u32[]{:S(2)}, u32[]{:S(2)}) collective-permute-start(bf16[48,4224]{1,0:T(8,128)(2,1)} %get-tuple-element.86), channel_id=1, source_target_pairs={{64,0},{65,1},{66,2},{67,3},{68,4},{69,5},{70,6},{71,7},{72,8},{73... | collective-permute-start | bytes 1216520 | tf_op jit(solution)/shard_map/ppermute | solution.py:222
  181.2 16.2 %collective-permute-start.25 = (bf16[48,4224]{1,0:T(8,128)(2,1)}, bf16[48,4224]{1,0:T(8,128)(2,1)}, u32[]{:S(2)}, u32[]{:S(2)}) collective-permute-start(bf16[48,4224]{1,0:T(8,128)(2,1)} %get-tuple-element.106), channel_id=1, source_target_pairs={{64,0},{128,64},{65,1},{129,65},{66,2},{130,66},{67,3},{131,67},{6... | collective-permute-start | bytes 1216520 | tf_op jit(solution)/shard_map/ppermute | solution.py:222
  211.5 34.6 %all-to-all-start.2 = ((bf16[8,192,128]{2,1,0:T(8,128)(2,1)}), bf16[8,192,128]{2,1,0:T(8,128)(2,1)S(1)}, u32[]{:S(2)}, u32[]{:S(2)}) async-start(bf16[8,192,128]{2,1,0:T(8,128)(2,1)} %broadcast_in_dim.331), calls=%async_computation.2 | async-start | bytes 786432 | tf_op jit(solution)/shard_map/all_to_all | solution.py:245
  270.6 29.1 %all-to-all-start.3 = ((bf16[16,16,8,512]{3,2,1,0:T(8,128)(2,1)}), bf16[16,16,8,512]{3,2,1,0:T(8,128)(2,1)S(1)}, u32[]{:S(2)}, u32[]{:S(2)}) async-start(bf16[16,16,8,512]{3,2,1,0:T(8,128)(2,1)} %bitcast.97), calls=%async_computation.3 | async-start | bytes 4194304 | tf_op jit(solution)/shard_map/all_to_all | solution.py:279
  (82 other events, 1679.0 us)
Sparse Core Ops, SparseCore 0:
  184.3 77.2 all-gather.2
